TPU v7x, 512 devices: a whole 4x4x16 slice. The times are simulated.
512 devices in a mesh: seg: 128 (over y, z, core), rep: 4 (over x).
Axes of the slice: x: 4, y: 4, z: 16, core: 2. Of those that a mesh axis runs over, the one named last changes fastest.
Arguments:
- currents: float32 [32, 786432], P('rep', 'seg'), may hold values from -6 to 6
- requested: int32 [128, 4, 128, 2], P('seg', 'rep'), may hold values from -1 to 47, as said below
- block_rows: int32 [128, 4, 128], P('seg', 'rep'), may hold values from 0 to 6143, as said below
- block_slots: int32 [128, 4, 128], P('seg', 'rep'), may hold values from 0 to 255, as said below
- coupling: bfloat16 [128, 4, 128, 128, 128], P('seg', 'rep'), may hold values from -0.15625 to 0.15625
Outputs:
- voltages: float32 [32, 786432], P('rep', 'seg')
Inputs may be any that keep to these rules, and one draw needn't show every extreme that they name: `requested`: each entry is -1 or a block number whose remainder modulo 4 equals the rep index r of its second dimension; the slots of one source list the non-empty ones first and name different blocks. Every reader requests exactly 2 blocks from its own index of seg, and at most 128 blocks in all for one rep index. `block_rows`: the block rows held by device s, for every rep index, lie in s * 48 - 48 // 4 to (s + 1) * 48 + 48 // 4 - 1, taken modulo 6144. `block_slots`: every slot named is non-empty in requested, and every non-empty slot of a device is named by one or more of its nonzero blocks.
All inputs are finite; a program needn't handle non-finite values.
Results may differ from a plain program's by a relative error of at most 0.0029.
Values may be sent and summed in bfloat16 or wider, within the bound.
No kernel may reach another device: no remote copies, remote signals or barrier semaphores. Data moves between devices by JAX's collectives and lax.ppermute only.
A program may use at most 64 MiB of HBM per device.

v0:
```python
import math

import jax
import jax.numpy as jnp
from jax import lax
from jax.sharding import PartitionSpec as P

ROOT_THREE = math.sqrt(3.0)
SCALE_NORM = 4.0 * math.sqrt(2.0)
LOW_PASS = (
    (1.0 + ROOT_THREE) / SCALE_NORM,
    (3.0 + ROOT_THREE) / SCALE_NORM,
    (3.0 - ROOT_THREE) / SCALE_NORM,
    (1.0 - ROOT_THREE) / SCALE_NORM,
)
HIGH_PASS = (LOW_PASS[3], -LOW_PASS[2], LOW_PASS[1], -LOW_PASS[0])


def from_behind(block, axis, distance):
    devices = range(lax.axis_size(axis))
    route = [((i - distance) % len(devices), i) for i in devices]
    return lax.ppermute(block, axis, route)


def shards(currents, requested, block_rows, block_slots, coupling):
    ports_dev, seg_len = currents.shape
    half_len = seg_len // 2
    block_size = coupling.shape[-1]
    blocks_here = seg_len // block_size
    margin = blocks_here // 4
    blocks_total = blocks_here * lax.axis_size("seg")
    next_pair = from_behind(currents[:, :2], "seg", -1)
    extended = jnp.concatenate([currents, next_pair], axis=1)
    tapped = [extended[:, offset : offset + seg_len : 2] for offset in range(4)]
    low_band = (
        LOW_PASS[0] * tapped[0]
        + LOW_PASS[1] * tapped[1]
        + LOW_PASS[2] * tapped[2]
        + LOW_PASS[3] * tapped[3]
    )
    high_band = (
        HIGH_PASS[0] * tapped[0]
        + HIGH_PASS[1] * tapped[1]
        + HIGH_PASS[2] * tapped[2]
        + HIGH_PASS[3] * tapped[3]
    )
    coefficients = jnp.concatenate([low_band, high_band], axis=1).astype(jnp.bfloat16)
    all_ports = lax.all_gather(coefficients, "rep", axis=0, tiled=True)
    ports_all = all_ports.shape[0]
    wanted = lax.all_to_all(requested[0, 0], "seg", split_axis=0, concat_axis=0, tiled=True)
    readers, slots_per = wanted.shape
    block_table = all_ports.reshape(ports_all, blocks_here, block_size)
    outgoing = jnp.take(block_table, jnp.maximum(wanted, 0).reshape(-1), axis=1)
    outgoing = outgoing.reshape(ports_all, readers, slots_per, block_size)
    arrived = lax.all_to_all(outgoing, "seg", split_axis=1, concat_axis=1, tiled=True)
    arrived = arrived.reshape(ports_all, readers * slots_per, block_size)
    vectors = jnp.take(arrived, block_slots[0, 0], axis=1)
    products = jnp.einsum(
        "nij,pnj->pni", coupling[0, 0], vectors, preferred_element_type=jnp.float32
    )
    seg_index = lax.axis_index("seg")
    local_row = (
        block_rows[0, 0] - (seg_index * blocks_here - margin) + blocks_total
    ) % blocks_total
    window = blocks_here + 2 * margin
    onehot = (local_row[None, :] == jnp.arange(window, dtype=jnp.int32)[:, None]).astype(
        jnp.float32
    )
    rows_window = jnp.einsum("wn,pni->pwi", onehot, products, precision=lax.Precision.HIGHEST)
    summed = lax.psum_scatter(rows_window, "rep", scatter_dimension=0, tiled=True)
    lower_part = from_behind(summed[:, :margin], "seg", -1)
    upper_part = from_behind(summed[:, margin + blocks_here :], "seg", 1)
    own_rows = summed[:, margin : margin + blocks_here]
    own_rows = own_rows.at[:, blocks_here - margin :].add(lower_part)
    own_rows = own_rows.at[:, :margin].add(upper_part)
    wave_out = own_rows.reshape(ports_dev, seg_len)
    low_out = wave_out[:, :half_len]
    high_out = wave_out[:, half_len:]
    prev_low, prev_high = from_behind((low_out[:, -1:], high_out[:, -1:]), "seg", 1)
    low_prev = jnp.concatenate([prev_low, low_out[:, :-1]], axis=1)
    high_prev = jnp.concatenate([prev_high, high_out[:, :-1]], axis=1)
    even_part = (
        LOW_PASS[0] * low_out
        + HIGH_PASS[0] * high_out
        + LOW_PASS[2] * low_prev
        + HIGH_PASS[2] * high_prev
    )
    odd_part = (
        LOW_PASS[1] * low_out
        + HIGH_PASS[1] * high_out
        + LOW_PASS[3] * low_prev
        + HIGH_PASS[3] * high_prev
    )
    return jnp.stack([even_part, odd_part], axis=-1).reshape(ports_dev, seg_len)


def solution(mesh):
    placed = (
        P("rep", "seg"),
        P("seg", "rep", None, None),
        P("seg", "rep", None),
        P("seg", "rep", None),
        P("seg", "rep", None, None, None),
    )
    return jax.shard_map(
        shards, mesh=mesh, in_specs=placed, out_specs=P("rep", "seg"), check_vma=False
    )
```

profile of v0, /device:TPU:2, one launch (start us, length us, event | category | flops | bytes accessed | tf_op | source)
XLA Modules:
  0.0 247.8 jit_solution(3774130113459167183)
XLA Ops:
  7.2 13.3 %collective-permute-start = (f32[8,2]{1,0:T(8,128)S(1)}, f32[8,2]{1,0:T(8,128)S(1)}, u32[]{:S(2)}, u32[]{:S(2)}) collective-permute-start(f32[8,2]{1,0:T(8,128)S(1)} %slice.96), channel_id=1, source_target_pairs={{4,0},{8,4},{12,8},{16,12},{20,16},{24,20},{28,24},{32,28},{36,32}... | collective-permute-start | bytes 200 | tf_op jit(solution)/shard_map/ppermute | solution.py:22
  20.5 1.4 copy.23
  21.9 8.7 %all-to-all-start = ((s32[128,1,2]{2,1,0:T(1,128)}), s32[128,1,2]{2,1,0:T(1,128)S(1)}, u32[]{:S(2)}, u32[]{:S(2)}) async-start(s32[128,1,2]{2,1,0:T(1,128)} %bitcast.1), calls=%async_computation | async-start | bytes 131072 | tf_op jit(solution)/shard_map/all_to_all | solution.py:50
  31.6 4.2 %slice.95 = f32[8,3072]{1,0:T(8,128)S(1)} slice(f32[8,6144]{1,0:T(8,128)} %param.9), slice={[0:8:1], [0:6144:2]} | slice | bytes 196608 | tf_op jit(solution)/shard_map/slice | solution.py:34
  35.8 3.3 %slice.97 = f32[8,3072]{1,0:T(8,128)S(1)} slice(f32[8,6146]{1,0:T(8,128)S(1)} %constant_dynamic-update-slice_fusion), slice={[0:8:1], [1:6145:2]} | slice | bytes 196608 | tf_op jit(solution)/shard_map/slice | solution.py:34
  39.1 3.3 %slice.98 = f32[8,3072]{1,0:T(8,128)S(1)} slice(f32[8,6146]{1,0:T(8,128)S(1)} %constant_dynamic-update-slice_fusion), slice={[0:8:1], [2:6146:2]} | slice | bytes 196608 | tf_op jit(solution)/shard_map/slice | solution.py:34
  42.4 3.3 %slice.99 = f32[8,3072]{1,0:T(8,128)S(1)} slice(f32[8,6146]{1,0:T(8,128)S(1)} %constant_dynamic-update-slice_fusion), slice={[0:8:1], [3:6146:2]} | slice | bytes 196608 | tf_op jit(solution)/shard_map/slice | solution.py:34
  45.8 13.0 %all_gather.3 = bf16[32,6144]{1,0:T(8,128)(2,1)S(1)} all-gather(bf16[8,6144]{1,0:T(8,128)(2,1)S(1)} %pad_maximum_fusion.1), channel_id=1, replica_groups=mesh['seg'=128,'rep'=4] {'rep'}, dimensions={0}, use_global_device_ids=true | all-gather | bytes 491520 | tf_op jit(solution)/shard_map/all_gather | solution.py:48
  59.5 1.0 gather_fusion
  60.5 1.6 broadcast_select_fusion
  62.1 16.6 %all-to-all-start.1 = ((bf16[32,128,2,128]{3,0,2,1:T(8,128)(2,1)}), bf16[32,128,2,128]{3,0,2,1:T(8,128)(2,1)S(1)}, u32[]{:S(2)}, u32[]{:S(2)}) async-start(bf16[32,128,2,128]{3,0,2,1:T(8,128)(2,1)} %broadcast_select_fusion), calls=%async_computation.1 | async-start | bytes 4194304 | tf_op jit(solution)/shard_map/all_to_all | solution.py:55
  78.8 98.7 %all-to-all-done.1 = bf16[32,128,2,128]{3,0,2,1:T(8,128)(2,1)S(1)} async-done(((bf16[32,128,2,128]{3,0,2,1:T(8,128)(2,1)}), bf16[32,128,2,128]{3,0,2,1:T(8,128)(2,1)S(1)}, u32[]{:S(2)}, u32[]{:S(2)}) %all-to-all-start.1) | async-done | bytes 2097184 | tf_op jit(solution)/shard_map/all_to_all | solution.py:55
  178.3 4.5 %fusion.4 = f32[32,128,128]{2,0,1:T(8,128)S(1)} fusion(bf16[1,1,128,128,128]{4,3,2,1,0:T(8,128)(2,1)} %param.13, bf16[128,32,128]{2,1,0:T(8,128)(2,1)S(1)} %gather_fusion.1, pred[128]{0:T(512)(128)(4,1)S(1)} %compare_and_fusion), kind=kOutput, calls=%fused_computation.7 | convolution fusion | flops 134742016 | bytes 7340160 | tf_op jit(solution)/shard_map/nij,pnj->pni/dot_general | solution.py:58
  182.8 3.2 %fusion.7 = f32[32,72,128]{2,1,0:T(8,128)} fusion(f32[32,128,128]{2,0,1:T(8,128)S(1)} %fusion.4, s32[128]{0:T(128)S(1)} %and_select_fusion), kind=kOutput, calls=%fused_computation.8 | convolution fusion | flops 452994048 | bytes 3277312 | tf_op jit(solution)/shard_map/wn,pni->pwi/dot_general | solution.py:69
  186.0 23.3 %reduce-scatter.2.cloned.1.call-done = f32[8,72,128]{2,1,0:T(8,128)} async-done(((f32[32,72,128]{2,1,0:T(8,128)}), f32[8,72,128]{2,1,0:T(8,128)}) %reduce-scatter.2.cloned.1.call-update) | async-done | bytes 294928 | tf_op jit(solution)/shard_map/reduce_scatter | solution.py:70
  210.1 6.5 %collective-permute-start.1 = (f32[8,12,128]{2,1,0:T(8,128)S(1)}, f32[8,12,128]{2,1,0:T(8,128)S(1)}, u32[]{:S(2)}, u32[]{:S(2)}) collective-permute-start(f32[8,12,128]{2,1,0:T(8,128)S(1)} %get-tuple-element.34), channel_id=1, source_target_pairs={{4,0},{8,4},{12,8},{16,12},{20,16},{24,20},{28,24},{32,28},{36,32}... | collective-permute-start | bytes 147464 | tf_op jit(solution)/shard_map/ppermute | solution.py:22
  216.7 1.9 collective-permute-start.2
  220.6 5.0 %collective-permute-done.2 = f32[8,12,128]{2,1,0:T(8,128)S(1)} collective-permute-done((f32[8,12,128]{2,1,0:T(8,128)S(1)}, f32[8,12,128]{2,1,0:T(8,128)S(1)}, u32[]{:S(2)}, u32[]{:S(2)}) %collective-permute-start.2) | collective-permute-done | bytes 49184 | tf_op jit(solution)/shard_map/ppermute | solution.py:22
  226.0 1.9 collective-permute-start.3
  227.9 1.9 collective-permute-start.4
  229.8 4.4 %collective-permute-done.3 = f32[8,1]{1,0:T(8,128)S(1)} collective-permute-done((f32[8,1]{1,0:T(8,128)S(1)}, f32[8,1]{1,0:T(8,128)S(1)}, u32[]{:S(2)}, u32[]{:S(2)}) %collective-permute-start.3) | collective-permute-done | bytes 64 | tf_op jit(solution)/shard_map/ppermute | solution.py:22
  234.2 1.9 collective-permute-done.4
  236.3 2.9 %copy.28 = f32[8,3072,2]{0,2,1:T(2,128)S(1)} copy(f32[8,3072,2]{1,0,2:T(8,128)S(1)} %pad_maximum_fusion) | data formatting | bytes 393216 | tf_op jit(solution)/shard_map/stack | solution.py:94
  239.2 1.8 copy.29
  (37 shorter events, 6.7 us)
Async XLA Ops:
  7.2 28.6 %collective-permute-start = (f32[8,2]{1,0:T(8,128)S(1)}, f32[8,2]{1,0:T(8,128)S(1)}, u32[]{:S(2)}, u32[]{:S(2)}) collective-permute-start(f32[8,2]{1,0:T(8,128)S(1)} %slice.96), channel_id=1, source_target_pairs={{4,0},{8,4},{12,8},{16,12},{20,16},{24,20},{28,24},{32,28},{36,32}... | collective-permute-start | bytes 200 | tf_op jit(solution)/shard_map/ppermute | solution.py:22
  21.9 36.9 %all-to-all-start = ((s32[128,1,2]{2,1,0:T(1,128)}), s32[128,1,2]{2,1,0:T(1,128)S(1)}, u32[]{:S(2)}, u32[]{:S(2)}) async-start(s32[128,1,2]{2,1,0:T(1,128)} %bitcast.1), calls=%async_computation | async-start | bytes 131072 | tf_op jit(solution)/shard_map/all_to_all | solution.py:50
  62.1 16.6 %copy-start = (s32[1,1,128]{2,1,0:T(1,128)S(1)}, s32[1,1,128]{2,1,0:T(1,128)}, u32[]{:S(2)}) copy-start(s32[1,1,128]{2,1,0:T(1,128)} %param.12) | copy-start | bytes 1540
  62.1 16.7 %copy-start.1 = (s32[1,1,128]{2,1,0:T(1,128)S(1)}, s32[1,1,128]{2,1,0:T(1,128)}, u32[]{:S(2)}) copy-start(s32[1,1,128]{2,1,0:T(1,128)} %param.11) | copy-start | bytes 1540
  62.1 115.4 %all-to-all-start.1 = ((bf16[32,128,2,128]{3,0,2,1:T(8,128)(2,1)}), bf16[32,128,2,128]{3,0,2,1:T(8,128)(2,1)S(1)}, u32[]{:S(2)}, u32[]{:S(2)}) async-start(bf16[32,128,2,128]{3,0,2,1:T(8,128)(2,1)} %broadcast_select_fusion), calls=%async_computation.1 | async-start | bytes 4194304 | tf_op jit(solution)/shard_map/all_to_all | solution.py:55
  78.7 130.6 %reduce-scatter.2.cloned.1.call-start = ((), (), s32[]{:S(2)}) async-start(), calls=%async_computation.3 | async-start | bytes 1474560 | tf_op jit(solution)/shard_map/reduce_scatter | solution.py:70
  210.1 9.4 %collective-permute-start.1 = (f32[8,12,128]{2,1,0:T(8,128)S(1)}, f32[8,12,128]{2,1,0:T(8,128)S(1)}, u32[]{:S(2)}, u32[]{:S(2)}) collective-permute-start(f32[8,12,128]{2,1,0:T(8,128)S(1)} %get-tuple-element.34), channel_id=1, source_target_pairs={{4,0},{8,4},{12,8},{16,12},{20,16},{24,20},{28,24},{32,28},{36,32}... | collective-permute-start | bytes 147464 | tf_op jit(solution)/shard_map/ppermute | solution.py:22
  216.7 8.9 %collective-permute-start.2 = (f32[8,12,128]{2,1,0:T(8,128)S(1)}, f32[8,12,128]{2,1,0:T(8,128)S(1)}, u32[]{:S(2)}, u32[]{:S(2)}) collective-permute-start(f32[8,12,128]{2,1,0:T(8,128)S(1)} %get-tuple-element.33), channel_id=1, source_target_pairs={{508,0},{0,4},{4,8},{8,12},{12,16},{16,20},{20,24},{24,28},{28,32}... | collective-permute-start | bytes 147464 | tf_op jit(solution)/shard_map/ppermute | solution.py:22
  226.0 8.2 %collective-permute-start.3 = (f32[8,1]{1,0:T(8,128)S(1)}, f32[8,1]{1,0:T(8,128)S(1)}, u32[]{:S(2)}, u32[]{:S(2)}) collective-permute-start(f32[8,1]{1,0:T(8,128)S(1)} %get-tuple-element.35), channel_id=1, source_target_pairs={{508,0},{0,4},{4,8},{8,12},{12,16},{16,20},{20,24},{24,28},{28,32}... | collective-permute-start | bytes 104 | tf_op jit(solution)/shard_map/ppermute | solution.py:22
  227.9 8.2 %collective-permute-start.4 = (f32[8,1]{1,0:T(8,128)S(1)}, f32[8,1]{1,0:T(8,128)S(1)}, u32[]{:S(2)}, u32[]{:S(2)}) collective-permute-start(f32[8,1]{1,0:T(8,128)S(1)} %get-tuple-element.36), channel_id=1, source_target_pairs={{508,0},{0,4},{4,8},{8,12},{12,16},{16,20},{20,24},{24,28},{28,32}... | collective-permute-start | bytes 104 | tf_op jit(solution)/shard_map/ppermute | solution.py:22
Sparse Core Ops, SparseCore 0:
  186.1 23.1 reduce-scatter.1
where the time goes:
time: 248 us
  waiting for transfers between devices  133 us (54%)
  starting transfers between devices  50.9 us (21%)
  local copies, waits for them, and re-layouts  26.3 us (11%)
  between operations  13.7 us (6%)
  blocking collectives  13 us (5%)
  matrix products  7.68 us (3%)
  other arithmetic  2.97 us (1%)
    all_to_all x1, waiting for transfers between devices, shards(): lax.all_to_all(outgoing, 'seg', split_axis=1, concat_axis=1, tiled=True)  98.7 us
    ppermute x5, starting transfers between devices, from_behind(): return lax.ppermute(block, axis, route)  25.6 us
    reduce_scatter x1, waiting for transfers between devices, shards(): lax.psum_scatter(rows_window, 'rep', scatter_dimension=0, tiled=True)  23.3 us
    all_to_all x1, starting transfers between devices, shards(): lax.all_to_all(outgoing, 'seg', split_axis=1, concat_axis=1, tiled=True)  16.6 us
    slice x4, local copies, waits for them, and re-layouts, shards(): tapped = [extended[:, offset:offset + seg_len:2] for offset in range(4)]  14.1 us
    all_gather x1, blocking collectives, shards(): all_ports = lax.all_gather(coefficients, 'rep', axis=0, tiled=True)  13 us
    ppermute x5, waiting for transfers between devices, from_behind(): return lax.ppermute(block, axis, route)  11.3 us
    all_to_all x1, starting transfers between devices, shards(): lax.all_to_all(requested[0, 0], 'seg', split_axis=0, concat_axis=0, tiled...  8.68 us
  transfers between devices with their start and end apart: 8, of which 5 were waited for; matrix products, arithmetic and copies ran while one was open for 8% of the time, Pallas kernels for 0%

commit v1 on v0

v1 whole, which is shorter than its diff:
```python
import functools
import math

import jax
import jax.numpy as jnp
import numpy as np
from jax import lax
from jax.experimental import pallas as pl
from jax.experimental.pallas import tpu as pltpu
from jax.sharding import Mesh, PartitionSpec as P

ROOT_THREE = math.sqrt(3.0)
SCALE_NORM = 4.0 * math.sqrt(2.0)
LOW_PASS = (
    (1.0 + ROOT_THREE) / SCALE_NORM,
    (3.0 + ROOT_THREE) / SCALE_NORM,
    (3.0 - ROOT_THREE) / SCALE_NORM,
    (1.0 - ROOT_THREE) / SCALE_NORM,
)
HIGH_PASS = (LOW_PASS[3], -LOW_PASS[2], LOW_PASS[1], -LOW_PASS[0])

NY, NZ, NC, NR = 4, 16, 2, 4
SEG = ("y", "z", "core")
PLANE = ("y", "core")
BS = 128
BLOCKS_HERE = 48
MARGIN = BLOCKS_HERE // 4
WINDOW = BLOCKS_HERE + 2 * MARGIN
BLOCKS_ALL = BLOCKS_HERE * NY * NZ * NC
LOWS = BLOCKS_HERE // 2
KEPT = BLOCKS_HERE // NR
PORTS_DEV = 8
PORTS = PORTS_DEV * NR
NNZ = 128
NNZ_STEP = 16
UP_ROWS = MARGIN + 2
VMEM = pl.BlockSpec(memory_space=pltpu.VMEM)
SMEM = pl.BlockSpec(memory_space=pltpu.SMEM)
PARAMS = pltpu.CompilerParams(vmem_limit_bytes=48 * 1024 * 1024)


def forward_matrix():
    taps = np.zeros((3 * BS, 2 * BS), np.float32)
    for k in range(BS):
        for j in range(4):
            taps[2 * k + j, k] = LOW_PASS[j]
            taps[2 * k + j, BS + k] = HIGH_PASS[j]
    return taps


def inverse_matrix():
    taps = np.zeros((4 * BS, 2 * BS), np.float32)
    for k in range(BS):
        for odd in range(2):
            taps[k, 2 * k + odd] = LOW_PASS[odd]
            taps[BS + k, 2 * k + odd] = HIGH_PASS[odd]
            before = k - 1 if k else 2 * BS + BS - 1
            taps[before, 2 * k + odd] = LOW_PASS[2 + odd]
            before = BS + k - 1 if k else 3 * BS + BS - 1
            taps[before, 2 * k + odd] = HIGH_PASS[2 + odd]
    return taps


def dot_exact(a, b):
    return jnp.dot(a, b, precision=lax.Precision.HIGHEST, preferred_element_type=jnp.float32)


def forward_kernel(x_ref, next_ref, taps_ref, out_ref):
    wide = 2 * BS
    here = jnp.concatenate(
        [x_ref[:, wide * b : wide * (b + 1)] for b in range(LOWS)], axis=0
    )
    after = jnp.concatenate(
        [x_ref[:, wide * b : wide * b + BS] for b in range(1, LOWS)] + [next_ref[...]], axis=0
    )
    bands = dot_exact(here, taps_ref[:wide]) + dot_exact(after, taps_ref[wide:])
    bands = bands.astype(jnp.bfloat16)
    for b in range(BLOCKS_HERE):
        rows = PORTS_DEV * (b % LOWS)
        lanes = BS * (b // LOWS)
        out_ref[b % NR, b // NR] = bands[rows : rows + PORTS_DEV, lanes : lanes + BS]


def select_kernel(wanted_ref, table_ref, out_ref):
    source = lax.axis_index("y") * (NZ * NC) + lax.axis_index("core")

    def one(step, carry):
        reader = step // NZ
        z = step % NZ
        for k in range(2):
            block = jnp.maximum(wanted_ref[reader, k, source + NC * z], 0) // NR
            for half in range(2):
                out_ref[reader, half, 2 * z + k] = table_ref[z, half, block]
        return carry

    lax.fori_loop(0, NY * NC * NZ, one, 0, unroll=8)


def product_kernel(
    rows_ref, slots_ref, first_ref, second_ref, coupling_ref, total_ref, up_ref, down_ref
):
    step = pl.program_id(0)
    seg = (lax.axis_index("y") * NZ + lax.axis_index("z")) * NC + lax.axis_index("core")
    edge = seg * BLOCKS_HERE - MARGIN

    @pl.when(step == 0)
    def _():
        total_ref[...] = jnp.zeros_like(total_ref)

    for i in range(NNZ_STEP):
        n = step * NNZ_STEP + i
        row = (rows_ref[0, n] - edge + BLOCKS_ALL) % BLOCKS_ALL
        slot = slots_ref[0, n]
        source = slot // 2
        group = source // (NZ * NC) * NC + source % NC
        place = (source // NC) % NZ * 2 + slot % 2
        vector = jnp.concatenate(
            [
                first_ref[group, 0, place],
                first_ref[group, 1, place],
                second_ref[group, 0, place],
                second_ref[group, 1, place],
            ],
            axis=0,
        )
        product = lax.dot_general(
            vector,
            coupling_ref[i],
            (((1,), (1,)), ((), ())),
            preferred_element_type=jnp.float32,
        )
        total_ref[row] += product

    @pl.when(step == NNZ // NNZ_STEP - 1)
    def _():
        down_ref[...] = total_ref[:MARGIN].astype(jnp.bfloat16)
        up_ref[:MARGIN] = total_ref[MARGIN + BLOCKS_HERE :].astype(jnp.bfloat16)
        up_ref[MARGIN] = total_ref[MARGIN + LOWS - 1].astype(jnp.bfloat16)
        up_ref[MARGIN + 1] = total_ref[MARGIN + BLOCKS_HERE - 1].astype(jnp.bfloat16)


def combine_kernel(total_ref, above_ref, below_ref, out_ref):
    for row in range(BLOCKS_HERE + 2):
        if row < BLOCKS_HERE:
            value = total_ref[MARGIN + row]
            if row < MARGIN:
                value = value + above_ref[row].astype(jnp.float32)
            if row >= BLOCKS_HERE - MARGIN:
                value = value + below_ref[row - BLOCKS_HERE + MARGIN].astype(jnp.float32)
        else:
            value = above_ref[MARGIN + row - BLOCKS_HERE].astype(jnp.float32)
            if row == BLOCKS_HERE + 1:
                value = value + total_ref[MARGIN - 1]
        for r in range(NR):
            out_ref[r, row] = value[PORTS_DEV * r : PORTS_DEV * (r + 1)].astype(jnp.bfloat16)


def inverse_kernel(parts_ref, taps_ref, out_ref):
    rows = parts_ref[0].astype(jnp.float32)
    for r in range(1, NR):
        rows = rows + parts_ref[r].astype(jnp.float32)
    flat = LOWS * PORTS_DEV
    low = rows[:LOWS].reshape(flat, BS)
    high = rows[LOWS:BLOCKS_HERE].reshape(flat, BS)
    low_before = jnp.concatenate([rows[BLOCKS_HERE], low[: flat - PORTS_DEV]], axis=0)
    high_before = jnp.concatenate([rows[BLOCKS_HERE + 1], high[: flat - PORTS_DEV]], axis=0)
    stacked = jnp.concatenate([low, high, low_before, high_before], axis=1)
    volts = dot_exact(stacked, taps_ref[...])
    for b in range(LOWS):
        out_ref[:, 2 * BS * b : 2 * BS * (b + 1)] = volts[PORTS_DEV * b : PORTS_DEV * (b + 1)]


def shift(block, distance):
    count = NY * NZ * NC
    route = [(i, (i + distance) % count) for i in range(count)]
    return lax.ppermute(block, SEG, route)


def shards(currents, requested, block_rows, block_slots, coupling):
    bf16 = jnp.bfloat16
    next_head = shift(currents[:, :BS], -1)
    wanted = lax.all_gather(requested[0, 0].T, PLANE, axis=0)
    residues = pl.pallas_call(
        forward_kernel,
        out_shape=jax.ShapeDtypeStruct((NR, KEPT, PORTS_DEV, BS), bf16),
        in_specs=[VMEM, VMEM, VMEM],
        out_specs=VMEM,
        compiler_params=PARAMS,
        name="forward",
    )(currents, next_head, jnp.asarray(forward_matrix()))
    residues = lax.all_to_all(residues, "rep", 0, 0, tiled=True)

    def fetch(part):
        table = lax.all_gather(part, "z", axis=0)
        chosen = pl.pallas_call(
            select_kernel,
            out_shape=jax.ShapeDtypeStruct((NY * NC, 2, 2 * NZ, PORTS_DEV, BS), bf16),
            in_specs=[SMEM, VMEM],
            out_specs=VMEM,
            compiler_params=PARAMS,
            name="select",
        )(wanted, table)
        return lax.all_to_all(chosen, PLANE, 0, 0, tiled=True)

    first = fetch(residues[:2])
    second = fetch(residues[2:])
    whole = lambda *shape: pl.BlockSpec(shape, lambda n: (0,) * len(shape))
    total, up, down = pl.pallas_call(
        product_kernel,
        grid=(NNZ // NNZ_STEP,),
        out_shape=[
            jax.ShapeDtypeStruct((WINDOW, PORTS, BS), jnp.float32),
            jax.ShapeDtypeStruct((UP_ROWS, PORTS, BS), bf16),
            jax.ShapeDtypeStruct((MARGIN, PORTS, BS), bf16),
        ],
        in_specs=[
            SMEM,
            SMEM,
            whole(*first.shape),
            whole(*second.shape),
            pl.BlockSpec((NNZ_STEP, BS, BS), lambda n: (n, 0, 0)),
        ],
        out_specs=[
            whole(WINDOW, PORTS, BS),
            whole(UP_ROWS, PORTS, BS),
            whole(MARGIN, PORTS, BS),
        ],
        compiler_params=PARAMS,
        name="products",
    )(block_rows[0], block_slots[0], first, second, coupling[0, 0])
    above = shift(up, 1)
    below = shift(down, -1)
    parts = pl.pallas_call(
        combine_kernel,
        out_shape=jax.ShapeDtypeStruct((NR, BLOCKS_HERE + 2, PORTS_DEV, BS), bf16),
        in_specs=[VMEM, VMEM, VMEM],
        out_specs=VMEM,
        compiler_params=PARAMS,
        name="combine",
    )(total, above, below)
    parts = lax.all_to_all(parts, "rep", 0, 0, tiled=True)
    return pl.pallas_call(
        inverse_kernel,
        out_shape=jax.ShapeDtypeStruct(currents.shape, jnp.float32),
        in_specs=[VMEM, VMEM],
        out_specs=VMEM,
        compiler_params=PARAMS,
        name="inverse",
    )(parts, jnp.asarray(inverse_matrix()))


def solution(mesh):
    grid = Mesh(mesh.devices.reshape(NY, NZ, NC, NR), SEG + ("rep",))
    placed = (
        P("rep", SEG),
        P(SEG, "rep", None, None),
        P(SEG, "rep", None),
        P(SEG, "rep", None),
        P(SEG, "rep", None, None, None),
    )
    return jax.shard_map(
        shards, mesh=grid, in_specs=placed, out_specs=P("rep", SEG), check_vma=False
    )
```

time: 248 us -> 157 us (0.63)
  waiting for transfers between devices: 133 us -> 3.51 us
  blocking collectives: 13 us -> 103 us
  local copies, waits for them, and re-layouts: 26.3 us -> 2.63 us
  starting transfers between devices: 50.9 us -> 30.5 us
  Pallas kernels: 0 us -> 16.5 us
  between operations: 13.7 us -> 0.08 us
  matrix products: 7.68 us -> 0 us
  other arithmetic: 2.97 us -> 0 us
    all_to_all x2, waiting for transfers between devices: 98.7 us -> 0.01 us  [the longest x1 0.01 us: shards(): residues = lax.all_to_all(residues, 'rep', 0, 0, tiled=True)]
    all_gather x1 -> x3, blocking collectives: 13 us -> 72.3 us  [the longest x2 63.5 us: fetch(): table = lax.all_gather(part, 'z', axis=0)]
    all_to_all x0 -> x2, blocking collectives: none -> 30.9 us  [the longest x1 20.3 us: fetch(): return lax.all_to_all(chosen, PLANE, 0, 0, tiled=True)]
    reduce_scatter x1 -> x0, waiting for transfers between devices: 23.3 us -> none  [shards(): lax.psum_scatter(rows_window, 'rep', scatter_dimension=0, tiled=True)]
    all_to_all x2, starting transfers between devices: 25.2 us -> 8.38 us  [the longest x1 4.82 us: shards(): residues = lax.all_to_all(residues, 'rep', 0, 0, tiled=True)]
    pallas_call x0 -> x6, Pallas kernels: none -> 16.5 us  [the longest x2 7.11 us: fetch(): pl.pallas_call(select_kernel, out_shape=jax.ShapeDtypeStruct((NY * NC, 2,...]
    slice x9 -> x2, local copies, waits for them, and re-layouts: 16.7 us -> 0.69 us  [the longest x1 0.69 us: shards(): next_head = shift(currents[:, :BS], -1)]
    ppermute x5 -> x3, waiting for transfers between devices: 11.3 us -> 3.5 us  [shift(): return lax.ppermute(block, SEG, route)]
  transfers between devices with their start and end apart: 8 -> 5, of which waited for: 5 -> 2; matrix products, arithmetic and copies ran while one was open for 8% -> 0% of each run, Pallas kernels for 0% -> 2%
where the time goes in v1:
time: 157 us; the launch traced here: 156 us
  blocking collectives  103 us (66%)
  starting transfers between devices  30.5 us (19%)
  Pallas kernels  16.5 us (11%)
  waiting for transfers between devices  3.51 us (2%)
  local copies, waits for them, and re-layouts  2.63 us (2%)
    all_gather x2, blocking collectives, fetch(): table = lax.all_gather(part, 'z', axis=0)  63.5 us
    ppermute x3, starting transfers between devices, shift(): return lax.ppermute(block, SEG, route)  22.2 us
    all_to_all x1, blocking collectives, fetch(): return lax.all_to_all(chosen, PLANE, 0, 0, tiled=True)  20.3 us
    all_to_all x1, blocking collectives, shards(): parts = lax.all_to_all(parts, 'rep', 0, 0, tiled=True)  10.6 us
    all_gather x1, blocking collectives, shards(): wanted = lax.all_gather(requested[0, 0].T, PLANE, axis=0)  8.77 us
    pallas_call x2, Pallas kernels, fetch(): pl.pallas_call(select_kernel, out_shape=jax.ShapeDtypeStruct((NY * NC, 2,...  7.11 us
    pallas_call x1, Pallas kernels, shards(): pl.pallas_call(product_kernel, grid=(NNZ // NNZ_STEP,), out_shape=[jax.Sh...  7 us
    all_to_all x1, starting transfers between devices, shards(): residues = lax.all_to_all(residues, 'rep', 0, 0, tiled=True)  4.82 us
  transfers between devices with their start and end apart: 5, of which 2 were waited for; matrix products, arithmetic and copies ran while one was open for 0% of the time, Pallas kernels for 2%

profile of v1, /device:TPU:2, one launch (start us, length us, event | category | flops | bytes accessed | tf_op | source)
XLA Modules:
  0.0 156.4 jit_solution(4139601702814458922)
XLA Ops:
  0.0 0.7 slice.9
  0.7 13.3 %collective-permute-start = (f32[8,128]{1,0:T(8,128)S(1)}, f32[8,128]{1,0:T(8,128)S(1)}, u32[]{:S(2)}, u32[]{:S(2)}) collective-permute-start(f32[8,128]{1,0:T(8,128)S(1)} %slice.9), channel_id=1, source_target_pairs={{0,508},{4,0},{8,4},{12,8},{16,12},{20,16},{24,20},{28,24},{32,28}... | collective-permute-start | bytes 12296 | tf_op jit(solution)/shard_map/ppermute | solution.py:176
  14.0 1.3 collective-permute-done.next_ref
  15.3 1.0 copy-done.1
  16.3 0.9 copy-done.2
  17.2 1.1 forward.1
  18.3 4.8 %all-to-all-start = ((bf16[4,12,8,128]{3,2,1,0:T(8,128)(2,1)}), bf16[4,12,8,128]{3,2,1,0:T(8,128)(2,1)S(1)}, u32[]{:S(2)}, u32[]{:S(2)}) async-start(bf16[4,12,8,128]{3,2,1,0:T(8,128)(2,1)} %forward.1), calls=%async_computation | async-start | bytes 196608 | tf_op jit(solution)/shard_map/all_to_all | solution.py:191
  23.2 8.8 %all-gather.3.wanted_ref = s32[8,2,128]{2,1,0:T(2,128)S(1)} all-gather(s32[1,2,128]{2,1,0:T(2,128)} %bitcast.15), channel_id=2, replica_groups=mesh['y'=4,'z'=16,'core'=2,'rep'=4] {'y','core'}, dimensions={0}, use_global_device_ids=true | all-gather | bytes 9216 | tf_op jit(solution)/shard_map/all_gather | solution.py:182
  31.9 0.0 all-to-all-done
  31.9 32.8 %all-gather.2 = bf16[32,12,8,128]{3,2,1,0:T(8,128)(2,1)S(1)} all-gather(bf16[2,12,8,128]{3,2,1,0:T(8,128)(2,1)S(1)} %get-tuple-element.11), channel_id=4, replica_groups=mesh['y'=4,'z'=16,'core'=2,'rep'=4] {'z'}, dimensions={0}, use_global_device_ids=true | all-gather | bytes 835584 | tf_op jit(solution)/shard_map/all_gather | solution.py:194
  64.7 4.0 %select.3 = bf16[8,2,32,8,128]{4,3,2,1,0:T(8,128)(2,1)} custom-call(s32[8,2,128]{2,1,0:T(2,128)S(1)} %all-gather.3.wanted_ref, bf16[16,2,12,8,128]{4,3,2,1,0:T(8,128)(2,1)S(1)} %bitcast.11), custom_call_target="tpu_custom_call" | custom-call | tf_op jit(solution)/shard_map/select/pallas_call | solution.py:195
  68.7 3.6 %all-to-all-start.2 = ((bf16[8,2,32,8,128]{4,3,2,1,0:T(8,128)(2,1)}), bf16[8,2,32,8,128]{4,3,2,1,0:T(8,128)(2,1)S(1)}, u32[]{:S(2)}, u32[]{:S(2)}) async-start(bf16[8,2,32,8,128]{4,3,2,1,0:T(8,128)(2,1)} %select.3), calls=%async_computation.2 | async-start | bytes 2097152 | tf_op jit(solution)/shard_map/all_to_all | solution.py:203
  72.3 30.7 %all-gather.1 = bf16[32,12,8,128]{3,2,1,0:T(8,128)(2,1)S(1)} all-gather(bf16[2,12,8,128]{3,2,1,0:T(8,128)(2,1)S(1)} %get-tuple-element.12), channel_id=3, replica_groups=mesh['y'=4,'z'=16,'core'=2,'rep'=4] {'z'}, dimensions={0}, use_global_device_ids=true | all-gather | bytes 835584 | tf_op jit(solution)/shard_map/all_gather | solution.py:194
  103.0 3.1 %select.2 = bf16[8,2,32,8,128]{4,3,2,1,0:T(8,128)(2,1)S(1)} custom-call(s32[8,2,128]{2,1,0:T(2,128)S(1)} %all-gather.3.wanted_ref, bf16[16,2,12,8,128]{4,3,2,1,0:T(8,128)(2,1)S(1)} %bitcast.10), custom_call_target="tpu_custom_call" | custom-call | tf_op jit(solution)/shard_map/select/pallas_call | solution.py:195
  106.1 0.0 all-to-all-done.2.second_ref
  106.1 20.3 %all_to_all.20.first_ref = bf16[8,2,32,8,128]{4,3,2,1,0:T(8,128)(2,1)S(1)} all-to-all(bf16[8,2,32,8,128]{4,3,2,1,0:T(8,128)(2,1)S(1)} %select.2), channel_id=1, replica_groups=mesh['y'=4,'z'=16,'core'=2,'rep'=4] {'y','core'}, dimensions={0} | all-to-all | bytes 2097152 | tf_op jit(solution)/shard_map/all_to_all | solution.py:203
  126.4 7.0 %products.1 = (f32[72,32,128]{2,1,0:T(8,128)S(1)}, bf16[14,32,128]{2,1,0:T(8,128)(2,1)S(1)}, bf16[12,32,128]{2,1,0:T(8,128)(2,1)S(1)}) custom-call(s32[1,128]{1,0:T(1,128)S(1)} %bitcast.12, s32[1,128]{1,0:T(1,128)S(1)} %bitcast.13, bf16[8,2,32,8,128]{4,3,2,1,0:T(8,128)(2,1)S(1)} %all_to_all.20.first_ref, ...), custom_call_target="tpu_custom_call" | custom-call | tf_op jit(solution)/shard_map/products/pallas_call | solution.py:208
  133.4 1.9 %collective-permute-start.1 = (bf16[14,32,128]{2,1,0:T(8,128)(2,1)S(1)}, bf16[14,32,128]{2,1,0:T(8,128)(2,1)S(1)}, u32[]{:S(2)}, u32[]{:S(2)}) collective-permute-start(bf16[14,32,128]{2,1,0:T(8,128)(2,1)S(1)} %get-tuple-element.9), channel_id=1, source_target_pairs={{0,4},{4,8},{8,12},{12,16},{16,20},{20,24},{24,28},{28,32},{32,36}... | collective-permute-start | bytes 344072 | tf_op jit(solution)/shard_map/ppermute | solution.py:176
  135.3 7.0 %collective-permute-start.2 = (bf16[12,32,128]{2,1,0:T(8,128)(2,1)S(1)}, bf16[12,32,128]{2,1,0:T(8,128)(2,1)S(1)}, u32[]{:S(2)}, u32[]{:S(2)}) collective-permute-start(bf16[12,32,128]{2,1,0:T(8,128)(2,1)S(1)} %get-tuple-element.10), channel_id=1, source_target_pairs={{0,508},{4,0},{8,4},{12,8},{16,12},{20,16},{24,20},{28,24},{32,28}... | collective-permute-start | bytes 294920 | tf_op jit(solution)/shard_map/ppermute | solution.py:176
  142.3 2.2 %collective-permute-done.2.below_ref = bf16[12,32,128]{2,1,0:T(8,128)(2,1)S(1)} collective-permute-done((bf16[12,32,128]{2,1,0:T(8,128)(2,1)S(1)}, bf16[12,32,128]{2,1,0:T(8,128)(2,1)S(1)}, u32[]{:S(2)}, u32[]{:S(2)}) %collective-permute-start.2) | collective-permute-done | bytes 98336 | tf_op jit(solution)/shard_map/ppermute | solution.py:176
  144.5 0.0 collective-permute-done.1.above_ref
  144.5 0.1 combine.1
  144.6 10.6 %all_to_all.21.parts_ref = bf16[4,50,8,128]{3,2,1,0:T(8,128)(2,1)S(1)} all-to-all(bf16[4,50,8,128]{3,2,1,0:T(8,128)(2,1)S(1)} %combine.1), channel_id=1, replica_groups=mesh['y'=4,'z'=16,'core'=2,'rep'=4] {'rep'}, dimensions={0} | all-to-all | bytes 819200 | tf_op jit(solution)/shard_map/all_to_all | solution.py:241
  155.2 1.2 inverse.1
  (9 shorter events, 0.0 us)
Async XLA Ops:
  0.7 14.6 %collective-permute-start = (f32[8,128]{1,0:T(8,128)S(1)}, f32[8,128]{1,0:T(8,128)S(1)}, u32[]{:S(2)}, u32[]{:S(2)}) collective-permute-start(f32[8,128]{1,0:T(8,128)S(1)} %slice.9), channel_id=1, source_target_pairs={{0,508},{4,0},{8,4},{12,8},{16,12},{20,16},{24,20},{28,24},{32,28}... | collective-permute-start | bytes 12296 | tf_op jit(solution)/shard_map/ppermute | solution.py:176
  15.3 1.0 copy-start.1
  16.3 0.9 copy-start.2
  18.3 13.6 %all-to-all-start = ((bf16[4,12,8,128]{3,2,1,0:T(8,128)(2,1)}), bf16[4,12,8,128]{3,2,1,0:T(8,128)(2,1)S(1)}, u32[]{:S(2)}, u32[]{:S(2)}) async-start(bf16[4,12,8,128]{3,2,1,0:T(8,128)(2,1)} %forward.1), calls=%async_computation | async-start | bytes 196608 | tf_op jit(solution)/shard_map/all_to_all | solution.py:191
  64.7 61.7 %copy-start.3 = (s32[1,1,128]{2,1,0:T(1,128)S(1)}, s32[1,1,128]{2,1,0:T(1,128)}, u32[]{:S(2)}) copy-start(s32[1,1,128]{2,1,0:T(1,128)} %param.9) | copy-start | bytes 1540
  64.7 61.7 %copy-start.4 = (s32[1,1,128]{2,1,0:T(1,128)S(1)}, s32[1,1,128]{2,1,0:T(1,128)}, u32[]{:S(2)}) copy-start(s32[1,1,128]{2,1,0:T(1,128)} %param.10) | copy-start | bytes 1540
  68.7 37.4 %all-to-all-start.2 = ((bf16[8,2,32,8,128]{4,3,2,1,0:T(8,128)(2,1)}), bf16[8,2,32,8,128]{4,3,2,1,0:T(8,128)(2,1)S(1)}, u32[]{:S(2)}, u32[]{:S(2)}) async-start(bf16[8,2,32,8,128]{4,3,2,1,0:T(8,128)(2,1)} %select.3), calls=%async_computation.2 | async-start | bytes 2097152 | tf_op jit(solution)/shard_map/all_to_all | solution.py:203
  126.4 28.8 %copy-start = (f32[512,256]{1,0:T(8,128)S(1)}, f32[512,256]{1,0:T(8,128)}, u32[]{:S(2)}) copy-start(f32[512,256]{1,0:T(8,128)} %constant.5.clone.taps_ref) | copy-start | bytes 1572868
  133.4 11.1 %collective-permute-start.1 = (bf16[14,32,128]{2,1,0:T(8,128)(2,1)S(1)}, bf16[14,32,128]{2,1,0:T(8,128)(2,1)S(1)}, u32[]{:S(2)}, u32[]{:S(2)}) collective-permute-start(bf16[14,32,128]{2,1,0:T(8,128)(2,1)S(1)} %get-tuple-element.9), channel_id=1, source_target_pairs={{0,4},{4,8},{8,12},{12,16},{16,20},{20,24},{24,28},{28,32},{32,36}... | collective-permute-start | bytes 344072 | tf_op jit(solution)/shard_map/ppermute | solution.py:176
  135.3 9.2 %collective-permute-start.2 = (bf16[12,32,128]{2,1,0:T(8,128)(2,1)S(1)}, bf16[12,32,128]{2,1,0:T(8,128)(2,1)S(1)}, u32[]{:S(2)}, u32[]{:S(2)}) collective-permute-start(bf16[12,32,128]{2,1,0:T(8,128)(2,1)S(1)} %get-tuple-element.10), channel_id=1, source_target_pairs={{0,508},{4,0},{8,4},{12,8},{16,12},{20,16},{24,20},{28,24},{32,28}... | collective-permute-start | bytes 294920 | tf_op jit(solution)/shard_map/ppermute | solution.py:176

commit v2 on v1

v2 whole, which is shorter than its diff:
```python
import math

import jax
import jax.numpy as jnp
import numpy as np
from jax import lax
from jax.experimental import pallas as pl
from jax.experimental.pallas import tpu as pltpu
from jax.sharding import Mesh, PartitionSpec as P

ROOT_THREE = math.sqrt(3.0)
SCALE_NORM = 4.0 * math.sqrt(2.0)
LOW_PASS = (
    (1.0 + ROOT_THREE) / SCALE_NORM,
    (3.0 + ROOT_THREE) / SCALE_NORM,
    (3.0 - ROOT_THREE) / SCALE_NORM,
    (1.0 - ROOT_THREE) / SCALE_NORM,
)
HIGH_PASS = (LOW_PASS[3], -LOW_PASS[2], LOW_PASS[1], -LOW_PASS[0])

NY, NZ, NC, NR = 4, 16, 2, 4
FINE = ("y", "zhigh", "zlow", "core")
EVERY = FINE + ("rep",)
NH = 4
NL = NZ // NH
BS = 128
BLOCKS_HERE = 48
MARGIN = BLOCKS_HERE // 4
WINDOW = BLOCKS_HERE + 2 * MARGIN
BLOCKS_ALL = BLOCKS_HERE * NY * NZ * NC
LOWS = BLOCKS_HERE // 2
SLOTS = NH * NC * 2
PORTS_DEV = 8
PORTS = PORTS_DEV * NR
NNZ = 128
NNZ_STEP = 16
UP_ROWS = MARGIN + 2
VMEM = pl.BlockSpec(memory_space=pltpu.VMEM)
SMEM = pl.BlockSpec(memory_space=pltpu.SMEM)
PARAMS = pltpu.CompilerParams(vmem_limit_bytes=48 * 1024 * 1024)


def forward_matrix():
    taps = np.zeros((3 * BS, 2 * BS), np.float32)
    for k in range(BS):
        for j in range(4):
            taps[2 * k + j, k] = LOW_PASS[j]
            taps[2 * k + j, BS + k] = HIGH_PASS[j]
    return taps


def inverse_matrix():
    taps = np.zeros((4 * BS, 2 * BS), np.float32)
    for k in range(BS):
        for odd in range(2):
            taps[k, 2 * k + odd] = LOW_PASS[odd]
            taps[BS + k, 2 * k + odd] = HIGH_PASS[odd]
            before = k - 1 if k else 2 * BS + BS - 1
            taps[before, 2 * k + odd] = LOW_PASS[2 + odd]
            before = BS + k - 1 if k else 3 * BS + BS - 1
            taps[before, 2 * k + odd] = HIGH_PASS[2 + odd]
    return taps


def dot_exact(a, b):
    return jnp.dot(a, b, precision=lax.Precision.HIGHEST, preferred_element_type=jnp.float32)


def forward_kernel(x_ref, next_ref, taps_ref, out_ref):
    wide = 2 * BS
    here = jnp.concatenate(
        [x_ref[:, wide * b : wide * (b + 1)] for b in range(LOWS)], axis=0
    )
    after = jnp.concatenate(
        [x_ref[:, wide * b : wide * b + BS] for b in range(1, LOWS)] + [next_ref[...]], axis=0
    )
    bands = dot_exact(here, taps_ref[:wide]) + dot_exact(after, taps_ref[wide:])
    bands = bands.astype(jnp.bfloat16)
    for b in range(BLOCKS_HERE):
        rows = PORTS_DEV * (b % LOWS)
        lanes = BS * (b // LOWS)
        out_ref[b] = bands[rows : rows + PORTS_DEV, lanes : lanes + BS]


def select_kernel(wanted_ref, table_ref, out_ref):
    def one(reader, carry):
        for high in range(NH):
            for core in range(NC):
                for k in range(2):
                    slot = (high * NC + core) * 2 + k
                    block = jnp.maximum(wanted_ref[reader, slot], 0)
                    out_ref[reader, slot] = table_ref[core, high, block]
        return carry

    lax.fori_loop(0, NY * NL * NR, one, 0, unroll=2)


def seg_index():
    high = lax.axis_index("y") * NH + lax.axis_index("zhigh")
    return (high * NL + lax.axis_index("zlow")) * NC + lax.axis_index("core")


def product_kernel(rows_ref, slots_ref, vectors_ref, coupling_ref, total_ref, near_ref, far_ref):
    step = pl.program_id(0)
    edge = seg_index() * BLOCKS_HERE - MARGIN

    @pl.when(step == 0)
    def _():
        total_ref[...] = jnp.zeros_like(total_ref)

    for i in range(NNZ_STEP):
        n = step * NNZ_STEP + i
        row = rows_ref[0, n] - edge
        row = jnp.where(row < 0, row + BLOCKS_ALL, row)
        row = jnp.where(row >= BLOCKS_ALL, row - BLOCKS_ALL, row)
        slot = slots_ref[0, n]
        source = slot >> 1
        z = (source >> 1) & (NZ - 1)
        sender = (source >> 5) * NL + (z & (NL - 1))
        place = ((z >> 2) * NC + (source & 1)) * 2 + (slot & 1)
        vector = jnp.concatenate([vectors_ref[sender, r, place] for r in range(NR)], axis=0)
        product = lax.dot_general(
            vector,
            coupling_ref[i],
            (((1,), (1,)), ((), ())),
            preferred_element_type=jnp.float32,
        )
        total_ref[row] += product

    def margins(up_ref, down_ref):
        down_ref[:MARGIN] = total_ref[:MARGIN].astype(jnp.bfloat16)
        down_ref[MARGIN:] = jnp.zeros((2, PORTS, BS), jnp.bfloat16)
        up_ref[:MARGIN] = total_ref[MARGIN + BLOCKS_HERE :].astype(jnp.bfloat16)
        up_ref[MARGIN] = total_ref[MARGIN + LOWS - 1].astype(jnp.bfloat16)
        up_ref[MARGIN + 1] = total_ref[MARGIN + BLOCKS_HERE - 1].astype(jnp.bfloat16)

    last = step == NNZ // NNZ_STEP - 1
    core = lax.axis_index("core")
    pl.when(last & (core == 0))(lambda: margins(near_ref, far_ref))
    pl.when(last & (core == 1))(lambda: margins(far_ref, near_ref))


def combine_kernel(total_ref, near_ref, far_ref, out_ref):
    def combine(above_ref, below_ref):
        for row in range(BLOCKS_HERE + 2):
            if row < BLOCKS_HERE:
                value = total_ref[MARGIN + row]
                if row < MARGIN:
                    value = value + above_ref[row].astype(jnp.float32)
                if row >= BLOCKS_HERE - MARGIN:
                    value = value + below_ref[row - BLOCKS_HERE + MARGIN].astype(jnp.float32)
            else:
                value = above_ref[MARGIN + row - BLOCKS_HERE].astype(jnp.float32)
                if row == BLOCKS_HERE + 1:
                    value = value + total_ref[MARGIN - 1]
            for r in range(NR):
                out_ref[r, row] = value[PORTS_DEV * r : PORTS_DEV * (r + 1)].astype(jnp.bfloat16)

    core = lax.axis_index("core")
    pl.when(core == 0)(lambda: combine(far_ref, near_ref))
    pl.when(core == 1)(lambda: combine(near_ref, far_ref))


def inverse_kernel(parts_ref, taps_ref, out_ref):
    rows = parts_ref[0].astype(jnp.float32)
    for r in range(1, NR):
        rows = rows + parts_ref[r].astype(jnp.float32)
    flat = LOWS * PORTS_DEV
    low = rows[:LOWS].reshape(flat, BS)
    high = rows[LOWS:BLOCKS_HERE].reshape(flat, BS)
    low_before = jnp.concatenate([rows[BLOCKS_HERE], low[: flat - PORTS_DEV]], axis=0)
    high_before = jnp.concatenate([rows[BLOCKS_HERE + 1], high[: flat - PORTS_DEV]], axis=0)
    stacked = jnp.concatenate([low, high, low_before, high_before], axis=1)
    volts = dot_exact(stacked, taps_ref[...])
    for b in range(LOWS):
        out_ref[:, 2 * BS * b : 2 * BS * (b + 1)] = volts[PORTS_DEV * b : PORTS_DEV * (b + 1)]


def route(block, partner):
    count = NY * NZ * NC
    return lax.ppermute(block, FINE, [(i, partner(i) % count) for i in range(count)])


def windows():
    groups = []
    for core in range(NC):
        for high in range(NH):
            start = NL * high + 2 * core
            members = sorted((z % NL, z % NZ) for z in range(start, start + NL))
            groups.append(
                [
                    ((y * NZ + z) * NC + core) * NR + r
                    for y in range(NY)
                    for _, z in members
                    for r in range(NR)
                ]
            )
    return groups


def to_window(block):
    return lax.all_to_all(block, EVERY, 0, 0, tiled=True, axis_index_groups=windows())


def shards(currents, requested, block_rows, block_slots, coupling):
    bf16 = jnp.bfloat16
    next_head = route(currents[:, :BS], lambda i: i - 1)
    wanted = requested.reshape(NY, NH, NL, NC, 2).transpose(0, 2, 1, 3, 4)
    wanted = jnp.broadcast_to(wanted.reshape(NY, NL, 1, SLOTS), (NY, NL, NR, SLOTS))
    wanted = to_window(wanted.reshape(NY * NL * NR, SLOTS))
    table = pl.pallas_call(
        forward_kernel,
        out_shape=jax.ShapeDtypeStruct((BLOCKS_HERE, PORTS_DEV, BS), bf16),
        in_specs=[VMEM, VMEM, VMEM],
        out_specs=VMEM,
        compiler_params=PARAMS,
        name="forward",
    )(currents, next_head, jnp.asarray(forward_matrix()))
    table = lax.all_gather(table, "zhigh", axis=0)
    table = lax.all_gather(table, "core", axis=0)
    chosen = pl.pallas_call(
        select_kernel,
        out_shape=jax.ShapeDtypeStruct((NY * NL * NR, SLOTS, PORTS_DEV, BS), bf16),
        in_specs=[SMEM, VMEM],
        out_specs=VMEM,
        compiler_params=PARAMS,
        name="select",
    )(wanted, table)
    vectors = to_window(chosen).reshape(NY * NL, NR, SLOTS, PORTS_DEV, BS)
    whole = lambda *shape: pl.BlockSpec(shape, lambda n: (0,) * len(shape))
    total, near, far = pl.pallas_call(
        product_kernel,
        grid=(NNZ // NNZ_STEP,),
        out_shape=[
            jax.ShapeDtypeStruct((WINDOW, PORTS, BS), jnp.float32),
            jax.ShapeDtypeStruct((UP_ROWS, PORTS, BS), bf16),
            jax.ShapeDtypeStruct((UP_ROWS, PORTS, BS), bf16),
        ],
        in_specs=[
            SMEM,
            SMEM,
            whole(*vectors.shape),
            pl.BlockSpec((NNZ_STEP, BS, BS), lambda n: (n, 0, 0)),
        ],
        out_specs=[
            whole(WINDOW, PORTS, BS),
            whole(UP_ROWS, PORTS, BS),
            whole(UP_ROWS, PORTS, BS),
        ],
        compiler_params=PARAMS,
        name="products",
    )(block_rows[0], block_slots[0], vectors, coupling[0, 0])
    near = route(near, lambda i: i ^ 1)
    far = route(far, lambda i: i + 1 if i % 2 else i - 1)
    parts = pl.pallas_call(
        combine_kernel,
        out_shape=jax.ShapeDtypeStruct((NR, BLOCKS_HERE + 2, PORTS_DEV, BS), bf16),
        in_specs=[VMEM, VMEM, VMEM],
        out_specs=VMEM,
        compiler_params=PARAMS,
        name="combine",
    )(total, near, far)
    parts = lax.all_to_all(parts, "rep", 0, 0, tiled=True)
    return pl.pallas_call(
        inverse_kernel,
        out_shape=jax.ShapeDtypeStruct(currents.shape, jnp.float32),
        in_specs=[VMEM, VMEM],
        out_specs=VMEM,
        compiler_params=PARAMS,
        name="inverse",
    )(parts, jnp.asarray(inverse_matrix()))


def solution(mesh):
    grid = Mesh(mesh.devices.reshape(NY, NH, NL, NC, NR), EVERY)
    placed = (
        P("rep", FINE),
        P(FINE, "rep", None, None),
        P(FINE, "rep", None),
        P(FINE, "rep", None),
        P(FINE, "rep", None, None, None),
    )
    return jax.shard_map(
        shards, mesh=grid, in_specs=placed, out_specs=P("rep", FINE), check_vma=False
    )
```

time: 157 us -> 134 us (0.85)
  blocking collectives: 103 us -> 86.7 us
  starting transfers between devices: 30.5 us -> 24.1 us
  Pallas kernels: 16.5 us -> 11.1 us
  waiting for transfers between devices: 3.51 us -> 7.08 us
  local copies, waits for them, and re-layouts: 2.63 us -> 4.5 us
    all_gather x3 -> x2, blocking collectives: 72.3 us -> 23.4 us  [the longest x1 21 us: shards(): table = lax.all_gather(table, 'zhigh', axis=0)]
    all_to_all x1, blocking collectives: 20.3 us -> 53.5 us  [to_window(): lax.all_to_all(block, EVERY, 0, 0, tiled=True, axis_index_groups=windows())]
    pallas_call x3 -> x2, Pallas kernels: 8.24 us -> 3.34 us  [the longest x1 2.86 us: shards(): pl.pallas_call(select_kernel, out_shape=jax.ShapeDtypeStruct((NY * NL * N...]
    ppermute x3, starting transfers between devices: 22.2 us -> 18.5 us  [route(): lax.ppermute(block, FINE, [(i, partner(i) % count) for i in range(count)])]
    ppermute x3, waiting for transfers between devices: 3.5 us -> 7.08 us  [route(): lax.ppermute(block, FINE, [(i, partner(i) % count) for i in range(count)])]
    all_to_all x2 -> x1, starting transfers between devices: 8.38 us -> 5.57 us  [to_window(): lax.all_to_all(block, EVERY, 0, 0, tiled=True, axis_index_groups=windows())]
  transfers between devices with their start and end apart: 5 -> 4, of which waited for: 2 -> 1; matrix products, arithmetic and copies ran while one was open for 0% -> 1% of each run, Pallas kernels for 2% -> 0%
where the time goes in v2:
time: 134 us
  blocking collectives  86.7 us (65%)
  starting transfers between devices  24.1 us (18%)
  Pallas kernels  11.1 us (8%)
  waiting for transfers between devices  7.08 us (5%)
  local copies, waits for them, and re-layouts  4.5 us (3%)
    all_to_all x1, blocking collectives, to_window(): lax.all_to_all(block, EVERY, 0, 0, tiled=True, axis_index_groups=windows())  53.5 us
    all_gather x1, blocking collectives, shards(): table = lax.all_gather(table, 'zhigh', axis=0)  21 us
    ppermute x3, starting transfers between devices, route(): lax.ppermute(block, FINE, [(i, partner(i) % count) for i in range(count)])  18.5 us
    all_to_all x1, blocking collectives, shards(): parts = lax.all_to_all(parts, 'rep', 0, 0, tiled=True)  9.8 us
    ppermute x3, waiting for transfers between devices, route(): lax.ppermute(block, FINE, [(i, partner(i) % count) for i in range(count)])  7.08 us
    pallas_call x1, Pallas kernels, shards(): pl.pallas_call(product_kernel, grid=(NNZ // NNZ_STEP,), out_shape=[jax.Sh...  6.48 us
    all_to_all x1, starting transfers between devices, to_window(): lax.all_to_all(block, EVERY, 0, 0, tiled=True, axis_index_groups=windows())  5.57 us
    pallas_call x1, Pallas kernels, shards(): pl.pallas_call(select_kernel, out_shape=jax.ShapeDtypeStruct((NY * NL * N...  2.86 us
  transfers between devices with their start and end apart: 4, of which 1 were waited for; matrix products, arithmetic and copies ran while one was open for 1% of the time, Pallas kernels for 0%

profile of v2, /device:TPU:2, one launch (start us, length us, event | category | flops | bytes accessed | tf_op | source)
XLA Modules:
  0.0 133.6 jit_solution(15135788939925501977)
XLA Ops:
  0.0 0.7 slice.3
  0.7 13.3 %collective-permute-start = (f32[8,128]{1,0:T(8,128)S(1)}, f32[8,128]{1,0:T(8,128)S(1)}, u32[]{:S(2)}, u32[]{:S(2)}) collective-permute-start(f32[8,128]{1,0:T(8,128)S(1)} %slice.3), channel_id=1, source_target_pairs={{0,508},{4,0},{8,4},{12,8},{16,12},{20,16},{24,20},{28,24},{32,28}... | collective-permute-start | bytes 12296 | tf_op jit(solution)/shard_map/ppermute | solution.py:181
  14.0 0.8 reshape.12
  14.8 0.3 copy.10
  15.1 0.1 copy.11
  15.2 0.6 broadcast_in_dim.8
  15.9 5.6 %all-to-all-start = ((s32[64,1,16]{2,1,0:T(1,128)}), s32[64,1,16]{2,1,0:T(1,128)S(1)}, u32[]{:S(2)}, u32[]{:S(2)}) async-start(s32[64,1,16]{2,1,0:T(1,128)} %bitcast.4), calls=%async_computation | async-start | bytes 65536 | tf_op jit(solution)/shard_map/all_to_all | solution.py:202
  21.4 0.0 copy-start.1
  21.5 1.0 copy-done.1
  22.5 0.9 copy-done.2
  23.4 0.5 forward.1
  23.9 21.0 %all-gather = bf16[192,8,128]{2,1,0:T(8,128)(2,1)S(1)} all-gather(bf16[48,8,128]{2,1,0:T(8,128)(2,1)S(1)} %forward.1), channel_id=2, replica_groups=mesh['y'=4,'zhigh'=4,'zlow'=4,'core'=2,'rep'=4] {'zhigh'}, dimensions={0}, use_global_device_ids=true | all-gather | bytes 491520 | tf_op jit(solution)/shard_map/all_gather | solution.py:219
  44.9 2.4 %all-gather.1 = bf16[8,48,8,128]{3,2,1,0:T(8,128)(2,1)S(1)} all-gather(bf16[4,48,8,128]{3,2,1,0:T(8,128)(2,1)S(1)} %bitcast.18), channel_id=3, replica_groups=mesh['y'=4,'zhigh'=4,'zlow'=4,'core'=2,'rep'=4] {'core'}, dimensions={0}, use_global_device_ids=true | all-gather | bytes 1179648 | tf_op jit(solution)/shard_map/all_gather | solution.py:220
  47.3 2.9 %select.1 = bf16[64,16,8,128]{3,2,1,0:T(8,128)(2,1)S(1)} custom-call(s32[64,16]{1,0:T(8,128)S(1)} %bitcast.14, bf16[2,4,48,8,128]{4,3,2,1,0:T(8,128)(2,1)S(1)} %bitcast.13), custom_call_target="tpu_custom_call" | custom-call | tf_op jit(solution)/shard_map/select/pallas_call | solution.py:221
  50.1 0.0 copy-start.3
  50.2 53.5 %all_to_all.21 = bf16[64,16,8,128]{3,2,1,0:T(8,128)(2,1)S(1)} all-to-all(bf16[64,16,8,128]{3,2,1,0:T(8,128)(2,1)S(1)} %select.1), channel_id=1, replica_groups={{0,1,2,3,8,9,10,11,16,17,18,19,24,25,26,27,128,129,130,131,136,137,138,..., dimensions={0} | all-to-all | bytes 4194304 | tf_op jit(solution)/shard_map/all_to_all | solution.py:202
  103.6 6.5 %products.1 = (f32[72,32,128]{2,1,0:T(8,128)S(1)}, bf16[14,32,128]{2,1,0:T(8,128)(2,1)S(1)}, bf16[14,32,128]{2,1,0:T(8,128)(2,1)S(1)}) custom-call(s32[1,128]{1,0:T(1,128)S(1)} %bitcast.15, s32[1,128]{1,0:T(1,128)S(1)} %bitcast.16, bf16[16,4,16,8,128]{4,3,2,1,0:T(8,128)(2,1)S(1)} %bitcast.12, bf16[128,128,128]{2,1,0:T(8,128)(2,1)} %bitcast.17), custom_call_target="tpu_custom_call" | custom-call | tf_op jit(solution)/shard_map/products/pallas_call | solution.py:231
  110.1 0.0 copy-start
  110.1 2.9 %collective-permute-start.1 = (bf16[14,32,128]{2,1,0:T(8,128)(2,1)S(1)}, bf16[14,32,128]{2,1,0:T(8,128)(2,1)S(1)}, u32[]{:S(2)}, u32[]{:S(2)}) collective-permute-start(bf16[14,32,128]{2,1,0:T(8,128)(2,1)S(1)} %get-tuple-element.9), channel_id=1, source_target_pairs={{0,4},{4,0},{8,12},{12,8},{16,20},{20,16},{24,28},{28,24},{32,36},... | collective-permute-start | bytes 344072 | tf_op jit(solution)/shard_map/ppermute | solution.py:181
  113.0 2.3 %collective-permute-start.2 = (bf16[14,32,128]{2,1,0:T(8,128)(2,1)S(1)}, bf16[14,32,128]{2,1,0:T(8,128)(2,1)S(1)}, u32[]{:S(2)}, u32[]{:S(2)}) collective-permute-start(bf16[14,32,128]{2,1,0:T(8,128)(2,1)S(1)} %get-tuple-element.10), channel_id=1, source_target_pairs={{0,508},{4,8},{8,4},{12,16},{16,12},{20,24},{24,20},{28,32},{32,28... | collective-permute-start | bytes 344072 | tf_op jit(solution)/shard_map/ppermute | solution.py:181
  115.4 7.1 %collective-permute-done.2.far_ref = bf16[14,32,128]{2,1,0:T(8,128)(2,1)S(1)} collective-permute-done((bf16[14,32,128]{2,1,0:T(8,128)(2,1)S(1)}, bf16[14,32,128]{2,1,0:T(8,128)(2,1)S(1)}, u32[]{:S(2)}, u32[]{:S(2)}) %collective-permute-start.2) | collective-permute-done | bytes 114720 | tf_op jit(solution)/shard_map/ppermute | solution.py:181
  122.5 0.1 combine.1
  122.5 9.8 %all_to_all.22.parts_ref = bf16[4,50,8,128]{3,2,1,0:T(8,128)(2,1)S(1)} all-to-all(bf16[4,50,8,128]{3,2,1,0:T(8,128)(2,1)S(1)} %combine.1), channel_id=1, replica_groups=mesh['y'=4,'zhigh'=4,'zlow'=4,'core'=2,'rep'=4] {'rep'}, dimensions={0} | all-to-all | bytes 819200 | tf_op jit(solution)/shard_map/all_to_all | solution.py:263
  132.4 1.2 inverse.1
  (8 shorter events, 0.0 us)
Async XLA Ops:
  0.7 20.8 %collective-permute-start = (f32[8,128]{1,0:T(8,128)S(1)}, f32[8,128]{1,0:T(8,128)S(1)}, u32[]{:S(2)}, u32[]{:S(2)}) collective-permute-start(f32[8,128]{1,0:T(8,128)S(1)} %slice.3), channel_id=1, source_target_pairs={{0,508},{4,0},{8,4},{12,8},{16,12},{20,16},{24,20},{28,24},{32,28}... | collective-permute-start | bytes 12296 | tf_op jit(solution)/shard_map/ppermute | solution.py:181
  15.9 31.4 %all-to-all-start = ((s32[64,1,16]{2,1,0:T(1,128)}), s32[64,1,16]{2,1,0:T(1,128)S(1)}, u32[]{:S(2)}, u32[]{:S(2)}) async-start(s32[64,1,16]{2,1,0:T(1,128)} %bitcast.4), calls=%async_computation | async-start | bytes 65536 | tf_op jit(solution)/shard_map/all_to_all | solution.py:202
  21.4 1.0 copy-start.1
  22.4 0.9 copy-start.2
  50.1 53.5 %copy-start.3 = (s32[1,1,128]{2,1,0:T(1,128)S(1)}, s32[1,1,128]{2,1,0:T(1,128)}, u32[]{:S(2)}) copy-start(s32[1,1,128]{2,1,0:T(1,128)} %param.9) | copy-start | bytes 1540
  50.1 53.5 %copy-start.4 = (s32[1,1,128]{2,1,0:T(1,128)S(1)}, s32[1,1,128]{2,1,0:T(1,128)}, u32[]{:S(2)}) copy-start(s32[1,1,128]{2,1,0:T(1,128)} %param.10) | copy-start | bytes 1540
  110.1 22.2 %copy-start = (f32[512,256]{1,0:T(8,128)S(1)}, f32[512,256]{1,0:T(8,128)}, u32[]{:S(2)}) copy-start(f32[512,256]{1,0:T(8,128)} %constant.5.clone.taps_ref) | copy-start | bytes 1572868
  110.1 5.2 %collective-permute-start.1 = (bf16[14,32,128]{2,1,0:T(8,128)(2,1)S(1)}, bf16[14,32,128]{2,1,0:T(8,128)(2,1)S(1)}, u32[]{:S(2)}, u32[]{:S(2)}) collective-permute-start(bf16[14,32,128]{2,1,0:T(8,128)(2,1)S(1)} %get-tuple-element.9), channel_id=1, source_target_pairs={{0,4},{4,0},{8,12},{12,8},{16,20},{20,16},{24,28},{28,24},{32,36},... | collective-permute-start | bytes 344072 | tf_op jit(solution)/shard_map/ppermute | solution.py:181
  113.0 9.4 %collective-permute-start.2 = (bf16[14,32,128]{2,1,0:T(8,128)(2,1)S(1)}, bf16[14,32,128]{2,1,0:T(8,128)(2,1)S(1)}, u32[]{:S(2)}, u32[]{:S(2)}) collective-permute-start(bf16[14,32,128]{2,1,0:T(8,128)(2,1)S(1)} %get-tuple-element.10), channel_id=1, source_target_pairs={{0,508},{4,8},{8,4},{12,16},{16,12},{20,24},{24,20},{28,32},{32,28... | collective-permute-start | bytes 344072 | tf_op jit(solution)/shard_map/ppermute | solution.py:181

commit v3 on v2

--- a/solution.py
+++ b/solution.py
@@ -19,17 +19,16 @@
 HIGH_PASS = (LOW_PASS[3], -LOW_PASS[2], LOW_PASS[1], -LOW_PASS[0])
 
 NY, NZ, NC, NR = 4, 16, 2, 4
-FINE = ("y", "zhigh", "zlow", "core")
+FINE = ("y", "zhigh", "zmid", "zlow", "core")
 EVERY = FINE + ("rep",)
-NH = 4
-NL = NZ // NH
+NH, NM, NL = 4, 2, 2
 BS = 128
 BLOCKS_HERE = 48
 MARGIN = BLOCKS_HERE // 4
 WINDOW = BLOCKS_HERE + 2 * MARGIN
 BLOCKS_ALL = BLOCKS_HERE * NY * NZ * NC
 LOWS = BLOCKS_HERE // 2
-SLOTS = NH * NC * 2
+SLOTS = NH * NL * NC * 2
 PORTS_DEV = 8
 PORTS = PORTS_DEV * NR
 NNZ = 128
@@ -38,15 +37,6 @@
 VMEM = pl.BlockSpec(memory_space=pltpu.VMEM)
 SMEM = pl.BlockSpec(memory_space=pltpu.SMEM)
 PARAMS = pltpu.CompilerParams(vmem_limit_bytes=48 * 1024 * 1024)
-
-
-def forward_matrix():
-    taps = np.zeros((3 * BS, 2 * BS), np.float32)
-    for k in range(BS):
-        for j in range(4):
-            taps[2 * k + j, k] = LOW_PASS[j]
-            taps[2 * k + j, BS + k] = HIGH_PASS[j]
-    return taps
 
 
 def inverse_matrix():
@@ -66,15 +56,22 @@
     return jnp.dot(a, b, precision=lax.Precision.HIGHEST, preferred_element_type=jnp.float32)
 
 
-def forward_kernel(x_ref, next_ref, taps_ref, out_ref):
+def forward_kernel(x_ref, next_ref, out_ref):
     wide = 2 * BS
+    row = lax.broadcasted_iota(jnp.int32, (wide + BS, wide), 0)
+    lane = lax.broadcasted_iota(jnp.int32, (wide + BS, wide), 1)
+    is_low = lane < BS
+    tap = row - 2 * jnp.where(is_low, lane, lane - BS)
+    taps = jnp.zeros((wide + BS, wide), jnp.float32)
+    for j in range(4):
+        taps = jnp.where(tap == j, jnp.where(is_low, LOW_PASS[j], HIGH_PASS[j]), taps)
     here = jnp.concatenate(
         [x_ref[:, wide * b : wide * (b + 1)] for b in range(LOWS)], axis=0
     )
     after = jnp.concatenate(
         [x_ref[:, wide * b : wide * b + BS] for b in range(1, LOWS)] + [next_ref[...]], axis=0
     )
-    bands = dot_exact(here, taps_ref[:wide]) + dot_exact(after, taps_ref[wide:])
+    bands = dot_exact(here, taps[:wide]) + dot_exact(after, taps[wide:])
     bands = bands.astype(jnp.bfloat16)
     for b in range(BLOCKS_HERE):
         rows = PORTS_DEV * (b % LOWS)
@@ -82,27 +79,33 @@
         out_ref[b] = bands[rows : rows + PORTS_DEV, lanes : lanes + BS]
 
 
-def select_kernel(wanted_ref, table_ref, out_ref):
+def select_kernel(wanted_ref, same_ref, other_ref, out_ref):
+    parity = lax.axis_index("zlow")
+
     def one(reader, carry):
         for high in range(NH):
-            for core in range(NC):
-                for k in range(2):
-                    slot = (high * NC + core) * 2 + k
-                    block = jnp.maximum(wanted_ref[reader, slot], 0)
-                    out_ref[reader, slot] = table_ref[core, high, block]
+            for swap, table_ref in enumerate((same_ref, other_ref)):
+                asked = (high * NL + (parity ^ swap)) * NC * 2
+                given = (high * NL + swap) * NC * 2
+                for core in range(NC):
+                    for k in range(2):
+                        block = jnp.maximum(wanted_ref[reader, asked + 2 * core + k], 0)
+                        out_ref[reader, given + 2 * core + k] = table_ref[core, high, block]
         return carry
 
-    lax.fori_loop(0, NY * NL * NR, one, 0, unroll=2)
+    lax.fori_loop(0, NY * NM * NR, one, 0)
 
 
 def seg_index():
-    high = lax.axis_index("y") * NH + lax.axis_index("zhigh")
-    return (high * NL + lax.axis_index("zlow")) * NC + lax.axis_index("core")
+    z = lax.axis_index("zhigh") * NM + lax.axis_index("zmid")
+    z = z * NL + lax.axis_index("zlow")
+    return (lax.axis_index("y") * NZ + z) * NC + lax.axis_index("core")
 
 
 def product_kernel(rows_ref, slots_ref, vectors_ref, coupling_ref, total_ref, near_ref, far_ref):
     step = pl.program_id(0)
     edge = seg_index() * BLOCKS_HERE - MARGIN
+    parity = lax.axis_index("zlow")
 
     @pl.when(step == 0)
     def _():
@@ -116,8 +119,8 @@
         slot = slots_ref[0, n]
         source = slot >> 1
         z = (source >> 1) & (NZ - 1)
-        sender = (source >> 5) * NL + (z & (NL - 1))
-        place = ((z >> 2) * NC + (source & 1)) * 2 + (slot & 1)
+        sender = (source >> 5) * NM + ((z >> 1) & 1)
+        place = ((z >> 2) * NL + ((z & 1) ^ parity)) * NC * 2 + (slot & 3)
         vector = jnp.concatenate([vectors_ref[sender, r, place] for r in range(NR)], axis=0)
         product = lax.dot_general(
             vector,
@@ -140,7 +143,7 @@
     pl.when(last & (core == 1))(lambda: margins(far_ref, near_ref))
 
 
-def combine_kernel(total_ref, near_ref, far_ref, out_ref):
+def combine_kernel(total_ref, nears_ref, far_ref, out_ref):
     def combine(above_ref, below_ref):
         for row in range(BLOCKS_HERE + 2):
             if row < BLOCKS_HERE:
@@ -157,8 +160,8 @@
                 out_ref[r, row] = value[PORTS_DEV * r : PORTS_DEV * (r + 1)].astype(jnp.bfloat16)
 
     core = lax.axis_index("core")
-    pl.when(core == 0)(lambda: combine(far_ref, near_ref))
-    pl.when(core == 1)(lambda: combine(near_ref, far_ref))
+    pl.when(core == 0)(lambda: combine(far_ref, nears_ref.at[1]))
+    pl.when(core == 1)(lambda: combine(nears_ref.at[0], far_ref))
 
 
 def inverse_kernel(parts_ref, taps_ref, out_ref):
@@ -184,17 +187,18 @@
 def windows():
     groups = []
     for core in range(NC):
-        for high in range(NH):
-            start = NL * high + 2 * core
-            members = sorted((z % NL, z % NZ) for z in range(start, start + NL))
-            groups.append(
-                [
-                    ((y * NZ + z) * NC + core) * NR + r
-                    for y in range(NY)
-                    for _, z in members
-                    for r in range(NR)
-                ]
-            )
+        for first in range(0, NZ, 4):
+            for odd in range(2):
+                start = first + odd + 2 * core
+                members = sorted(((z >> 1) & 1, z % NZ) for z in (start, start + 2))
+                groups.append(
+                    [
+                        ((y * NZ + z) * NC + core) * NR + r
+                        for y in range(NY)
+                        for _, z in members
+                        for r in range(NR)
+                    ]
+                )
     return groups
 
 
@@ -205,28 +209,32 @@
 def shards(currents, requested, block_rows, block_slots, coupling):
     bf16 = jnp.bfloat16
     next_head = route(currents[:, :BS], lambda i: i - 1)
-    wanted = requested.reshape(NY, NH, NL, NC, 2).transpose(0, 2, 1, 3, 4)
-    wanted = jnp.broadcast_to(wanted.reshape(NY, NL, 1, SLOTS), (NY, NL, NR, SLOTS))
-    wanted = to_window(wanted.reshape(NY * NL * NR, SLOTS))
-    table = pl.pallas_call(
+    same = pl.pallas_call(
         forward_kernel,
         out_shape=jax.ShapeDtypeStruct((BLOCKS_HERE, PORTS_DEV, BS), bf16),
-        in_specs=[VMEM, VMEM, VMEM],
+        in_specs=[VMEM, VMEM],
         out_specs=VMEM,
         compiler_params=PARAMS,
         name="forward",
-    )(currents, next_head, jnp.asarray(forward_matrix()))
-    table = lax.all_gather(table, "zhigh", axis=0)
-    table = lax.all_gather(table, "core", axis=0)
+    )(currents, next_head)
+    wanted = requested.reshape(NY, NH, NM, NL * NC * 2).transpose(0, 2, 1, 3)
+    wanted = jnp.broadcast_to(wanted.reshape(NY, NM, 1, SLOTS), (NY, NM, NR, SLOTS))
+    wanted = wanted.reshape(NY * NM * NR, SLOTS)
+    same = lax.all_gather(same, "zhigh", axis=0)
+    same, wanted = lax.optimization_barrier((same, wanted))
+    other = route(same, lambda i: i ^ NC)
+    same = lax.all_gather(same, "core", axis=0)
+    wanted = to_window(wanted)
+    other = lax.all_gather(other, "core", axis=0)
     chosen = pl.pallas_call(
         select_kernel,
-        out_shape=jax.ShapeDtypeStruct((NY * NL * NR, SLOTS, PORTS_DEV, BS), bf16),
-        in_specs=[SMEM, VMEM],
+        out_shape=jax.ShapeDtypeStruct((NY * NM * NR, SLOTS, PORTS_DEV, BS), bf16),
+        in_specs=[SMEM, VMEM, VMEM],
         out_specs=VMEM,
         compiler_params=PARAMS,
         name="select",
-    )(wanted, table)
-    vectors = to_window(chosen).reshape(NY * NL, NR, SLOTS, PORTS_DEV, BS)
+    )(wanted, same, other)
+    vectors = to_window(chosen).reshape(NY * NM, NR, SLOTS, PORTS_DEV, BS)
     whole = lambda *shape: pl.BlockSpec(shape, lambda n: (0,) * len(shape))
     total, near, far = pl.pallas_call(
         product_kernel,
@@ -250,7 +258,7 @@
         compiler_params=PARAMS,
         name="products",
     )(block_rows[0], block_slots[0], vectors, coupling[0, 0])
-    near = route(near, lambda i: i ^ 1)
+    nears = lax.all_gather(near, "core", axis=0)
     far = route(far, lambda i: i + 1 if i % 2 else i - 1)
     parts = pl.pallas_call(
         combine_kernel,
@@ -259,7 +267,7 @@
         out_specs=VMEM,
         compiler_params=PARAMS,
         name="combine",
-    )(total, near, far)
+    )(total, nears, far)
     parts = lax.all_to_all(parts, "rep", 0, 0, tiled=True)
     return pl.pallas_call(
         inverse_kernel,
@@ -272,7 +280,7 @@
 
 
 def solution(mesh):
-    grid = Mesh(mesh.devices.reshape(NY, NH, NL, NC, NR), EVERY)
+    grid = Mesh(mesh.devices.reshape(NY, NH, NM, NL, NC, NR), EVERY)
     placed = (
         P("rep", FINE),
         P(FINE, "rep", None, None),

time: 134 us -> 123 us (0.918)
  the two profiles are of different devices: /device:TPU:2 before, /device:TPU:32 now
where the time goes in v3:
time: 123 us
  blocking collectives  85.6 us (70%)
  starting transfers between devices  15.2 us (12%)
  Pallas kernels  12.3 us (10%)
  waiting for transfers between devices  6.23 us (5%)
  local copies, waits for them, and re-layouts  3.21 us (3%)
    all_to_all x1, blocking collectives, to_window(): lax.all_to_all(block, EVERY, 0, 0, tiled=True, axis_index_groups=windows())  34.3 us
    all_gather x1, blocking collectives, shards(): same = lax.all_gather(same, 'zhigh', axis=0)  31 us
    all_to_all x1, blocking collectives, shards(): parts = lax.all_to_all(parts, 'rep', 0, 0, tiled=True)  13.5 us
    ppermute x3, starting transfers between devices, route(): lax.ppermute(block, FINE, [(i, partner(i) % count) for i in range(count)])  8.48 us
    all_to_all x1, starting transfers between devices, to_window(): lax.all_to_all(block, EVERY, 0, 0, tiled=True, axis_index_groups=windows())  6.73 us
    pallas_call x1, Pallas kernels, shards(): pl.pallas_call(product_kernel, grid=(NNZ // NNZ_STEP,), out_shape=[jax.Sh...  6.5 us
    all_to_all x1, waiting for transfers between devices, to_window(): lax.all_to_all(block, EVERY, 0, 0, tiled=True, axis_index_groups=windows())  4.38 us
    pallas_call x1, Pallas kernels, shards(): pl.pallas_call(select_kernel, out_shape=jax.ShapeDtypeStruct((NY * NM * N...  3.94 us
  transfers between devices with their start and end apart: 4, of which 3 were waited for; matrix products, arithmetic and copies ran while one was open for 1% of the time, Pallas kernels for 0%

profile of v3, /device:TPU:32, one launch (start us, length us, event | category | flops | bytes accessed | tf_op | source)
XLA Modules:
  0.0 122.7 jit_solution(15994283310088063224)
XLA Ops:
  0.0 0.7 slice.3
  0.7 1.9 %collective-permute-start = (f32[8,128]{1,0:T(8,128)S(1)}, f32[8,128]{1,0:T(8,128)S(1)}, u32[]{:S(2)}, u32[]{:S(2)}) collective-permute-start(f32[8,128]{1,0:T(8,128)S(1)} %slice.3), channel_id=1, source_target_pairs={{0,508},{4,0},{8,4},{12,8},{16,12},{20,16},{24,20},{28,24},{32,28}... | collective-permute-start | bytes 12296 | tf_op jit(solution)/shard_map/ppermute | solution.py:184
  2.6 0.8 copy.10
  3.4 0.1 reshape.13
  3.5 0.1 broadcast_in_dim.7
  3.6 0.3 collective-permute-done.next_ref
  3.9 0.9 copy-done.1
  4.8 0.6 forward.1
  5.4 31.0 %all-gather = bf16[192,8,128]{2,1,0:T(8,128)(2,1)S(1)} all-gather(bf16[48,8,128]{2,1,0:T(8,128)(2,1)S(1)} %forward.1), channel_id=2, replica_groups=mesh['y'=4,'zhigh'=4,'zmid'=2,'zlow'=2,'core'=2,'rep'=4] {'zhigh'}, dimensions={0}, use_global_device_ids=true | all-gather | bytes 491520 | tf_op jit(solution)/shard_map/all_gather | solution.py:223
  36.4 0.6 broadcast_in_dim.8
  37.0 4.0 %collective-permute-start.1 = (bf16[4,48,8,128]{3,2,1,0:T(8,128)(2,1)S(1)}, bf16[4,48,8,128]{3,2,1,0:T(8,128)(2,1)S(1)}, u32[]{:S(2)}, u32[]{:S(2)}) collective-permute-start(bf16[4,48,8,128]{3,2,1,0:T(8,128)(2,1)S(1)} %bitcast.22), channel_id=1, source_target_pairs={{0,8},{4,12},{8,0},{12,4},{16,24},{20,28},{24,16},{28,20},{32,40},... | collective-permute-start | bytes 1179656 | tf_op jit(solution)/shard_map/ppermute | solution.py:184
  41.0 6.7 %all-to-all-start = ((s32[32,1,32]{2,1,0:T(1,128)}), s32[32,1,32]{2,1,0:T(1,128)S(1)}, u32[]{:S(2)}, u32[]{:S(2)}) async-start(s32[32,1,32]{2,1,0:T(1,128)} %bitcast.5), calls=%async_computation | async-start | bytes 32768 | tf_op jit(solution)/shard_map/all_to_all | solution.py:206
  47.8 2.4 %all-gather.1 = bf16[8,48,8,128]{3,2,1,0:T(8,128)(2,1)S(1)} all-gather(bf16[4,48,8,128]{3,2,1,0:T(8,128)(2,1)S(1)} %bitcast.23), channel_id=3, replica_groups=mesh['y'=4,'zhigh'=4,'zmid'=2,'zlow'=2,'core'=2,'rep'=4] {'core'}, dimensions={0}, use_global_device_ids=true | all-gather | bytes 1179648 | tf_op jit(solution)/shard_map/all_gather | solution.py:226
  50.1 2.4 %all-gather.2 = bf16[8,48,8,128]{3,2,1,0:T(8,128)(2,1)S(1)} all-gather(bf16[4,48,8,128]{3,2,1,0:T(8,128)(2,1)S(1)} %collective-permute-done.1), channel_id=4, replica_groups=mesh['y'=4,'zhigh'=4,'zmid'=2,'zlow'=2,'core'=2,'rep'=4] {'core'}, dimensions={0}, use_global_device_ids=true | all-gather | bytes 1179648 | tf_op jit(solution)/shard_map/all_gather | solution.py:228
  52.5 4.4 %all-to-all-done = s32[32,1,32]{2,1,0:T(1,128)S(1)} async-done(((s32[32,1,32]{2,1,0:T(1,128)}), s32[32,1,32]{2,1,0:T(1,128)S(1)}, u32[]{:S(2)}, u32[]{:S(2)}) %all-to-all-start) | async-done | bytes 4128 | tf_op jit(solution)/shard_map/all_to_all | solution.py:206
  56.9 3.9 %select.1 = bf16[32,32,8,128]{3,2,1,0:T(8,128)(2,1)S(1)} custom-call(s32[32,32]{1,0:T(8,128)S(1)} %bitcast.18, bf16[2,4,48,8,128]{4,3,2,1,0:T(8,128)(2,1)S(1)} %bitcast.15, bf16[2,4,48,8,128]{4,3,2,1,0:T(8,128)(2,1)S(1)} %bitcast.16), custom_call_target="tpu_custom_call" | custom-call | tf_op jit(solution)/shard_map/select/pallas_call | solution.py:229
  60.8 34.3 %all_to_all.21 = bf16[32,32,8,128]{3,2,1,0:T(8,128)(2,1)S(1)} all-to-all(bf16[32,32,8,128]{3,2,1,0:T(8,128)(2,1)S(1)} %select.1), channel_id=1, replica_groups={{0,1,2,3,16,17,18,19,128,129,130,131,144,145,146,147,256,257,258,259,27..., dimensions={0} | all-to-all | bytes 4194304 | tf_op jit(solution)/shard_map/all_to_all | solution.py:206
  95.1 6.5 %products.1 = (f32[72,32,128]{2,1,0:T(8,128)S(1)}, bf16[14,32,128]{2,1,0:T(8,128)(2,1)S(1)}, bf16[14,32,128]{2,1,0:T(8,128)(2,1)S(1)}) custom-call(s32[1,128]{1,0:T(1,128)S(1)} %bitcast.19, s32[1,128]{1,0:T(1,128)S(1)} %bitcast.20, bf16[8,4,32,8,128]{4,3,2,1,0:T(8,128)(2,1)S(1)} %bitcast.14, bf16[128,128,128]{2,1,0:T(8,128)(2,1)} %bitcast.21), custom_call_target="tpu_custom_call" | custom-call | tf_op jit(solution)/shard_map/products/pallas_call | solution.py:239
  101.6 2.6 %collective-permute-start.2 = (bf16[14,32,128]{2,1,0:T(8,128)(2,1)S(1)}, bf16[14,32,128]{2,1,0:T(8,128)(2,1)S(1)}, u32[]{:S(2)}, u32[]{:S(2)}) collective-permute-start(bf16[14,32,128]{2,1,0:T(8,128)(2,1)S(1)} %get-tuple-element.14), channel_id=1, source_target_pairs={{0,508},{4,8},{8,4},{12,16},{16,12},{20,24},{24,20},{28,32},{32,28... | collective-permute-start | bytes 344072 | tf_op jit(solution)/shard_map/ppermute | solution.py:184
  104.2 2.1 %all-gather.3 = bf16[28,32,128]{2,1,0:T(8,128)(2,1)S(1)} all-gather(bf16[14,32,128]{2,1,0:T(8,128)(2,1)S(1)} %get-tuple-element.13), channel_id=5, replica_groups=mesh['y'=4,'zhigh'=4,'zmid'=2,'zlow'=2,'core'=2,'rep'=4] {'core'}, dimensions={0}, use_global_device_ids=true | all-gather | bytes 344064 | tf_op jit(solution)/shard_map/all_gather | solution.py:261
  106.4 1.5 %collective-permute-done.2.far_ref = bf16[14,32,128]{2,1,0:T(8,128)(2,1)S(1)} collective-permute-done((bf16[14,32,128]{2,1,0:T(8,128)(2,1)S(1)}, bf16[14,32,128]{2,1,0:T(8,128)(2,1)S(1)}, u32[]{:S(2)}, u32[]{:S(2)}) %collective-permute-start.2) | collective-permute-done | bytes 114720 | tf_op jit(solution)/shard_map/ppermute | solution.py:184
  107.9 0.1 combine.1
  108.0 13.5 %all_to_all.22.parts_ref = bf16[4,50,8,128]{3,2,1,0:T(8,128)(2,1)S(1)} all-to-all(bf16[4,50,8,128]{3,2,1,0:T(8,128)(2,1)S(1)} %combine.1), channel_id=1, replica_groups=mesh['y'=4,'zhigh'=4,'zmid'=2,'zlow'=2,'core'=2,'rep'=4] {'rep'}, dimensions={0} | all-to-all | bytes 819200 | tf_op jit(solution)/shard_map/all_to_all | solution.py:271
  121.4 1.2 %inverse.1 = f32[8,6144]{1,0:T(8,128)} custom-call(bf16[4,50,8,128]{3,2,1,0:T(8,128)(2,1)S(1)} %all_to_all.22.parts_ref, f32[512,256]{1,0:T(8,128)S(1)} %copy-done), custom_call_target="tpu_custom_call" | custom-call | tf_op jit(solution)/shard_map/inverse/pallas_call | solution.py:272
  (9 shorter events, 0.0 us)
Async XLA Ops:
  0.7 3.2 %collective-permute-start = (f32[8,128]{1,0:T(8,128)S(1)}, f32[8,128]{1,0:T(8,128)S(1)}, u32[]{:S(2)}, u32[]{:S(2)}) collective-permute-start(f32[8,128]{1,0:T(8,128)S(1)} %slice.3), channel_id=1, source_target_pairs={{0,508},{4,0},{8,4},{12,8},{16,12},{20,16},{24,20},{28,24},{32,28}... | collective-permute-start | bytes 12296 | tf_op jit(solution)/shard_map/ppermute | solution.py:184
  3.9 0.9 copy-start.1
  37.0 13.1 %collective-permute-start.1 = (bf16[4,48,8,128]{3,2,1,0:T(8,128)(2,1)S(1)}, bf16[4,48,8,128]{3,2,1,0:T(8,128)(2,1)S(1)}, u32[]{:S(2)}, u32[]{:S(2)}) collective-permute-start(bf16[4,48,8,128]{3,2,1,0:T(8,128)(2,1)S(1)} %bitcast.22), channel_id=1, source_target_pairs={{0,8},{4,12},{8,0},{12,4},{16,24},{20,28},{24,16},{28,20},{32,40},... | collective-permute-start | bytes 1179656 | tf_op jit(solution)/shard_map/ppermute | solution.py:184
  41.0 15.9 %all-to-all-start = ((s32[32,1,32]{2,1,0:T(1,128)}), s32[32,1,32]{2,1,0:T(1,128)S(1)}, u32[]{:S(2)}, u32[]{:S(2)}) async-start(s32[32,1,32]{2,1,0:T(1,128)} %bitcast.5), calls=%async_computation | async-start | bytes 32768 | tf_op jit(solution)/shard_map/all_to_all | solution.py:206
  60.8 34.3 %copy-start.2 = (s32[1,1,128]{2,1,0:T(1,128)S(1)}, s32[1,1,128]{2,1,0:T(1,128)}, u32[]{:S(2)}) copy-start(s32[1,1,128]{2,1,0:T(1,128)} %param.8) | copy-start | bytes 1540
  60.8 34.3 %copy-start.3 = (s32[1,1,128]{2,1,0:T(1,128)S(1)}, s32[1,1,128]{2,1,0:T(1,128)}, u32[]{:S(2)}) copy-start(s32[1,1,128]{2,1,0:T(1,128)} %param.9) | copy-start | bytes 1540
  101.6 19.8 %copy-start = (f32[512,256]{1,0:T(8,128)S(1)}, f32[512,256]{1,0:T(8,128)}, u32[]{:S(2)}) copy-start(f32[512,256]{1,0:T(8,128)} %constant.2.clone.taps_ref) | copy-start | bytes 1572868
  101.6 6.2 %collective-permute-start.2 = (bf16[14,32,128]{2,1,0:T(8,128)(2,1)S(1)}, bf16[14,32,128]{2,1,0:T(8,128)(2,1)S(1)}, u32[]{:S(2)}, u32[]{:S(2)}) collective-permute-start(bf16[14,32,128]{2,1,0:T(8,128)(2,1)S(1)} %get-tuple-element.14), channel_id=1, source_target_pairs={{0,508},{4,8},{8,4},{12,16},{16,12},{20,24},{24,20},{28,32},{32,28... | collective-permute-start | bytes 344072 | tf_op jit(solution)/shard_map/ppermute | solution.py:184

commit v4 on v3

--- a/solution.py
+++ b/solution.py
@@ -26,13 +26,14 @@
 BLOCKS_HERE = 48
 MARGIN = BLOCKS_HERE // 4
 WINDOW = BLOCKS_HERE + 2 * MARGIN
+KEPT = BLOCKS_HERE // NR
 BLOCKS_ALL = BLOCKS_HERE * NY * NZ * NC
 LOWS = BLOCKS_HERE // 2
 SLOTS = NH * NL * NC * 2
 PORTS_DEV = 8
 PORTS = PORTS_DEV * NR
 NNZ = 128
-NNZ_STEP = 16
+NNZ_STEP = 64
 UP_ROWS = MARGIN + 2
 VMEM = pl.BlockSpec(memory_space=pltpu.VMEM)
 SMEM = pl.BlockSpec(memory_space=pltpu.SMEM)
@@ -76,7 +77,7 @@
     for b in range(BLOCKS_HERE):
         rows = PORTS_DEV * (b % LOWS)
         lanes = BS * (b // LOWS)
-        out_ref[b] = bands[rows : rows + PORTS_DEV, lanes : lanes + BS]
+        out_ref[b % NR, b // NR] = bands[rows : rows + PORTS_DEV, lanes : lanes + BS]
 
 
 def select_kernel(wanted_ref, same_ref, other_ref, out_ref):
@@ -84,16 +85,18 @@
 
     def one(reader, carry):
         for high in range(NH):
+            found = []
             for swap, table_ref in enumerate((same_ref, other_ref)):
                 asked = (high * NL + (parity ^ swap)) * NC * 2
-                given = (high * NL + swap) * NC * 2
                 for core in range(NC):
                     for k in range(2):
                         block = jnp.maximum(wanted_ref[reader, asked + 2 * core + k], 0)
-                        out_ref[reader, given + 2 * core + k] = table_ref[core, high, block]
+                        found.append(table_ref[core, high, block >> 2])
+            for i, block in enumerate(found):
+                out_ref[reader, high * NL * NC * 2 + i] = block
         return carry
 
-    lax.fori_loop(0, NY * NM * NR, one, 0)
+    lax.fori_loop(0, NY * NM, one, 0)
 
 
 def seg_index():
@@ -121,9 +124,8 @@
         z = (source >> 1) & (NZ - 1)
         sender = (source >> 5) * NM + ((z >> 1) & 1)
         place = ((z >> 2) * NL + ((z & 1) ^ parity)) * NC * 2 + (slot & 3)
-        vector = jnp.concatenate([vectors_ref[sender, r, place] for r in range(NR)], axis=0)
         product = lax.dot_general(
-            vector,
+            vectors_ref[sender, place],
             coupling_ref[i],
             (((1,), (1,)), ((), ())),
             preferred_element_type=jnp.float32,
@@ -191,14 +193,14 @@
             for odd in range(2):
                 start = first + odd + 2 * core
                 members = sorted(((z >> 1) & 1, z % NZ) for z in (start, start + 2))
-                groups.append(
-                    [
-                        ((y * NZ + z) * NC + core) * NR + r
-                        for y in range(NY)
-                        for _, z in members
-                        for r in range(NR)
-                    ]
-                )
+                for r in range(NR):
+                    groups.append(
+                        [
+                            ((y * NZ + z) * NC + core) * NR + r
+                            for y in range(NY)
+                            for _, z in members
+                        ]
+                    )
     return groups
 
 
@@ -209,17 +211,18 @@
 def shards(currents, requested, block_rows, block_slots, coupling):
     bf16 = jnp.bfloat16
     next_head = route(currents[:, :BS], lambda i: i - 1)
-    same = pl.pallas_call(
+    residues = pl.pallas_call(
         forward_kernel,
-        out_shape=jax.ShapeDtypeStruct((BLOCKS_HERE, PORTS_DEV, BS), bf16),
+        out_shape=jax.ShapeDtypeStruct((NR, KEPT, PORTS_DEV, BS), bf16),
         in_specs=[VMEM, VMEM],
         out_specs=VMEM,
         compiler_params=PARAMS,
         name="forward",
     )(currents, next_head)
+    residues = lax.all_to_all(residues, "rep", 0, 0, tiled=True)
+    same = residues.transpose(1, 0, 2, 3).reshape(KEPT, PORTS, BS)
     wanted = requested.reshape(NY, NH, NM, NL * NC * 2).transpose(0, 2, 1, 3)
-    wanted = jnp.broadcast_to(wanted.reshape(NY, NM, 1, SLOTS), (NY, NM, NR, SLOTS))
-    wanted = wanted.reshape(NY * NM * NR, SLOTS)
+    wanted = wanted.reshape(NY * NM, SLOTS)
     same = lax.all_gather(same, "zhigh", axis=0)
     same, wanted = lax.optimization_barrier((same, wanted))
     other = route(same, lambda i: i ^ NC)
@@ -228,13 +231,13 @@
     other = lax.all_gather(other, "core", axis=0)
     chosen = pl.pallas_call(
         select_kernel,
-        out_shape=jax.ShapeDtypeStruct((NY * NM * NR, SLOTS, PORTS_DEV, BS), bf16),
+        out_shape=jax.ShapeDtypeStruct((NY * NM, SLOTS, PORTS, BS), bf16),
         in_specs=[SMEM, VMEM, VMEM],
         out_specs=VMEM,
         compiler_params=PARAMS,
         name="select",
     )(wanted, same, other)
-    vectors = to_window(chosen).reshape(NY * NM, NR, SLOTS, PORTS_DEV, BS)
+    vectors = to_window(chosen)
     whole = lambda *shape: pl.BlockSpec(shape, lambda n: (0,) * len(shape))
     total, near, far = pl.pallas_call(
         product_kernel,

time: 123 us -> 124 us (level)
  the two profiles are of different devices: /device:TPU:32 before, /device:TPU:2 now
where the time goes in v4:
time: 124 us; the launch traced here: 123 us
  blocking collectives  72.9 us (59%)
  starting transfers between devices  29.9 us (24%)
  waiting for transfers between devices  8.88 us (7%)
  Pallas kernels  8.19 us (7%)
  local copies, waits for them, and re-layouts  3.19 us (3%)
    all_to_all x1, blocking collectives, to_window(): lax.all_to_all(block, EVERY, 0, 0, tiled=True, axis_index_groups=windows())  31.5 us
    all_gather x1, blocking collectives, shards(): same = lax.all_gather(same, 'zhigh', axis=0)  23.5 us
    ppermute x3, starting transfers between devices, route(): lax.ppermute(block, FINE, [(i, partner(i) % count) for i in range(count)])  20.3 us
    all_to_all x1, blocking collectives, shards(): parts = lax.all_to_all(parts, 'rep', 0, 0, tiled=True)  11.3 us
    all_to_all x1, starting transfers between devices, shards(): residues = lax.all_to_all(residues, 'rep', 0, 0, tiled=True)  4.83 us
    all_to_all x1, starting transfers between devices, to_window(): lax.all_to_all(block, EVERY, 0, 0, tiled=True, axis_index_groups=windows())  4.76 us
    ppermute x3, waiting for transfers between devices, route(): lax.ppermute(block, FINE, [(i, partner(i) % count) for i in range(count)])  4.4 us
    pallas_call x1, Pallas kernels, shards(): pl.pallas_call(product_kernel, grid=(NNZ // NNZ_STEP,), out_shape=[jax.Sh...  4.2 us
  transfers between devices with their start and end apart: 5, of which 5 were waited for; matrix products, arithmetic and copies ran while one was open for 1% of the time, Pallas kernels for 0%

profile of v4, /device:TPU:2, one launch (start us, length us, event | category | flops | bytes accessed | tf_op | source)
XLA Modules:
  0.0 123.2 jit_solution(4023422846267623974)
XLA Ops:
  0.0 0.7 slice.3
  0.7 13.3 %collective-permute-start = (f32[8,128]{1,0:T(8,128)S(1)}, f32[8,128]{1,0:T(8,128)S(1)}, u32[]{:S(2)}, u32[]{:S(2)}) collective-permute-start(f32[8,128]{1,0:T(8,128)S(1)} %slice.3), channel_id=1, source_target_pairs={{0,508},{4,0},{8,4},{12,8},{16,12},{20,16},{24,20},{28,24},{32,28}... | collective-permute-start | bytes 12296 | tf_op jit(solution)/shard_map/ppermute | solution.py:186
  14.0 1.3 %collective-permute-done.next_ref = f32[8,128]{1,0:T(8,128)S(1)} collective-permute-done((f32[8,128]{1,0:T(8,128)S(1)}, f32[8,128]{1,0:T(8,128)S(1)}, u32[]{:S(2)}, u32[]{:S(2)}) %collective-permute-start) | collective-permute-done | bytes 4128 | tf_op jit(solution)/shard_map/ppermute | solution.py:186
  15.3 0.9 copy-done.1
  16.2 1.2 forward.1
  17.4 4.8 %all-to-all-start = ((bf16[4,12,8,128]{3,2,1,0:T(8,128)(2,1)}), bf16[4,12,8,128]{3,2,1,0:T(8,128)(2,1)S(1)}, u32[]{:S(2)}, u32[]{:S(2)}) async-start(bf16[4,12,8,128]{3,2,1,0:T(8,128)(2,1)} %forward.1), calls=%async_computation | async-start | bytes 196608 | tf_op jit(solution)/shard_map/all_to_all | solution.py:222
  22.3 0.8 copy.13
  23.1 0.7 reshape.9
  23.8 2.8 %all-to-all-done = bf16[4,12,8,128]{3,2,1,0:T(8,128)(2,1)S(1)} async-done(((bf16[4,12,8,128]{3,2,1,0:T(8,128)(2,1)}), bf16[4,12,8,128]{3,2,1,0:T(8,128)(2,1)S(1)}, u32[]{:S(2)}, u32[]{:S(2)}) %all-to-all-start) | async-done | bytes 98336 | tf_op jit(solution)/shard_map/all_to_all | solution.py:222
  26.6 23.5 %all_gather.21 = bf16[4,12,32,128]{3,2,1,0:T(8,128)(2,1)S(1)} all-gather(bf16[1,12,32,128]{3,2,1,0:T(8,128)(2,1)S(1)} %copy_bitcast_fusion), channel_id=1, replica_groups=mesh['y'=4,'zhigh'=4,'zmid'=2,'zlow'=2,'core'=2,'rep'=4] {'zhigh'}, dimensions={0}, use_global_device_ids=true | all-gather | bytes 491520 | tf_op jit(solution)/shard_map/all_gather | solution.py:226
  50.1 1.9 %collective-permute-start.1 = (bf16[4,12,32,128]{3,2,1,0:T(8,128)(2,1)S(1)}, bf16[4,12,32,128]{3,2,1,0:T(8,128)(2,1)S(1)}, u32[]{:S(2)}, u32[]{:S(2)}) collective-permute-start(bf16[4,12,32,128]{3,2,1,0:T(8,128)(2,1)S(1)} %all_gather.21), channel_id=1, source_target_pairs={{0,8},{4,12},{8,0},{12,4},{16,24},{20,28},{24,16},{28,20},{32,40},... | collective-permute-start | bytes 1179656 | tf_op jit(solution)/shard_map/ppermute | solution.py:186
  52.0 4.8 %all-to-all-start.1 = ((s32[8,1,32]{2,1,0:T(1,128)}), s32[8,1,32]{2,1,0:T(1,128)S(1)}, u32[]{:S(2)}, u32[]{:S(2)}) async-start(s32[8,1,32]{2,1,0:T(1,128)} %bitcast.6), calls=%async_computation.1 | async-start | bytes 8192 | tf_op jit(solution)/shard_map/all_to_all | solution.py:208
  56.8 2.4 %all-gather = bf16[8,12,32,128]{3,2,1,0:T(8,128)(2,1)S(1)} all-gather(bf16[4,12,32,128]{3,2,1,0:T(8,128)(2,1)S(1)} %all_gather.21), channel_id=2, replica_groups=mesh['y'=4,'zhigh'=4,'zmid'=2,'zlow'=2,'core'=2,'rep'=4] {'core'}, dimensions={0}, use_global_device_ids=true | all-gather | bytes 1179648 | tf_op jit(solution)/shard_map/all_gather | solution.py:229
  59.1 0.6 collective-permute-done.1
  59.8 2.4 %all-gather.1 = bf16[8,12,32,128]{3,2,1,0:T(8,128)(2,1)S(1)} all-gather(bf16[4,12,32,128]{3,2,1,0:T(8,128)(2,1)S(1)} %collective-permute-done.1), channel_id=3, replica_groups=mesh['y'=4,'zhigh'=4,'zmid'=2,'zlow'=2,'core'=2,'rep'=4] {'core'}, dimensions={0}, use_global_device_ids=true | all-gather | bytes 1179648 | tf_op jit(solution)/shard_map/all_gather | solution.py:231
  62.1 1.7 %all-to-all-done.1 = s32[8,1,32]{2,1,0:T(1,128)S(1)} async-done(((s32[8,1,32]{2,1,0:T(1,128)}), s32[8,1,32]{2,1,0:T(1,128)S(1)}, u32[]{:S(2)}, u32[]{:S(2)}) %all-to-all-start.1) | async-done | bytes 1056 | tf_op jit(solution)/shard_map/all_to_all | solution.py:208
  63.8 1.5 %select.1 = bf16[8,32,32,128]{3,2,1,0:T(8,128)(2,1)S(1)} custom-call(s32[8,32]{1,0:T(8,128)S(1)} %bitcast.21, bf16[2,4,12,32,128]{4,3,2,1,0:T(8,128)(2,1)S(1)} %bitcast.18, bf16[2,4,12,32,128]{4,3,2,1,0:T(8,128)(2,1)S(1)} %bitcast.19), custom_call_target="tpu_custom_call" | custom-call | tf_op jit(solution)/shard_map/select/pallas_call | solution.py:232
  65.3 31.5 %all_to_all.26.vectors_ref = bf16[8,32,32,128]{3,2,1,0:T(8,128)(2,1)S(1)} all-to-all(bf16[8,32,32,128]{3,2,1,0:T(8,128)(2,1)S(1)} %select.1), channel_id=1, replica_groups={{0,16,128,144,256,272,384,400},{1,17,129,145,257,273,385,401},{2,18,130..., dimensions={0} | all-to-all | bytes 4194304 | tf_op jit(solution)/shard_map/all_to_all | solution.py:208
  96.8 4.2 %products.1 = (f32[72,32,128]{2,1,0:T(8,128)S(1)}, bf16[14,32,128]{2,1,0:T(8,128)(2,1)S(1)}, bf16[14,32,128]{2,1,0:T(8,128)(2,1)S(1)}) custom-call(s32[1,128]{1,0:T(1,128)S(1)} %bitcast.22, s32[1,128]{1,0:T(1,128)S(1)} %bitcast.23, bf16[8,32,32,128]{3,2,1,0:T(8,128)(2,1)S(1)} %all_to_all.26.vectors_ref, bf16[128,128,128]{2,1,0:T(8,128)(2,1)} %bitcast.24), custom_call_target="tpu_custom_call" | custom-call | tf_op jit(solution)/shard_map/products/pallas_call | solution.py:242
  101.1 5.1 %collective-permute-start.2 = (bf16[14,32,128]{2,1,0:T(8,128)(2,1)S(1)}, bf16[14,32,128]{2,1,0:T(8,128)(2,1)S(1)}, u32[]{:S(2)}, u32[]{:S(2)}) collective-permute-start(bf16[14,32,128]{2,1,0:T(8,128)(2,1)S(1)} %get-tuple-element.14), channel_id=1, source_target_pairs={{0,508},{4,8},{8,4},{12,16},{16,12},{20,24},{24,20},{28,32},{32,28... | collective-permute-start | bytes 344072 | tf_op jit(solution)/shard_map/ppermute | solution.py:186
  106.2 2.0 %all-gather.2 = bf16[28,32,128]{2,1,0:T(8,128)(2,1)S(1)} all-gather(bf16[14,32,128]{2,1,0:T(8,128)(2,1)S(1)} %get-tuple-element.13), channel_id=4, replica_groups=mesh['y'=4,'zhigh'=4,'zmid'=2,'zlow'=2,'core'=2,'rep'=4] {'core'}, dimensions={0}, use_global_device_ids=true | all-gather | bytes 344064 | tf_op jit(solution)/shard_map/all_gather | solution.py:264
  108.2 2.4 %collective-permute-done.2.far_ref = bf16[14,32,128]{2,1,0:T(8,128)(2,1)S(1)} collective-permute-done((bf16[14,32,128]{2,1,0:T(8,128)(2,1)S(1)}, bf16[14,32,128]{2,1,0:T(8,128)(2,1)S(1)}, u32[]{:S(2)}, u32[]{:S(2)}) %collective-permute-start.2) | collective-permute-done | bytes 114720 | tf_op jit(solution)/shard_map/ppermute | solution.py:186
  110.7 11.3 %all_to_all.27.parts_ref = bf16[4,50,8,128]{3,2,1,0:T(8,128)(2,1)S(1)} all-to-all(bf16[4,50,8,128]{3,2,1,0:T(8,128)(2,1)S(1)} %combine.1), channel_id=1, replica_groups=mesh['y'=4,'zhigh'=4,'zmid'=2,'zlow'=2,'core'=2,'rep'=4] {'rep'}, dimensions={0} | all-to-all | bytes 819200 | tf_op jit(solution)/shard_map/all_to_all | solution.py:274
  122.0 1.2 %inverse.1 = f32[8,6144]{1,0:T(8,128)} custom-call(bf16[4,50,8,128]{3,2,1,0:T(8,128)(2,1)S(1)} %all_to_all.27.parts_ref, f32[512,256]{1,0:T(8,128)S(1)} %copy-done), custom_call_target="tpu_custom_call" | custom-call | tf_op jit(solution)/shard_map/inverse/pallas_call | solution.py:275
  (11 shorter events, 0.2 us)
Async XLA Ops:
  0.7 14.6 %collective-permute-start = (f32[8,128]{1,0:T(8,128)S(1)}, f32[8,128]{1,0:T(8,128)S(1)}, u32[]{:S(2)}, u32[]{:S(2)}) collective-permute-start(f32[8,128]{1,0:T(8,128)S(1)} %slice.3), channel_id=1, source_target_pairs={{0,508},{4,0},{8,4},{12,8},{16,12},{20,16},{24,20},{28,24},{32,28}... | collective-permute-start | bytes 12296 | tf_op jit(solution)/shard_map/ppermute | solution.py:186
  15.3 0.9 copy-start.1
  17.4 9.2 %all-to-all-start = ((bf16[4,12,8,128]{3,2,1,0:T(8,128)(2,1)}), bf16[4,12,8,128]{3,2,1,0:T(8,128)(2,1)S(1)}, u32[]{:S(2)}, u32[]{:S(2)}) async-start(bf16[4,12,8,128]{3,2,1,0:T(8,128)(2,1)} %forward.1), calls=%async_computation | async-start | bytes 196608 | tf_op jit(solution)/shard_map/all_to_all | solution.py:222
  50.1 9.7 %collective-permute-start.1 = (bf16[4,12,32,128]{3,2,1,0:T(8,128)(2,1)S(1)}, bf16[4,12,32,128]{3,2,1,0:T(8,128)(2,1)S(1)}, u32[]{:S(2)}, u32[]{:S(2)}) collective-permute-start(bf16[4,12,32,128]{3,2,1,0:T(8,128)(2,1)S(1)} %all_gather.21), channel_id=1, source_target_pairs={{0,8},{4,12},{8,0},{12,4},{16,24},{20,28},{24,16},{28,20},{32,40},... | collective-permute-start | bytes 1179656 | tf_op jit(solution)/shard_map/ppermute | solution.py:186
  52.0 11.8 %all-to-all-start.1 = ((s32[8,1,32]{2,1,0:T(1,128)}), s32[8,1,32]{2,1,0:T(1,128)S(1)}, u32[]{:S(2)}, u32[]{:S(2)}) async-start(s32[8,1,32]{2,1,0:T(1,128)} %bitcast.6), calls=%async_computation.1 | async-start | bytes 8192 | tf_op jit(solution)/shard_map/all_to_all | solution.py:208
  65.3 31.5 %copy-start.2 = (s32[1,1,128]{2,1,0:T(1,128)S(1)}, s32[1,1,128]{2,1,0:T(1,128)}, u32[]{:S(2)}) copy-start(s32[1,1,128]{2,1,0:T(1,128)} %param.8) | copy-start | bytes 1540
  65.3 31.5 %copy-start.3 = (s32[1,1,128]{2,1,0:T(1,128)S(1)}, s32[1,1,128]{2,1,0:T(1,128)}, u32[]{:S(2)}) copy-start(s32[1,1,128]{2,1,0:T(1,128)} %param.9) | copy-start | bytes 1540
  101.0 20.9 %copy-start = (f32[512,256]{1,0:T(8,128)S(1)}, f32[512,256]{1,0:T(8,128)}, u32[]{:S(2)}) copy-start(f32[512,256]{1,0:T(8,128)} %constant.2.clone.taps_ref) | copy-start | bytes 1572868
  101.1 9.6 %collective-permute-start.2 = (bf16[14,32,128]{2,1,0:T(8,128)(2,1)S(1)}, bf16[14,32,128]{2,1,0:T(8,128)(2,1)S(1)}, u32[]{:S(2)}, u32[]{:S(2)}) collective-permute-start(bf16[14,32,128]{2,1,0:T(8,128)(2,1)S(1)} %get-tuple-element.14), channel_id=1, source_target_pairs={{0,508},{4,8},{8,4},{12,16},{16,12},{20,24},{24,20},{28,32},{32,28... | collective-permute-start | bytes 344072 | tf_op jit(solution)/shard_map/ppermute | solution.py:186

commit v5 on v4

--- a/solution.py
+++ b/solution.py
@@ -29,7 +29,7 @@
 KEPT = BLOCKS_HERE // NR
 BLOCKS_ALL = BLOCKS_HERE * NY * NZ * NC
 LOWS = BLOCKS_HERE // 2
-SLOTS = NH * NL * NC * 2
+SLOTS = NH * NM * NC * 2
 PORTS_DEV = 8
 PORTS = PORTS_DEV * NR
 NNZ = 128
@@ -81,22 +81,23 @@
 
 
 def select_kernel(wanted_ref, same_ref, other_ref, out_ref):
-    parity = lax.axis_index("zlow")
+    middle = lax.axis_index("zmid")
 
     def one(reader, carry):
         for high in range(NH):
             found = []
             for swap, table_ref in enumerate((same_ref, other_ref)):
-                asked = (high * NL + (parity ^ swap)) * NC * 2
+                place = (high * NM + (middle ^ swap)) * NC * 2
                 for core in range(NC):
                     for k in range(2):
-                        block = jnp.maximum(wanted_ref[reader, asked + 2 * core + k], 0)
-                        found.append(table_ref[core, high, block >> 2])
-            for i, block in enumerate(found):
-                out_ref[reader, high * NL * NC * 2 + i] = block
+                        slot = place + 2 * core + k
+                        block = jnp.maximum(wanted_ref[reader, slot], 0)
+                        found.append((slot, table_ref[core, high, block >> 2]))
+            for slot, block in found:
+                out_ref[reader, slot] = block
         return carry
 
-    lax.fori_loop(0, NY * NM, one, 0)
+    lax.fori_loop(0, NY * NL, one, 0)
 
 
 def seg_index():
@@ -108,7 +109,6 @@
 def product_kernel(rows_ref, slots_ref, vectors_ref, coupling_ref, total_ref, near_ref, far_ref):
     step = pl.program_id(0)
     edge = seg_index() * BLOCKS_HERE - MARGIN
-    parity = lax.axis_index("zlow")
 
     @pl.when(step == 0)
     def _():
@@ -122,8 +122,8 @@
         slot = slots_ref[0, n]
         source = slot >> 1
         z = (source >> 1) & (NZ - 1)
-        sender = (source >> 5) * NM + ((z >> 1) & 1)
-        place = ((z >> 2) * NL + ((z & 1) ^ parity)) * NC * 2 + (slot & 3)
+        sender = (source >> 5) * NL + (z & 1)
+        place = (z >> 1) * NC * 2 + (slot & 3)
         product = lax.dot_general(
             vectors_ref[sender, place],
             coupling_ref[i],
@@ -189,19 +189,23 @@
 def windows():
     groups = []
     for core in range(NC):
-        for first in range(0, NZ, 4):
-            for odd in range(2):
-                start = first + odd + 2 * core
-                members = sorted(((z >> 1) & 1, z % NZ) for z in (start, start + 2))
-                for r in range(NR):
-                    groups.append(
-                        [
-                            ((y * NZ + z) * NC + core) * NR + r
-                            for y in range(NY)
-                            for _, z in members
-                        ]
-                    )
+        for even in range(0, NZ, 2):
+            odd = (even + 1 - 2 * core) % NZ
+            for r in range(NR):
+                groups.append(
+                    [
+                        ((y * NZ + z) * NC + core) * NR + r
+                        for y in range(NY)
+                        for z in (even, odd)
+                    ]
+                )
     return groups
+
+
+def two_away(i):
+    core, z, y = i % NC, i // NC % NZ, i // (NC * NZ)
+    step = 2 if (z >> 1) % 2 == core else -2
+    return (y * NZ + (z + step) % NZ) * NC + core
 
 
 def to_window(block):
@@ -221,17 +225,17 @@
     )(currents, next_head)
     residues = lax.all_to_all(residues, "rep", 0, 0, tiled=True)
     same = residues.transpose(1, 0, 2, 3).reshape(KEPT, PORTS, BS)
-    wanted = requested.reshape(NY, NH, NM, NL * NC * 2).transpose(0, 2, 1, 3)
-    wanted = wanted.reshape(NY * NM, SLOTS)
+    wanted = requested.reshape(NY, NH * NM, NL, NC * 2).transpose(0, 2, 1, 3)
+    wanted = wanted.reshape(NY * NL, SLOTS)
     same = lax.all_gather(same, "zhigh", axis=0)
     same, wanted = lax.optimization_barrier((same, wanted))
-    other = route(same, lambda i: i ^ NC)
+    other = route(same, two_away)
     same = lax.all_gather(same, "core", axis=0)
     wanted = to_window(wanted)
     other = lax.all_gather(other, "core", axis=0)
     chosen = pl.pallas_call(
         select_kernel,
-        out_shape=jax.ShapeDtypeStruct((NY * NM, SLOTS, PORTS, BS), bf16),
+        out_shape=jax.ShapeDtypeStruct((NY * NL, SLOTS, PORTS, BS), bf16),
         in_specs=[SMEM, VMEM, VMEM],
         out_specs=VMEM,
         compiler_params=PARAMS,

time: 124 us -> 123 us (level)
  waiting for transfers between devices: 8.88 us -> 13.2 us
  blocking collectives: 72.9 us -> 69.4 us
    ppermute x3, waiting for transfers between devices: 4.4 us -> 10.4 us  [route(): lax.ppermute(block, FINE, [(i, partner(i) % count) for i in range(count)])]
    all_to_all x1, blocking collectives: 31.5 us -> 29.3 us  [to_window(): lax.all_to_all(block, EVERY, 0, 0, tiled=True, axis_index_groups=windows())]
    all_to_all x1, waiting for transfers between devices: 1.69 us -> 0.01 us  [to_window(): lax.all_to_all(block, EVERY, 0, 0, tiled=True, axis_index_groups=windows())]
    all_to_all x1, blocking collectives: 11.3 us -> 9.83 us  [shards(): parts = lax.all_to_all(parts, 'rep', 0, 0, tiled=True)]
  transfers between devices with their start and end apart: 5 -> 5, of which waited for: 5 -> 4; matrix products, arithmetic and copies ran while one was open for 1% -> 1% of each run, Pallas kernels for 0% -> 0%
where the time goes in v5:
time: 123 us
  blocking collectives  69.4 us (56%)
  starting transfers between devices  28.7 us (23%)
  waiting for transfers between devices  13.2 us (11%)
  Pallas kernels  8.38 us (7%)
  local copies, waits for them, and re-layouts  3.19 us (3%)
    all_to_all x1, blocking collectives, to_window(): lax.all_to_all(block, EVERY, 0, 0, tiled=True, axis_index_groups=windows())  29.3 us
    all_gather x1, blocking collectives, shards(): same = lax.all_gather(same, 'zhigh', axis=0)  23.5 us
    ppermute x3, starting transfers between devices, route(): lax.ppermute(block, FINE, [(i, partner(i) % count) for i in range(count)])  19.1 us
    ppermute x3, waiting for transfers between devices, route(): lax.ppermute(block, FINE, [(i, partner(i) % count) for i in range(count)])  10.4 us
    all_to_all x1, blocking collectives, shards(): parts = lax.all_to_all(parts, 'rep', 0, 0, tiled=True)  9.83 us
    all_to_all x1, starting transfers between devices, shards(): residues = lax.all_to_all(residues, 'rep', 0, 0, tiled=True)  4.83 us
    all_to_all x1, starting transfers between devices, to_window(): lax.all_to_all(block, EVERY, 0, 0, tiled=True, axis_index_groups=windows())  4.76 us
    pallas_call x1, Pallas kernels, shards(): pl.pallas_call(product_kernel, grid=(NNZ // NNZ_STEP,), out_shape=[jax.Sh...  4.19 us
  transfers between devices with their start and end apart: 5, of which 4 were waited for; matrix products, arithmetic and copies ran while one was open for 1% of the time, Pallas kernels for 0%

profile of v5, /device:TPU:2, one launch (start us, length us, event | category | flops | bytes accessed | tf_op | source)
XLA Modules:
  0.0 122.9 jit_solution(15804185498166806297)
XLA Ops:
  0.0 0.7 slice.3
  0.7 13.3 %collective-permute-start = (f32[8,128]{1,0:T(8,128)S(1)}, f32[8,128]{1,0:T(8,128)S(1)}, u32[]{:S(2)}, u32[]{:S(2)}) collective-permute-start(f32[8,128]{1,0:T(8,128)S(1)} %slice.3), channel_id=1, source_target_pairs={{0,508},{4,0},{8,4},{12,8},{16,12},{20,16},{24,20},{28,24},{32,28}... | collective-permute-start | bytes 12296 | tf_op jit(solution)/shard_map/ppermute | solution.py:186
  14.0 1.3 %collective-permute-done.next_ref = f32[8,128]{1,0:T(8,128)S(1)} collective-permute-done((f32[8,128]{1,0:T(8,128)S(1)}, f32[8,128]{1,0:T(8,128)S(1)}, u32[]{:S(2)}, u32[]{:S(2)}) %collective-permute-start) | collective-permute-done | bytes 4128 | tf_op jit(solution)/shard_map/ppermute | solution.py:186
  15.3 0.9 copy-done.1
  16.2 1.2 forward.1
  17.4 4.8 %all-to-all-start = ((bf16[4,12,8,128]{3,2,1,0:T(8,128)(2,1)}), bf16[4,12,8,128]{3,2,1,0:T(8,128)(2,1)S(1)}, u32[]{:S(2)}, u32[]{:S(2)}) async-start(bf16[4,12,8,128]{3,2,1,0:T(8,128)(2,1)} %forward.1), calls=%async_computation | async-start | bytes 196608 | tf_op jit(solution)/shard_map/all_to_all | solution.py:226
  22.3 0.8 copy.11
  23.0 0.1 reshape.8
  23.1 0.7 reshape.9
  23.8 2.8 %all-to-all-done = bf16[4,12,8,128]{3,2,1,0:T(8,128)(2,1)S(1)} async-done(((bf16[4,12,8,128]{3,2,1,0:T(8,128)(2,1)}), bf16[4,12,8,128]{3,2,1,0:T(8,128)(2,1)S(1)}, u32[]{:S(2)}, u32[]{:S(2)}) %all-to-all-start) | async-done | bytes 98336 | tf_op jit(solution)/shard_map/all_to_all | solution.py:226
  26.6 23.5 %all_gather.21 = bf16[4,12,32,128]{3,2,1,0:T(8,128)(2,1)S(1)} all-gather(bf16[1,12,32,128]{3,2,1,0:T(8,128)(2,1)S(1)} %copy_bitcast_fusion), channel_id=1, replica_groups=mesh['y'=4,'zhigh'=4,'zmid'=2,'zlow'=2,'core'=2,'rep'=4] {'zhigh'}, dimensions={0}, use_global_device_ids=true | all-gather | bytes 491520 | tf_op jit(solution)/shard_map/all_gather | solution.py:230
  50.1 1.9 %collective-permute-start.1 = (bf16[4,12,32,128]{3,2,1,0:T(8,128)(2,1)S(1)}, bf16[4,12,32,128]{3,2,1,0:T(8,128)(2,1)S(1)}, u32[]{:S(2)}, u32[]{:S(2)}) collective-permute-start(bf16[4,12,32,128]{3,2,1,0:T(8,128)(2,1)S(1)} %all_gather.21), channel_id=1, source_target_pairs={{0,16},{4,116},{8,24},{12,124},{16,0},{20,36},{24,8},{28,44},{32,4... | collective-permute-start | bytes 1179656 | tf_op jit(solution)/shard_map/ppermute | solution.py:186
  52.0 4.8 %all-to-all-start.1 = ((s32[8,1,32]{2,1,0:T(1,128)}), s32[8,1,32]{2,1,0:T(1,128)S(1)}, u32[]{:S(2)}, u32[]{:S(2)}) async-start(s32[8,1,32]{2,1,0:T(1,128)} %bitcast.6), calls=%async_computation.1 | async-start | bytes 8192 | tf_op jit(solution)/shard_map/all_to_all | solution.py:212
  56.8 2.4 %all-gather = bf16[8,12,32,128]{3,2,1,0:T(8,128)(2,1)S(1)} all-gather(bf16[4,12,32,128]{3,2,1,0:T(8,128)(2,1)S(1)} %all_gather.21), channel_id=2, replica_groups=mesh['y'=4,'zhigh'=4,'zmid'=2,'zlow'=2,'core'=2,'rep'=4] {'core'}, dimensions={0}, use_global_device_ids=true | all-gather | bytes 1179648 | tf_op jit(solution)/shard_map/all_gather | solution.py:233
  59.1 5.5 %collective-permute-done.1 = bf16[4,12,32,128]{3,2,1,0:T(8,128)(2,1)S(1)} collective-permute-done((bf16[4,12,32,128]{3,2,1,0:T(8,128)(2,1)S(1)}, bf16[4,12,32,128]{3,2,1,0:T(8,128)(2,1)S(1)}, u32[]{:S(2)}, u32[]{:S(2)}) %collective-permute-start.1) | collective-permute-done | bytes 393248 | tf_op jit(solution)/shard_map/ppermute | solution.py:186
  64.6 2.4 %all-gather.1 = bf16[8,12,32,128]{3,2,1,0:T(8,128)(2,1)S(1)} all-gather(bf16[4,12,32,128]{3,2,1,0:T(8,128)(2,1)S(1)} %collective-permute-done.1), channel_id=3, replica_groups=mesh['y'=4,'zhigh'=4,'zmid'=2,'zlow'=2,'core'=2,'rep'=4] {'core'}, dimensions={0}, use_global_device_ids=true | all-gather | bytes 1179648 | tf_op jit(solution)/shard_map/all_gather | solution.py:235
  67.0 1.6 %select.1 = bf16[8,32,32,128]{3,2,1,0:T(8,128)(2,1)S(1)} custom-call(s32[8,32]{1,0:T(8,128)S(1)} %bitcast.23, bf16[2,4,12,32,128]{4,3,2,1,0:T(8,128)(2,1)S(1)} %bitcast.20, bf16[2,4,12,32,128]{4,3,2,1,0:T(8,128)(2,1)S(1)} %bitcast.21), custom_call_target="tpu_custom_call" | custom-call | tf_op jit(solution)/shard_map/select/pallas_call | solution.py:236
  68.6 29.3 %all_to_all.26.vectors_ref = bf16[8,32,32,128]{3,2,1,0:T(8,128)(2,1)S(1)} all-to-all(bf16[8,32,32,128]{3,2,1,0:T(8,128)(2,1)S(1)} %select.1), channel_id=1, replica_groups={{0,8,128,136,256,264,384,392},{1,9,129,137,257,265,385,393},{2,10,130,1..., dimensions={0} | all-to-all | bytes 4194304 | tf_op jit(solution)/shard_map/all_to_all | solution.py:212
  98.0 4.2 %products.1 = (f32[72,32,128]{2,1,0:T(8,128)S(1)}, bf16[14,32,128]{2,1,0:T(8,128)(2,1)S(1)}, bf16[14,32,128]{2,1,0:T(8,128)(2,1)S(1)}) custom-call(s32[1,128]{1,0:T(1,128)S(1)} %bitcast.24, s32[1,128]{1,0:T(1,128)S(1)} %bitcast.25, bf16[8,32,32,128]{3,2,1,0:T(8,128)(2,1)S(1)} %all_to_all.26.vectors_ref, bf16[128,128,128]{2,1,0:T(8,128)(2,1)} %bitcast.26), custom_call_target="tpu_custom_call" | custom-call | tf_op jit(solution)/shard_map/products/pallas_call | solution.py:246
  102.2 3.9 %collective-permute-start.2 = (bf16[14,32,128]{2,1,0:T(8,128)(2,1)S(1)}, bf16[14,32,128]{2,1,0:T(8,128)(2,1)S(1)}, u32[]{:S(2)}, u32[]{:S(2)}) collective-permute-start(bf16[14,32,128]{2,1,0:T(8,128)(2,1)S(1)} %get-tuple-element.14), channel_id=1, source_target_pairs={{0,508},{4,8},{8,4},{12,16},{16,12},{20,24},{24,20},{28,32},{32,28... | collective-permute-start | bytes 344072 | tf_op jit(solution)/shard_map/ppermute | solution.py:186
  106.2 2.0 %all-gather.2 = bf16[28,32,128]{2,1,0:T(8,128)(2,1)S(1)} all-gather(bf16[14,32,128]{2,1,0:T(8,128)(2,1)S(1)} %get-tuple-element.13), channel_id=4, replica_groups=mesh['y'=4,'zhigh'=4,'zmid'=2,'zlow'=2,'core'=2,'rep'=4] {'core'}, dimensions={0}, use_global_device_ids=true | all-gather | bytes 344064 | tf_op jit(solution)/shard_map/all_gather | solution.py:268
  108.1 3.6 %collective-permute-done.2.far_ref = bf16[14,32,128]{2,1,0:T(8,128)(2,1)S(1)} collective-permute-done((bf16[14,32,128]{2,1,0:T(8,128)(2,1)S(1)}, bf16[14,32,128]{2,1,0:T(8,128)(2,1)S(1)}, u32[]{:S(2)}, u32[]{:S(2)}) %collective-permute-start.2) | collective-permute-done | bytes 114720 | tf_op jit(solution)/shard_map/ppermute | solution.py:186
  111.9 9.8 %all_to_all.27.parts_ref = bf16[4,50,8,128]{3,2,1,0:T(8,128)(2,1)S(1)} all-to-all(bf16[4,50,8,128]{3,2,1,0:T(8,128)(2,1)S(1)} %combine.1), channel_id=1, replica_groups=mesh['y'=4,'zhigh'=4,'zmid'=2,'zlow'=2,'core'=2,'rep'=4] {'rep'}, dimensions={0} | all-to-all | bytes 819200 | tf_op jit(solution)/shard_map/all_to_all | solution.py:278
  121.7 1.2 %inverse.1 = f32[8,6144]{1,0:T(8,128)} custom-call(bf16[4,50,8,128]{3,2,1,0:T(8,128)(2,1)S(1)} %all_to_all.27.parts_ref, f32[512,256]{1,0:T(8,128)S(1)} %copy-done), custom_call_target="tpu_custom_call" | custom-call | tf_op jit(solution)/shard_map/inverse/pallas_call | solution.py:279
  (11 shorter events, 0.1 us)
Async XLA Ops:
  0.7 14.6 %collective-permute-start = (f32[8,128]{1,0:T(8,128)S(1)}, f32[8,128]{1,0:T(8,128)S(1)}, u32[]{:S(2)}, u32[]{:S(2)}) collective-permute-start(f32[8,128]{1,0:T(8,128)S(1)} %slice.3), channel_id=1, source_target_pairs={{0,508},{4,0},{8,4},{12,8},{16,12},{20,16},{24,20},{28,24},{32,28}... | collective-permute-start | bytes 12296 | tf_op jit(solution)/shard_map/ppermute | solution.py:186
  15.3 0.9 copy-start.1
  17.4 9.2 %all-to-all-start = ((bf16[4,12,8,128]{3,2,1,0:T(8,128)(2,1)}), bf16[4,12,8,128]{3,2,1,0:T(8,128)(2,1)S(1)}, u32[]{:S(2)}, u32[]{:S(2)}) async-start(bf16[4,12,8,128]{3,2,1,0:T(8,128)(2,1)} %forward.1), calls=%async_computation | async-start | bytes 196608 | tf_op jit(solution)/shard_map/all_to_all | solution.py:226
  50.1 14.5 %collective-permute-start.1 = (bf16[4,12,32,128]{3,2,1,0:T(8,128)(2,1)S(1)}, bf16[4,12,32,128]{3,2,1,0:T(8,128)(2,1)S(1)}, u32[]{:S(2)}, u32[]{:S(2)}) collective-permute-start(bf16[4,12,32,128]{3,2,1,0:T(8,128)(2,1)S(1)} %all_gather.21), channel_id=1, source_target_pairs={{0,16},{4,116},{8,24},{12,124},{16,0},{20,36},{24,8},{28,44},{32,4... | collective-permute-start | bytes 1179656 | tf_op jit(solution)/shard_map/ppermute | solution.py:186
  52.0 14.9 %all-to-all-start.1 = ((s32[8,1,32]{2,1,0:T(1,128)}), s32[8,1,32]{2,1,0:T(1,128)S(1)}, u32[]{:S(2)}, u32[]{:S(2)}) async-start(s32[8,1,32]{2,1,0:T(1,128)} %bitcast.6), calls=%async_computation.1 | async-start | bytes 8192 | tf_op jit(solution)/shard_map/all_to_all | solution.py:212
  68.6 29.4 %copy-start.2 = (s32[1,1,128]{2,1,0:T(1,128)S(1)}, s32[1,1,128]{2,1,0:T(1,128)}, u32[]{:S(2)}) copy-start(s32[1,1,128]{2,1,0:T(1,128)} %param.8) | copy-start | bytes 1540
  68.6 29.4 %copy-start.3 = (s32[1,1,128]{2,1,0:T(1,128)S(1)}, s32[1,1,128]{2,1,0:T(1,128)}, u32[]{:S(2)}) copy-start(s32[1,1,128]{2,1,0:T(1,128)} %param.9) | copy-start | bytes 1540
  102.2 19.5 %copy-start = (f32[512,256]{1,0:T(8,128)S(1)}, f32[512,256]{1,0:T(8,128)}, u32[]{:S(2)}) copy-start(f32[512,256]{1,0:T(8,128)} %constant.2.clone.taps_ref) | copy-start | bytes 1572868
  102.2 9.6 %collective-permute-start.2 = (bf16[14,32,128]{2,1,0:T(8,128)(2,1)S(1)}, bf16[14,32,128]{2,1,0:T(8,128)(2,1)S(1)}, u32[]{:S(2)}, u32[]{:S(2)}) collective-permute-start(bf16[14,32,128]{2,1,0:T(8,128)(2,1)S(1)} %get-tuple-element.14), channel_id=1, source_target_pairs={{0,508},{4,8},{8,4},{12,16},{16,12},{20,24},{24,20},{28,32},{32,28... | collective-permute-start | bytes 344072 | tf_op jit(solution)/shard_map/ppermute | solution.py:186

commit v6 on v4

--- a/solution.py
+++ b/solution.py
@@ -33,7 +33,6 @@
 PORTS_DEV = 8
 PORTS = PORTS_DEV * NR
 NNZ = 128
-NNZ_STEP = 64
 UP_ROWS = MARGIN + 2
 VMEM = pl.BlockSpec(memory_space=pltpu.VMEM)
 SMEM = pl.BlockSpec(memory_space=pltpu.SMEM)
@@ -77,7 +76,9 @@
     for b in range(BLOCKS_HERE):
         rows = PORTS_DEV * (b % LOWS)
         lanes = BS * (b // LOWS)
-        out_ref[b % NR, b // NR] = bands[rows : rows + PORTS_DEV, lanes : lanes + BS]
+        block = bands[rows : rows + PORTS_DEV, lanes : lanes + BS]
+        for high in range(NH):
+            out_ref[high, b % NR, b // NR] = block
 
 
 def select_kernel(wanted_ref, same_ref, other_ref, out_ref):
@@ -106,16 +107,10 @@
 
 
 def product_kernel(rows_ref, slots_ref, vectors_ref, coupling_ref, total_ref, near_ref, far_ref):
-    step = pl.program_id(0)
     edge = seg_index() * BLOCKS_HERE - MARGIN
     parity = lax.axis_index("zlow")
-
-    @pl.when(step == 0)
-    def _():
-        total_ref[...] = jnp.zeros_like(total_ref)
-
-    for i in range(NNZ_STEP):
-        n = step * NNZ_STEP + i
+    total_ref[...] = jnp.zeros_like(total_ref)
+    for n in range(NNZ):
         row = rows_ref[0, n] - edge
         row = jnp.where(row < 0, row + BLOCKS_ALL, row)
         row = jnp.where(row >= BLOCKS_ALL, row - BLOCKS_ALL, row)
@@ -126,7 +121,7 @@
         place = ((z >> 2) * NL + ((z & 1) ^ parity)) * NC * 2 + (slot & 3)
         product = lax.dot_general(
             vectors_ref[sender, place],
-            coupling_ref[i],
+            coupling_ref[n],
             (((1,), (1,)), ((), ())),
             preferred_element_type=jnp.float32,
         )
@@ -139,10 +134,9 @@
         up_ref[MARGIN] = total_ref[MARGIN + LOWS - 1].astype(jnp.bfloat16)
         up_ref[MARGIN + 1] = total_ref[MARGIN + BLOCKS_HERE - 1].astype(jnp.bfloat16)
 
-    last = step == NNZ // NNZ_STEP - 1
     core = lax.axis_index("core")
-    pl.when(last & (core == 0))(lambda: margins(near_ref, far_ref))
-    pl.when(last & (core == 1))(lambda: margins(far_ref, near_ref))
+    pl.when(core == 0)(lambda: margins(near_ref, far_ref))
+    pl.when(core == 1)(lambda: margins(far_ref, near_ref))
 
 
 def combine_kernel(total_ref, nears_ref, far_ref, out_ref):
@@ -213,17 +207,18 @@
     next_head = route(currents[:, :BS], lambda i: i - 1)
     residues = pl.pallas_call(
         forward_kernel,
-        out_shape=jax.ShapeDtypeStruct((NR, KEPT, PORTS_DEV, BS), bf16),
+        out_shape=jax.ShapeDtypeStruct((NH, NR, KEPT, PORTS_DEV, BS), bf16),
         in_specs=[VMEM, VMEM],
         out_specs=VMEM,
         compiler_params=PARAMS,
         name="forward",
     )(currents, next_head)
-    residues = lax.all_to_all(residues, "rep", 0, 0, tiled=True)
-    same = residues.transpose(1, 0, 2, 3).reshape(KEPT, PORTS, BS)
+    residues = residues.reshape(NH * NR, KEPT, PORTS_DEV, BS)
+    same = lax.all_to_all(residues, ("zhigh", "rep"), 0, 0, tiled=True)
+    same = same.reshape(NH, NR, KEPT, PORTS_DEV, BS).transpose(0, 2, 1, 3, 4)
+    same = same.reshape(NH, KEPT, PORTS, BS)
     wanted = requested.reshape(NY, NH, NM, NL * NC * 2).transpose(0, 2, 1, 3)
     wanted = wanted.reshape(NY * NM, SLOTS)
-    same = lax.all_gather(same, "zhigh", axis=0)
     same, wanted = lax.optimization_barrier((same, wanted))
     other = route(same, lambda i: i ^ NC)
     same = lax.all_gather(same, "core", axis=0)
@@ -238,27 +233,16 @@
         name="select",
     )(wanted, same, other)
     vectors = to_window(chosen)
-    whole = lambda *shape: pl.BlockSpec(shape, lambda n: (0,) * len(shape))
     total, near, far = pl.pallas_call(
         product_kernel,
-        grid=(NNZ // NNZ_STEP,),
         out_shape=[
             jax.ShapeDtypeStruct((WINDOW, PORTS, BS), jnp.float32),
             jax.ShapeDtypeStruct((UP_ROWS, PORTS, BS), bf16),
             jax.ShapeDtypeStruct((UP_ROWS, PORTS, BS), bf16),
         ],
-        in_specs=[
-            SMEM,
-            SMEM,
-            whole(*vectors.shape),
-            pl.BlockSpec((NNZ_STEP, BS, BS), lambda n: (n, 0, 0)),
-        ],
-        out_specs=[
-            whole(WINDOW, PORTS, BS),
-            whole(UP_ROWS, PORTS, BS),
-            whole(UP_ROWS, PORTS, BS),
-        ],
-        compiler_params=PARAMS,
+        in_specs=[SMEM, SMEM, VMEM, VMEM],
+        out_specs=[VMEM, VMEM, VMEM],
+        compiler_params=pltpu.CompilerParams(vmem_limit_bytes=24 * 1024 * 1024),
         name="products",
     )(block_rows[0], block_slots[0], vectors, coupling[0, 0])
     nears = lax.all_gather(near, "core", axis=0)

time: 124 us -> 128 us (1.032)
  blocking collectives: 72.9 us -> 54.3 us
  waiting for transfers between devices: 8.88 us -> 23 us
  starting transfers between devices: 29.9 us -> 39.6 us
    all_gather x1 -> x0, blocking collectives: 23.5 us -> none  [shards(): same = lax.all_gather(same, 'zhigh', axis=0)]
    all_to_all x1, waiting for transfers between devices: 2.79 us -> 17.7 us  [shards(): same = lax.all_to_all(residues, ('zhigh', 'rep'), 0, 0, tiled=True)]
    ppermute x3, starting transfers between devices: 20.3 us -> 28.4 us  [route(): lax.ppermute(block, FINE, [(i, partner(i) % count) for i in range(count)])]
    all_to_all x1, blocking collectives: 31.5 us -> 34.7 us  [to_window(): lax.all_to_all(block, EVERY, 0, 0, tiled=True, axis_index_groups=windows())]
    all_to_all x1, starting transfers between devices: 4.83 us -> 6.72 us  [shards(): same = lax.all_to_all(residues, ('zhigh', 'rep'), 0, 0, tiled=True)]
    all_to_all x1, waiting for transfers between devices: 1.69 us -> 0.01 us  [to_window(): lax.all_to_all(block, EVERY, 0, 0, tiled=True, axis_index_groups=windows())]
  transfers between devices with their start and end apart: 5 -> 5, of which waited for: 5 -> 4; matrix products, arithmetic and copies ran while one was open for 1% -> 1% of each run, Pallas kernels for 0% -> 0%
where the time goes in v6:
time: 128 us; the launch traced here: 127 us
  blocking collectives  54.3 us (42%)
  starting transfers between devices  39.6 us (31%)
  waiting for transfers between devices  23 us (18%)
  Pallas kernels  6.99 us (5%)
  local copies, waits for them, and re-layouts  3.26 us (3%)
    all_to_all x1, blocking collectives, to_window(): lax.all_to_all(block, EVERY, 0, 0, tiled=True, axis_index_groups=windows())  34.7 us
    ppermute x3, starting transfers between devices, route(): lax.ppermute(block, FINE, [(i, partner(i) % count) for i in range(count)])  28.4 us
    all_to_all x1, waiting for transfers between devices, shards(): same = lax.all_to_all(residues, ('zhigh', 'rep'), 0, 0, tiled=True)  17.7 us
    all_to_all x1, blocking collectives, shards(): parts = lax.all_to_all(parts, 'rep', 0, 0, tiled=True)  11.8 us
    all_to_all x1, starting transfers between devices, shards(): same = lax.all_to_all(residues, ('zhigh', 'rep'), 0, 0, tiled=True)  6.72 us
    ppermute x3, waiting for transfers between devices, route(): lax.ppermute(block, FINE, [(i, partner(i) % count) for i in range(count)])  5.32 us
    all_to_all x1, starting transfers between devices, to_window(): lax.all_to_all(block, EVERY, 0, 0, tiled=True, axis_index_groups=windows())  4.48 us
    all_gather x1, blocking collectives, shards(): same = lax.all_gather(same, 'core', axis=0)  3.47 us
  transfers between devices with their start and end apart: 5, of which 4 were waited for; matrix products, arithmetic and copies ran while one was open for 1% of the time, Pallas kernels for 0%

profile of v6, /device:TPU:2, one launch (start us, length us, event | category | flops | bytes accessed | tf_op | source)
XLA Modules:
  0.0 127.3 jit_solution(2756047005316070367)
XLA Ops:
  0.0 0.7 slice.3
  0.7 13.3 %collective-permute-start = (f32[8,128]{1,0:T(8,128)S(1)}, f32[8,128]{1,0:T(8,128)S(1)}, u32[]{:S(2)}, u32[]{:S(2)}) collective-permute-start(f32[8,128]{1,0:T(8,128)S(1)} %slice.3), channel_id=1, source_target_pairs={{0,508},{4,0},{8,4},{12,8},{16,12},{20,16},{24,20},{28,24},{32,28}... | collective-permute-start | bytes 12296 | tf_op jit(solution)/shard_map/ppermute | solution.py:180
  14.0 1.3 %collective-permute-done.next_ref = f32[8,128]{1,0:T(8,128)S(1)} collective-permute-done((f32[8,128]{1,0:T(8,128)S(1)}, f32[8,128]{1,0:T(8,128)S(1)}, u32[]{:S(2)}, u32[]{:S(2)}) %collective-permute-start) | collective-permute-done | bytes 4128 | tf_op jit(solution)/shard_map/ppermute | solution.py:180
  15.3 0.9 copy-done.2
  16.2 1.3 %forward.1 = bf16[4,4,12,8,128]{4,3,2,1,0:T(8,128)(2,1)} custom-call(f32[8,6144]{1,0:T(8,128)S(1)} %copy-done.2, f32[8,128]{1,0:T(8,128)S(1)} %collective-permute-done.next_ref), custom_call_target="tpu_custom_call" | custom-call | tf_op jit(solution)/shard_map/forward/pallas_call | solution.py:208
  17.5 6.7 %all-to-all-start = ((bf16[16,12,8,128]{3,2,1,0:T(8,128)(2,1)}), bf16[16,12,8,128]{3,2,1,0:T(8,128)(2,1)S(1)}, u32[]{:S(2)}, u32[]{:S(2)}) async-start(bf16[16,12,8,128]{3,2,1,0:T(8,128)(2,1)} %bitcast.2), calls=%async_computation | async-start | bytes 786432 | tf_op jit(solution)/shard_map/all_to_all | solution.py:217
  24.3 0.8 copy.14
  25.0 0.1 reshape.20
  25.1 0.7 reshape.21
  25.8 17.7 %all-to-all-done = bf16[16,12,8,128]{3,2,1,0:T(8,128)(2,1)S(1)} async-done(((bf16[16,12,8,128]{3,2,1,0:T(8,128)(2,1)}), bf16[16,12,8,128]{3,2,1,0:T(8,128)(2,1)S(1)}, u32[]{:S(2)}, u32[]{:S(2)}) %all-to-all-start) | async-done | bytes 393248 | tf_op jit(solution)/shard_map/all_to_all | solution.py:217
  43.5 0.1 copy.18
  43.6 10.3 %collective-permute-start.1 = (bf16[4,12,32,128]{3,2,1,0:T(8,128)(2,1)S(1)}, bf16[4,12,32,128]{3,2,1,0:T(8,128)(2,1)S(1)}, u32[]{:S(2)}, u32[]{:S(2)}) collective-permute-start(bf16[4,12,32,128]{3,2,1,0:T(8,128)(2,1)S(1)} %bitcast.28), channel_id=1, source_target_pairs={{0,8},{4,12},{8,0},{12,4},{16,24},{20,28},{24,16},{28,20},{32,40},... | collective-permute-start | bytes 1179656 | tf_op jit(solution)/shard_map/ppermute | solution.py:180
  54.0 4.5 %all-to-all-start.1 = ((s32[8,1,32]{2,1,0:T(1,128)}), s32[8,1,32]{2,1,0:T(1,128)S(1)}, u32[]{:S(2)}, u32[]{:S(2)}) async-start(s32[8,1,32]{2,1,0:T(1,128)} %bitcast.8), calls=%async_computation.1 | async-start | bytes 8192 | tf_op jit(solution)/shard_map/all_to_all | solution.py:202
  58.4 3.5 %all-gather = bf16[8,12,32,128]{3,2,1,0:T(8,128)(2,1)S(1)} all-gather(bf16[4,12,32,128]{3,2,1,0:T(8,128)(2,1)S(1)} %bitcast.29), channel_id=2, replica_groups=mesh['y'=4,'zhigh'=4,'zmid'=2,'zlow'=2,'core'=2,'rep'=4] {'core'}, dimensions={0}, use_global_device_ids=true | all-gather | bytes 1179648 | tf_op jit(solution)/shard_map/all_gather | solution.py:224
  61.9 1.2 collective-permute-done.1
  63.2 2.4 %all-gather.1 = bf16[8,12,32,128]{3,2,1,0:T(8,128)(2,1)S(1)} all-gather(bf16[4,12,32,128]{3,2,1,0:T(8,128)(2,1)S(1)} %collective-permute-done.1), channel_id=3, replica_groups=mesh['y'=4,'zhigh'=4,'zmid'=2,'zlow'=2,'core'=2,'rep'=4] {'core'}, dimensions={0}, use_global_device_ids=true | all-gather | bytes 1179648 | tf_op jit(solution)/shard_map/all_gather | solution.py:226
  65.5 1.5 %select.1 = bf16[8,32,32,128]{3,2,1,0:T(8,128)(2,1)S(1)} custom-call(s32[8,32]{1,0:T(8,128)S(1)} %bitcast.24, bf16[2,4,12,32,128]{4,3,2,1,0:T(8,128)(2,1)S(1)} %bitcast.21, bf16[2,4,12,32,128]{4,3,2,1,0:T(8,128)(2,1)S(1)} %bitcast.22), custom_call_target="tpu_custom_call" | custom-call | tf_op jit(solution)/shard_map/select/pallas_call | solution.py:227
  67.0 34.7 %all_to_all.26.vectors_ref = bf16[8,32,32,128]{3,2,1,0:T(8,128)(2,1)S(1)} all-to-all(bf16[8,32,32,128]{3,2,1,0:T(8,128)(2,1)S(1)} %select.1), channel_id=1, replica_groups={{0,16,128,144,256,272,384,400},{1,17,129,145,257,273,385,401},{2,18,130..., dimensions={0} | all-to-all | bytes 4194304 | tf_op jit(solution)/shard_map/all_to_all | solution.py:202
  101.7 2.9 %products.1 = (f32[72,32,128]{2,1,0:T(8,128)S(1)}, bf16[14,32,128]{2,1,0:T(8,128)(2,1)S(1)}, bf16[14,32,128]{2,1,0:T(8,128)(2,1)S(1)}) custom-call(s32[1,128]{1,0:T(1,128)S(1)} %bitcast.25, s32[1,128]{1,0:T(1,128)S(1)} %bitcast.26, bf16[8,32,32,128]{3,2,1,0:T(8,128)(2,1)S(1)} %all_to_all.26.vectors_ref, bf16[128,128,128]{2,1,0:T(8,128)(2,1)S(1)} %bitcast.20), custom_call_target="tpu_custom_call" | custom-call | tf_op jit(solution)/shard_map/products/pallas_call | solution.py:236
  104.6 4.8 %collective-permute-start.2 = (bf16[14,32,128]{2,1,0:T(8,128)(2,1)S(1)}, bf16[14,32,128]{2,1,0:T(8,128)(2,1)S(1)}, u32[]{:S(2)}, u32[]{:S(2)}) collective-permute-start(bf16[14,32,128]{2,1,0:T(8,128)(2,1)S(1)} %get-tuple-element.14), channel_id=1, source_target_pairs={{0,508},{4,8},{8,4},{12,16},{16,12},{20,24},{24,20},{28,32},{32,28... | collective-permute-start | bytes 344072 | tf_op jit(solution)/shard_map/ppermute | solution.py:180
  109.5 2.0 %all-gather.2 = bf16[28,32,128]{2,1,0:T(8,128)(2,1)S(1)} all-gather(bf16[14,32,128]{2,1,0:T(8,128)(2,1)S(1)} %get-tuple-element.13), channel_id=4, replica_groups=mesh['y'=4,'zhigh'=4,'zmid'=2,'zlow'=2,'core'=2,'rep'=4] {'core'}, dimensions={0}, use_global_device_ids=true | all-gather | bytes 344064 | tf_op jit(solution)/shard_map/all_gather | solution.py:248
  111.4 2.8 %collective-permute-done.2.far_ref = bf16[14,32,128]{2,1,0:T(8,128)(2,1)S(1)} collective-permute-done((bf16[14,32,128]{2,1,0:T(8,128)(2,1)S(1)}, bf16[14,32,128]{2,1,0:T(8,128)(2,1)S(1)}, u32[]{:S(2)}, u32[]{:S(2)}) %collective-permute-start.2) | collective-permute-done | bytes 114720 | tf_op jit(solution)/shard_map/ppermute | solution.py:180
  114.3 11.8 %all_to_all.27.parts_ref = bf16[4,50,8,128]{3,2,1,0:T(8,128)(2,1)S(1)} all-to-all(bf16[4,50,8,128]{3,2,1,0:T(8,128)(2,1)S(1)} %combine.1), channel_id=1, replica_groups=mesh['y'=4,'zhigh'=4,'zmid'=2,'zlow'=2,'core'=2,'rep'=4] {'rep'}, dimensions={0} | all-to-all | bytes 819200 | tf_op jit(solution)/shard_map/all_to_all | solution.py:258
  126.1 1.2 inverse.1
  (12 shorter events, 0.1 us)
Async XLA Ops:
  0.7 14.6 %collective-permute-start = (f32[8,128]{1,0:T(8,128)S(1)}, f32[8,128]{1,0:T(8,128)S(1)}, u32[]{:S(2)}, u32[]{:S(2)}) collective-permute-start(f32[8,128]{1,0:T(8,128)S(1)} %slice.3), channel_id=1, source_target_pairs={{0,508},{4,0},{8,4},{12,8},{16,12},{20,16},{24,20},{28,24},{32,28}... | collective-permute-start | bytes 12296 | tf_op jit(solution)/shard_map/ppermute | solution.py:180
  15.3 0.9 copy-start.2
  17.5 26.0 %all-to-all-start = ((bf16[16,12,8,128]{3,2,1,0:T(8,128)(2,1)}), bf16[16,12,8,128]{3,2,1,0:T(8,128)(2,1)S(1)}, u32[]{:S(2)}, u32[]{:S(2)}) async-start(bf16[16,12,8,128]{3,2,1,0:T(8,128)(2,1)} %bitcast.2), calls=%async_computation | async-start | bytes 786432 | tf_op jit(solution)/shard_map/all_to_all | solution.py:217
  43.6 19.5 %collective-permute-start.1 = (bf16[4,12,32,128]{3,2,1,0:T(8,128)(2,1)S(1)}, bf16[4,12,32,128]{3,2,1,0:T(8,128)(2,1)S(1)}, u32[]{:S(2)}, u32[]{:S(2)}) collective-permute-start(bf16[4,12,32,128]{3,2,1,0:T(8,128)(2,1)S(1)} %bitcast.28), channel_id=1, source_target_pairs={{0,8},{4,12},{8,0},{12,4},{16,24},{20,28},{24,16},{28,20},{32,40},... | collective-permute-start | bytes 1179656 | tf_op jit(solution)/shard_map/ppermute | solution.py:180
  54.0 11.6 %all-to-all-start.1 = ((s32[8,1,32]{2,1,0:T(1,128)}), s32[8,1,32]{2,1,0:T(1,128)S(1)}, u32[]{:S(2)}, u32[]{:S(2)}) async-start(s32[8,1,32]{2,1,0:T(1,128)} %bitcast.8), calls=%async_computation.1 | async-start | bytes 8192 | tf_op jit(solution)/shard_map/all_to_all | solution.py:202
  67.0 34.7 %copy-start = (bf16[1,1,128,128,128]{4,3,2,1,0:T(8,128)(2,1)S(1)}, bf16[1,1,128,128,128]{4,3,2,1,0:T(8,128)(2,1)}, u32[]{:S(2)}) copy-start(bf16[1,1,128,128,128]{4,3,2,1,0:T(8,128)(2,1)} %param.10) | copy-start | bytes 12582916
  67.0 34.7 %copy-start.3 = (s32[1,1,128]{2,1,0:T(1,128)S(1)}, s32[1,1,128]{2,1,0:T(1,128)}, u32[]{:S(2)}) copy-start(s32[1,1,128]{2,1,0:T(1,128)} %param.8) | copy-start | bytes 1540
  67.0 34.7 %copy-start.4 = (s32[1,1,128]{2,1,0:T(1,128)S(1)}, s32[1,1,128]{2,1,0:T(1,128)}, u32[]{:S(2)}) copy-start(s32[1,1,128]{2,1,0:T(1,128)} %param.9) | copy-start | bytes 1540
  104.6 21.5 %copy-start.1 = (f32[512,256]{1,0:T(8,128)S(1)}, f32[512,256]{1,0:T(8,128)}, u32[]{:S(2)}) copy-start(f32[512,256]{1,0:T(8,128)} %constant.2.clone.taps_ref) | copy-start | bytes 1572868
  104.6 9.6 %collective-permute-start.2 = (bf16[14,32,128]{2,1,0:T(8,128)(2,1)S(1)}, bf16[14,32,128]{2,1,0:T(8,128)(2,1)S(1)}, u32[]{:S(2)}, u32[]{:S(2)}) collective-permute-start(bf16[14,32,128]{2,1,0:T(8,128)(2,1)S(1)} %get-tuple-element.14), channel_id=1, source_target_pairs={{0,508},{4,8},{8,4},{12,16},{16,12},{20,24},{24,20},{28,32},{32,28... | collective-permute-start | bytes 344072 | tf_op jit(solution)/shard_map/ppermute | solution.py:180

commit v7 on v6

--- a/solution.py
+++ b/solution.py
@@ -26,10 +26,9 @@
 BLOCKS_HERE = 48
 MARGIN = BLOCKS_HERE // 4
 WINDOW = BLOCKS_HERE + 2 * MARGIN
-KEPT = BLOCKS_HERE // NR
 BLOCKS_ALL = BLOCKS_HERE * NY * NZ * NC
 LOWS = BLOCKS_HERE // 2
-SLOTS = NH * NL * NC * 2
+SLOTS = NH * NM * NC * 2
 PORTS_DEV = 8
 PORTS = PORTS_DEV * NR
 NNZ = 128
@@ -76,28 +75,23 @@
     for b in range(BLOCKS_HERE):
         rows = PORTS_DEV * (b % LOWS)
         lanes = BS * (b // LOWS)
-        block = bands[rows : rows + PORTS_DEV, lanes : lanes + BS]
-        for high in range(NH):
-            out_ref[high, b % NR, b // NR] = block
+        out_ref[b] = bands[rows : rows + PORTS_DEV, lanes : lanes + BS]
 
 
 def select_kernel(wanted_ref, same_ref, other_ref, out_ref):
-    parity = lax.axis_index("zlow")
+    middle = lax.axis_index("zmid")
 
     def one(reader, carry):
         for high in range(NH):
-            found = []
             for swap, table_ref in enumerate((same_ref, other_ref)):
-                asked = (high * NL + (parity ^ swap)) * NC * 2
+                place = (high * NM + (middle ^ swap)) * NC * 2
                 for core in range(NC):
                     for k in range(2):
-                        block = jnp.maximum(wanted_ref[reader, asked + 2 * core + k], 0)
-                        found.append(table_ref[core, high, block >> 2])
-            for i, block in enumerate(found):
-                out_ref[reader, high * NL * NC * 2 + i] = block
+                        slot = place + 2 * core + k
+                        out_ref[reader, slot] = table_ref[core, high, wanted_ref[reader, slot]]
         return carry
 
-    lax.fori_loop(0, NY * NM, one, 0)
+    lax.fori_loop(0, NY * NL * NR, one, 0)
 
 
 def seg_index():
@@ -108,7 +102,6 @@
 
 def product_kernel(rows_ref, slots_ref, vectors_ref, coupling_ref, total_ref, near_ref, far_ref):
     edge = seg_index() * BLOCKS_HERE - MARGIN
-    parity = lax.axis_index("zlow")
     total_ref[...] = jnp.zeros_like(total_ref)
     for n in range(NNZ):
         row = rows_ref[0, n] - edge
@@ -117,10 +110,11 @@
         slot = slots_ref[0, n]
         source = slot >> 1
         z = (source >> 1) & (NZ - 1)
-        sender = (source >> 5) * NM + ((z >> 1) & 1)
-        place = ((z >> 2) * NL + ((z & 1) ^ parity)) * NC * 2 + (slot & 3)
+        sender = (source >> 5) * NL + (z & 1)
+        place = (z >> 1) * NC * 2 + (slot & 3)
+        vector = jnp.concatenate([vectors_ref[sender, r, place] for r in range(NR)], axis=0)
         product = lax.dot_general(
-            vectors_ref[sender, place],
+            vector,
             coupling_ref[n],
             (((1,), (1,)), ((), ())),
             preferred_element_type=jnp.float32,
@@ -183,19 +177,23 @@
 def windows():
     groups = []
     for core in range(NC):
-        for first in range(0, NZ, 4):
-            for odd in range(2):
-                start = first + odd + 2 * core
-                members = sorted(((z >> 1) & 1, z % NZ) for z in (start, start + 2))
-                for r in range(NR):
-                    groups.append(
-                        [
-                            ((y * NZ + z) * NC + core) * NR + r
-                            for y in range(NY)
-                            for _, z in members
-                        ]
-                    )
+        for even in range(0, NZ, 2):
+            odd = (even + 1 - 2 * core) % NZ
+            groups.append(
+                [
+                    ((y * NZ + z) * NC + core) * NR + r
+                    for y in range(NY)
+                    for z in (even, odd)
+                    for r in range(NR)
+                ]
+            )
     return groups
+
+
+def two_away(i):
+    core, z, y = i % NC, i // NC % NZ, i // (NC * NZ)
+    step = 2 if (z >> 1) % 2 == core else -2
+    return (y * NZ + (z + step) % NZ) * NC + core
 
 
 def to_window(block):
@@ -205,34 +203,32 @@
 def shards(currents, requested, block_rows, block_slots, coupling):
     bf16 = jnp.bfloat16
     next_head = route(currents[:, :BS], lambda i: i - 1)
-    residues = pl.pallas_call(
+    same = pl.pallas_call(
         forward_kernel,
-        out_shape=jax.ShapeDtypeStruct((NH, NR, KEPT, PORTS_DEV, BS), bf16),
+        out_shape=jax.ShapeDtypeStruct((BLOCKS_HERE, PORTS_DEV, BS), bf16),
         in_specs=[VMEM, VMEM],
         out_specs=VMEM,
         compiler_params=PARAMS,
         name="forward",
     )(currents, next_head)
-    residues = residues.reshape(NH * NR, KEPT, PORTS_DEV, BS)
-    same = lax.all_to_all(residues, ("zhigh", "rep"), 0, 0, tiled=True)
-    same = same.reshape(NH, NR, KEPT, PORTS_DEV, BS).transpose(0, 2, 1, 3, 4)
-    same = same.reshape(NH, KEPT, PORTS, BS)
-    wanted = requested.reshape(NY, NH, NM, NL * NC * 2).transpose(0, 2, 1, 3)
-    wanted = wanted.reshape(NY * NM, SLOTS)
+    wanted = jnp.maximum(requested, 0).reshape(NY, NH * NM, NL, NC * 2).transpose(0, 2, 1, 3)
+    wanted = jnp.broadcast_to(wanted.reshape(NY, NL, 1, SLOTS), (NY, NL, NR, SLOTS))
+    wanted = wanted.reshape(NY * NL * NR, SLOTS)
+    same = lax.all_gather(same, "zhigh", axis=0)
     same, wanted = lax.optimization_barrier((same, wanted))
-    other = route(same, lambda i: i ^ NC)
+    other = route(same, two_away)
     same = lax.all_gather(same, "core", axis=0)
     wanted = to_window(wanted)
     other = lax.all_gather(other, "core", axis=0)
     chosen = pl.pallas_call(
         select_kernel,
-        out_shape=jax.ShapeDtypeStruct((NY * NM, SLOTS, PORTS, BS), bf16),
+        out_shape=jax.ShapeDtypeStruct((NY * NL * NR, SLOTS, PORTS_DEV, BS), bf16),
         in_specs=[SMEM, VMEM, VMEM],
         out_specs=VMEM,
         compiler_params=PARAMS,
         name="select",
     )(wanted, same, other)
-    vectors = to_window(chosen)
+    vectors = to_window(chosen).reshape(NY * NL, NR, SLOTS, PORTS_DEV, BS)
     total, near, far = pl.pallas_call(
         product_kernel,
         out_shape=[

time: 128 us -> 119 us (0.930)
  the two profiles are of different devices: /device:TPU:2 before, /device:TPU:8 now
where the time goes in v7:
time: 119 us
  blocking collectives  76.3 us (64%)
  starting transfers between devices  25.4 us (21%)
  Pallas kernels  8.53 us (7%)
  waiting for transfers between devices  5.25 us (4%)
  local copies, waits for them, and re-layouts  2.54 us (2%)
    all_to_all x1, blocking collectives, to_window(): lax.all_to_all(block, EVERY, 0, 0, tiled=True, axis_index_groups=windows())  34.4 us
    all_gather x1, blocking collectives, shards(): same = lax.all_gather(same, 'zhigh', axis=0)  22.9 us
    ppermute x3, starting transfers between devices, route(): lax.ppermute(block, FINE, [(i, partner(i) % count) for i in range(count)])  17.9 us
    all_to_all x1, blocking collectives, shards(): parts = lax.all_to_all(parts, 'rep', 0, 0, tiled=True)  12 us
    all_to_all x1, starting transfers between devices, to_window(): lax.all_to_all(block, EVERY, 0, 0, tiled=True, axis_index_groups=windows())  7.55 us
    ppermute x3, waiting for transfers between devices, route(): lax.ppermute(block, FINE, [(i, partner(i) % count) for i in range(count)])  4.29 us
    pallas_call x1, Pallas kernels, shards(): pl.pallas_call(select_kernel, out_shape=jax.ShapeDtypeStruct((NY * NL * N...  3.72 us
    pallas_call x1, Pallas kernels, shards(): pl.pallas_call(product_kernel, out_shape=[jax.ShapeDtypeStruct((WINDOW, P...  2.92 us
  transfers between devices with their start and end apart: 4, of which 4 were waited for; matrix products, arithmetic and copies ran while one was open for 1% of the time, Pallas kernels for 0%

profile of v7, /device:TPU:8, one launch (start us, length us, event | category | flops | bytes accessed | tf_op | source)
XLA Modules:
  0.0 118.8 jit_solution(10216412392103246703)
XLA Ops:
  0.0 0.7 slice.3
  0.7 10.7 %collective-permute-start = (f32[8,128]{1,0:T(8,128)S(1)}, f32[8,128]{1,0:T(8,128)S(1)}, u32[]{:S(2)}, u32[]{:S(2)}) collective-permute-start(f32[8,128]{1,0:T(8,128)S(1)} %slice.3), channel_id=1, source_target_pairs={{0,508},{4,0},{8,4},{12,8},{16,12},{20,16},{24,20},{28,24},{32,28}... | collective-permute-start | bytes 12296 | tf_op jit(solution)/shard_map/ppermute | solution.py:174
  11.4 0.7 broadcast_maximum_fusion
  12.1 0.1 copy.9
  12.2 0.1 reshape.13
  12.4 0.3 collective-permute-done.next_ref
  12.7 0.9 copy-done.2
  13.6 0.6 forward.1
  14.2 22.9 %all-gather = bf16[192,8,128]{2,1,0:T(8,128)(2,1)S(1)} all-gather(bf16[48,8,128]{2,1,0:T(8,128)(2,1)S(1)} %forward.1), channel_id=2, replica_groups=mesh['y'=4,'zhigh'=4,'zmid'=2,'zlow'=2,'core'=2,'rep'=4] {'zhigh'}, dimensions={0}, use_global_device_ids=true | all-gather | bytes 491520 | tf_op jit(solution)/shard_map/all_gather | solution.py:217
  37.2 0.6 broadcast_in_dim.8
  37.8 3.1 %collective-permute-start.1 = (bf16[4,48,8,128]{3,2,1,0:T(8,128)(2,1)S(1)}, bf16[4,48,8,128]{3,2,1,0:T(8,128)(2,1)S(1)}, u32[]{:S(2)}, u32[]{:S(2)}) collective-permute-start(bf16[4,48,8,128]{3,2,1,0:T(8,128)(2,1)S(1)} %bitcast.24), channel_id=1, source_target_pairs={{0,16},{4,116},{8,24},{12,124},{16,0},{20,36},{24,8},{28,44},{32,4... | collective-permute-start | bytes 1179656 | tf_op jit(solution)/shard_map/ppermute | solution.py:174
  40.9 7.6 %all-to-all-start = ((s32[32,1,32]{2,1,0:T(1,128)}), s32[32,1,32]{2,1,0:T(1,128)S(1)}, u32[]{:S(2)}, u32[]{:S(2)}) async-start(s32[32,1,32]{2,1,0:T(1,128)} %bitcast.5), calls=%async_computation | async-start | bytes 32768 | tf_op jit(solution)/shard_map/all_to_all | solution.py:200
  48.4 2.6 %all-gather.1 = bf16[8,48,8,128]{3,2,1,0:T(8,128)(2,1)S(1)} all-gather(bf16[4,48,8,128]{3,2,1,0:T(8,128)(2,1)S(1)} %bitcast.25), channel_id=3, replica_groups=mesh['y'=4,'zhigh'=4,'zmid'=2,'zlow'=2,'core'=2,'rep'=4] {'core'}, dimensions={0}, use_global_device_ids=true | all-gather | bytes 1179648 | tf_op jit(solution)/shard_map/all_gather | solution.py:220
  51.0 1.7 %collective-permute-done.1 = bf16[4,48,8,128]{3,2,1,0:T(8,128)(2,1)S(1)} collective-permute-done((bf16[4,48,8,128]{3,2,1,0:T(8,128)(2,1)S(1)}, bf16[4,48,8,128]{3,2,1,0:T(8,128)(2,1)S(1)}, u32[]{:S(2)}, u32[]{:S(2)}) %collective-permute-start.1) | collective-permute-done | bytes 393248 | tf_op jit(solution)/shard_map/ppermute | solution.py:174
  52.7 2.4 %all-gather.2 = bf16[8,48,8,128]{3,2,1,0:T(8,128)(2,1)S(1)} all-gather(bf16[4,48,8,128]{3,2,1,0:T(8,128)(2,1)S(1)} %collective-permute-done.1), channel_id=4, replica_groups=mesh['y'=4,'zhigh'=4,'zmid'=2,'zlow'=2,'core'=2,'rep'=4] {'core'}, dimensions={0}, use_global_device_ids=true | all-gather | bytes 1179648 | tf_op jit(solution)/shard_map/all_gather | solution.py:222
  55.0 1.0 all-to-all-done
  56.0 3.7 %select.1 = bf16[32,32,8,128]{3,2,1,0:T(8,128)(2,1)S(1)} custom-call(s32[32,32]{1,0:T(8,128)S(1)} %bitcast.21, bf16[2,4,48,8,128]{4,3,2,1,0:T(8,128)(2,1)S(1)} %bitcast.18, bf16[2,4,48,8,128]{4,3,2,1,0:T(8,128)(2,1)S(1)} %bitcast.19), custom_call_target="tpu_custom_call" | custom-call | tf_op jit(solution)/shard_map/select/pallas_call | solution.py:223
  59.7 34.4 %all_to_all.21 = bf16[32,32,8,128]{3,2,1,0:T(8,128)(2,1)S(1)} all-to-all(bf16[32,32,8,128]{3,2,1,0:T(8,128)(2,1)S(1)} %select.1), channel_id=1, replica_groups={{0,1,2,3,8,9,10,11,128,129,130,131,136,137,138,139,256,257,258,259,264,..., dimensions={0} | all-to-all | bytes 4194304 | tf_op jit(solution)/shard_map/all_to_all | solution.py:200
  94.2 2.9 %products.1 = (f32[72,32,128]{2,1,0:T(8,128)S(1)}, bf16[14,32,128]{2,1,0:T(8,128)(2,1)S(1)}, bf16[14,32,128]{2,1,0:T(8,128)(2,1)S(1)}) custom-call(s32[1,128]{1,0:T(1,128)S(1)} %bitcast.22, s32[1,128]{1,0:T(1,128)S(1)} %bitcast.23, bf16[8,4,32,8,128]{4,3,2,1,0:T(8,128)(2,1)S(1)} %bitcast.16, bf16[128,128,128]{2,1,0:T(8,128)(2,1)S(1)} %bitcast.17), custom_call_target="tpu_custom_call" | custom-call | tf_op jit(solution)/shard_map/products/pallas_call | solution.py:232
  97.1 4.0 %collective-permute-start.2 = (bf16[14,32,128]{2,1,0:T(8,128)(2,1)S(1)}, bf16[14,32,128]{2,1,0:T(8,128)(2,1)S(1)}, u32[]{:S(2)}, u32[]{:S(2)}) collective-permute-start(bf16[14,32,128]{2,1,0:T(8,128)(2,1)S(1)} %get-tuple-element.14), channel_id=1, source_target_pairs={{0,508},{4,8},{8,4},{12,16},{16,12},{20,24},{24,20},{28,32},{32,28... | collective-permute-start | bytes 344072 | tf_op jit(solution)/shard_map/ppermute | solution.py:174
  101.2 2.0 %all-gather.3 = bf16[28,32,128]{2,1,0:T(8,128)(2,1)S(1)} all-gather(bf16[14,32,128]{2,1,0:T(8,128)(2,1)S(1)} %get-tuple-element.13), channel_id=5, replica_groups=mesh['y'=4,'zhigh'=4,'zmid'=2,'zlow'=2,'core'=2,'rep'=4] {'core'}, dimensions={0}, use_global_device_ids=true | all-gather | bytes 344064 | tf_op jit(solution)/shard_map/all_gather | solution.py:244
  103.1 2.3 %collective-permute-done.2.far_ref = bf16[14,32,128]{2,1,0:T(8,128)(2,1)S(1)} collective-permute-done((bf16[14,32,128]{2,1,0:T(8,128)(2,1)S(1)}, bf16[14,32,128]{2,1,0:T(8,128)(2,1)S(1)}, u32[]{:S(2)}, u32[]{:S(2)}) %collective-permute-start.2) | collective-permute-done | bytes 114720 | tf_op jit(solution)/shard_map/ppermute | solution.py:174
  105.5 12.0 %all_to_all.22.parts_ref = bf16[4,50,8,128]{3,2,1,0:T(8,128)(2,1)S(1)} all-to-all(bf16[4,50,8,128]{3,2,1,0:T(8,128)(2,1)S(1)} %combine.1), channel_id=1, replica_groups=mesh['y'=4,'zhigh'=4,'zmid'=2,'zlow'=2,'core'=2,'rep'=4] {'rep'}, dimensions={0} | all-to-all | bytes 819200 | tf_op jit(solution)/shard_map/all_to_all | solution.py:254
  117.6 1.2 %inverse.1 = f32[8,6144]{1,0:T(8,128)} custom-call(bf16[4,50,8,128]{3,2,1,0:T(8,128)(2,1)S(1)} %all_to_all.22.parts_ref, f32[512,256]{1,0:T(8,128)S(1)} %copy-done.1), custom_call_target="tpu_custom_call" | custom-call | tf_op jit(solution)/shard_map/inverse/pallas_call | solution.py:255
  (12 shorter events, 0.2 us)
Async XLA Ops:
  0.7 12.0 %collective-permute-start = (f32[8,128]{1,0:T(8,128)S(1)}, f32[8,128]{1,0:T(8,128)S(1)}, u32[]{:S(2)}, u32[]{:S(2)}) collective-permute-start(f32[8,128]{1,0:T(8,128)S(1)} %slice.3), channel_id=1, source_target_pairs={{0,508},{4,0},{8,4},{12,8},{16,12},{20,16},{24,20},{28,24},{32,28}... | collective-permute-start | bytes 12296 | tf_op jit(solution)/shard_map/ppermute | solution.py:174
  12.7 0.9 copy-start.2
  37.8 14.9 %collective-permute-start.1 = (bf16[4,48,8,128]{3,2,1,0:T(8,128)(2,1)S(1)}, bf16[4,48,8,128]{3,2,1,0:T(8,128)(2,1)S(1)}, u32[]{:S(2)}, u32[]{:S(2)}) collective-permute-start(bf16[4,48,8,128]{3,2,1,0:T(8,128)(2,1)S(1)} %bitcast.24), channel_id=1, source_target_pairs={{0,16},{4,116},{8,24},{12,124},{16,0},{20,36},{24,8},{28,44},{32,4... | collective-permute-start | bytes 1179656 | tf_op jit(solution)/shard_map/ppermute | solution.py:174
  40.9 15.1 %all-to-all-start = ((s32[32,1,32]{2,1,0:T(1,128)}), s32[32,1,32]{2,1,0:T(1,128)S(1)}, u32[]{:S(2)}, u32[]{:S(2)}) async-start(s32[32,1,32]{2,1,0:T(1,128)} %bitcast.5), calls=%async_computation | async-start | bytes 32768 | tf_op jit(solution)/shard_map/all_to_all | solution.py:200
  59.7 34.5 %copy-start = (bf16[1,1,128,128,128]{4,3,2,1,0:T(8,128)(2,1)S(1)}, bf16[1,1,128,128,128]{4,3,2,1,0:T(8,128)(2,1)}, u32[]{:S(2)}) copy-start(bf16[1,1,128,128,128]{4,3,2,1,0:T(8,128)(2,1)} %param.10) | copy-start | bytes 12582916
  59.7 34.4 %copy-start.3 = (s32[1,1,128]{2,1,0:T(1,128)S(1)}, s32[1,1,128]{2,1,0:T(1,128)}, u32[]{:S(2)}) copy-start(s32[1,1,128]{2,1,0:T(1,128)} %param.8) | copy-start | bytes 1540
  59.7 34.4 %copy-start.4 = (s32[1,1,128]{2,1,0:T(1,128)S(1)}, s32[1,1,128]{2,1,0:T(1,128)}, u32[]{:S(2)}) copy-start(s32[1,1,128]{2,1,0:T(1,128)} %param.9) | copy-start | bytes 1540
  97.1 20.5 %copy-start.1 = (f32[512,256]{1,0:T(8,128)S(1)}, f32[512,256]{1,0:T(8,128)}, u32[]{:S(2)}) copy-start(f32[512,256]{1,0:T(8,128)} %constant.4.clone.taps_ref) | copy-start | bytes 1572868
  97.1 8.4 %collective-permute-start.2 = (bf16[14,32,128]{2,1,0:T(8,128)(2,1)S(1)}, bf16[14,32,128]{2,1,0:T(8,128)(2,1)S(1)}, u32[]{:S(2)}, u32[]{:S(2)}) collective-permute-start(bf16[14,32,128]{2,1,0:T(8,128)(2,1)S(1)} %get-tuple-element.14), channel_id=1, source_target_pairs={{0,508},{4,8},{8,4},{12,16},{16,12},{20,24},{24,20},{28,32},{32,28... | collective-permute-start | bytes 344072 | tf_op jit(solution)/shard_map/ppermute | solution.py:174

commit v8 on v7

--- a/solution.py
+++ b/solution.py
@@ -55,7 +55,7 @@
     return jnp.dot(a, b, precision=lax.Precision.HIGHEST, preferred_element_type=jnp.float32)
 
 
-def forward_kernel(x_ref, next_ref, out_ref):
+def forward_kernel(x_ref, out_ref):
     wide = 2 * BS
     row = lax.broadcasted_iota(jnp.int32, (wide + BS, wide), 0)
     lane = lax.broadcasted_iota(jnp.int32, (wide + BS, wide), 1)
@@ -68,14 +68,29 @@
         [x_ref[:, wide * b : wide * (b + 1)] for b in range(LOWS)], axis=0
     )
     after = jnp.concatenate(
-        [x_ref[:, wide * b : wide * b + BS] for b in range(1, LOWS)] + [next_ref[...]], axis=0
+        [x_ref[:, wide * b : wide * b + BS] for b in range(1, LOWS)]
+        + [jnp.zeros((PORTS_DEV, BS), jnp.float32)],
+        axis=0,
     )
     bands = dot_exact(here, taps[:wide]) + dot_exact(after, taps[wide:])
-    bands = bands.astype(jnp.bfloat16)
     for b in range(BLOCKS_HERE):
         rows = PORTS_DEV * (b % LOWS)
         lanes = BS * (b // LOWS)
         out_ref[b] = bands[rows : rows + PORTS_DEV, lanes : lanes + BS]
+
+
+def finish_kernel(bands_ref, next_ref, asked_ref, out_ref, wanted_ref):
+    lane = lax.broadcasted_iota(jnp.int32, (PORTS_DEV, BS), 1)
+    for b in range(BLOCKS_HERE):
+        band = bands_ref[b]
+        if b % LOWS == LOWS - 1:
+            taps = HIGH_PASS if b // LOWS else LOW_PASS
+            head = taps[2] * next_ref[:, 0:1] + taps[3] * next_ref[:, 1:2]
+            band = band + jnp.where(lane == BS - 1, head, 0.0)
+        out_ref[b] = band.astype(jnp.bfloat16)
+    for i in range(NY * NL):
+        row = jnp.maximum(asked_ref[i : i + 1], 0)
+        wanted_ref[NR * i : NR * (i + 1)] = jnp.broadcast_to(row, (NR, SLOTS))
 
 
 def select_kernel(wanted_ref, same_ref, other_ref, out_ref):
@@ -203,17 +218,27 @@
 def shards(currents, requested, block_rows, block_slots, coupling):
     bf16 = jnp.bfloat16
     next_head = route(currents[:, :BS], lambda i: i - 1)
-    same = pl.pallas_call(
+    bands = pl.pallas_call(
         forward_kernel,
-        out_shape=jax.ShapeDtypeStruct((BLOCKS_HERE, PORTS_DEV, BS), bf16),
-        in_specs=[VMEM, VMEM],
+        out_shape=jax.ShapeDtypeStruct((BLOCKS_HERE, PORTS_DEV, BS), jnp.float32),
+        in_specs=[VMEM],
         out_specs=VMEM,
         compiler_params=PARAMS,
         name="forward",
-    )(currents, next_head)
-    wanted = jnp.maximum(requested, 0).reshape(NY, NH * NM, NL, NC * 2).transpose(0, 2, 1, 3)
-    wanted = jnp.broadcast_to(wanted.reshape(NY, NL, 1, SLOTS), (NY, NL, NR, SLOTS))
-    wanted = wanted.reshape(NY * NL * NR, SLOTS)
+    )(currents)
+    asked = requested.reshape(NY, NH * NM, NL, NC * 2).transpose(0, 2, 1, 3)
+    asked = asked.reshape(NY * NL, SLOTS)
+    same, wanted = pl.pallas_call(
+        finish_kernel,
+        out_shape=[
+            jax.ShapeDtypeStruct((BLOCKS_HERE, PORTS_DEV, BS), bf16),
+            jax.ShapeDtypeStruct((NY * NL * NR, SLOTS), jnp.int32),
+        ],
+        in_specs=[VMEM, VMEM, VMEM],
+        out_specs=[VMEM, VMEM],
+        compiler_params=PARAMS,
+        name="finish",
+    )(bands, next_head, asked)
     same = lax.all_gather(same, "zhigh", axis=0)
     same, wanted = lax.optimization_barrier((same, wanted))
     other = route(same, two_away)

time: 119 us -> 119 us (level)
  the two profiles are of different devices: /device:TPU:8 before, /device:TPU:2 now
where the time goes in v8:
time: 119 us
  blocking collectives  72.7 us (61%)
  starting transfers between devices  28.2 us (24%)
  Pallas kernels  9.16 us (8%)
  waiting for transfers between devices  5.92 us (5%)
  local copies, waits for them, and re-layouts  2.59 us (2%)
    all_to_all x1, blocking collectives, to_window(): lax.all_to_all(block, EVERY, 0, 0, tiled=True, axis_index_groups=windows())  31.5 us
    all_gather x1, blocking collectives, shards(): same = lax.all_gather(same, 'zhigh', axis=0)  22.5 us
    ppermute x3, starting transfers between devices, route(): lax.ppermute(block, FINE, [(i, partner(i) % count) for i in range(count)])  19 us
    all_to_all x1, blocking collectives, shards(): parts = lax.all_to_all(parts, 'rep', 0, 0, tiled=True)  11.9 us
    all_to_all x1, starting transfers between devices, to_window(): lax.all_to_all(block, EVERY, 0, 0, tiled=True, axis_index_groups=windows())  9.17 us
    pallas_call x1, Pallas kernels, shards(): pl.pallas_call(select_kernel, out_shape=jax.ShapeDtypeStruct((NY * NL * N...  3.72 us
    ppermute x3, waiting for transfers between devices, route(): lax.ppermute(block, FINE, [(i, partner(i) % count) for i in range(count)])  3.65 us
    pallas_call x1, Pallas kernels, shards(): pl.pallas_call(product_kernel, out_shape=[jax.ShapeDtypeStruct((WINDOW, P...  2.92 us
  transfers between devices with their start and end apart: 4, of which 2 were waited for; matrix products, arithmetic and copies ran while one was open for 1% of the time, Pallas kernels for 0%

profile of v8, /device:TPU:2, one launch (start us, length us, event | category | flops | bytes accessed | tf_op | source)
XLA Modules:
  0.0 118.7 jit_solution(12232783780037440356)
XLA Ops:
  0.0 0.7 slice.3
  0.7 13.3 %collective-permute-start = (f32[8,128]{1,0:T(8,128)S(1)}, f32[8,128]{1,0:T(8,128)S(1)}, u32[]{:S(2)}, u32[]{:S(2)}) collective-permute-start(f32[8,128]{1,0:T(8,128)S(1)} %slice.3), channel_id=1, source_target_pairs={{0,508},{4,0},{8,4},{12,8},{16,12},{20,16},{24,20},{28,24},{32,28}... | collective-permute-start | bytes 12296 | tf_op jit(solution)/shard_map/ppermute | solution.py:189
  14.0 0.9 copy-done.2
  14.9 0.6 forward.1.bands_ref
  15.5 0.8 copy.9
  16.3 0.1 reshape.11
  16.4 0.1 reshape.12.asked_ref
  16.5 0.6 finish.1
  17.1 22.5 %all-gather = bf16[192,8,128]{2,1,0:T(8,128)(2,1)S(1)} all-gather(bf16[48,8,128]{2,1,0:T(8,128)(2,1)S(1)} %get-tuple-element.12), channel_id=2, replica_groups=mesh['y'=4,'zhigh'=4,'zmid'=2,'zlow'=2,'core'=2,'rep'=4] {'zhigh'}, dimensions={0}, use_global_device_ids=true | all-gather | bytes 491520 | tf_op jit(solution)/shard_map/all_gather | solution.py:242
  39.6 1.9 %collective-permute-start.1 = (bf16[4,48,8,128]{3,2,1,0:T(8,128)(2,1)S(1)}, bf16[4,48,8,128]{3,2,1,0:T(8,128)(2,1)S(1)}, u32[]{:S(2)}, u32[]{:S(2)}) collective-permute-start(bf16[4,48,8,128]{3,2,1,0:T(8,128)(2,1)S(1)} %bitcast.25), channel_id=1, source_target_pairs={{0,16},{4,116},{8,24},{12,124},{16,0},{20,36},{24,8},{28,44},{32,4... | collective-permute-start | bytes 1179656 | tf_op jit(solution)/shard_map/ppermute | solution.py:189
  41.5 9.2 %all-to-all-start = ((s32[32,1,32]{2,1,0:T(1,128)}), s32[32,1,32]{2,1,0:T(1,128)S(1)}, u32[]{:S(2)}, u32[]{:S(2)}) async-start(s32[32,1,32]{2,1,0:T(1,128)} %bitcast.5), calls=%async_computation | async-start | bytes 32768 | tf_op jit(solution)/shard_map/all_to_all | solution.py:215
  50.7 2.4 %all-gather.1 = bf16[8,48,8,128]{3,2,1,0:T(8,128)(2,1)S(1)} all-gather(bf16[4,48,8,128]{3,2,1,0:T(8,128)(2,1)S(1)} %bitcast.26), channel_id=3, replica_groups=mesh['y'=4,'zhigh'=4,'zmid'=2,'zlow'=2,'core'=2,'rep'=4] {'core'}, dimensions={0}, use_global_device_ids=true | all-gather | bytes 1179648 | tf_op jit(solution)/shard_map/all_gather | solution.py:245
  53.1 2.4 %all-gather.2 = bf16[8,48,8,128]{3,2,1,0:T(8,128)(2,1)S(1)} all-gather(bf16[4,48,8,128]{3,2,1,0:T(8,128)(2,1)S(1)} %collective-permute-done.1), channel_id=4, replica_groups=mesh['y'=4,'zhigh'=4,'zmid'=2,'zlow'=2,'core'=2,'rep'=4] {'core'}, dimensions={0}, use_global_device_ids=true | all-gather | bytes 1179648 | tf_op jit(solution)/shard_map/all_gather | solution.py:247
  55.4 2.3 %all-to-all-done = s32[32,1,32]{2,1,0:T(1,128)S(1)} async-done(((s32[32,1,32]{2,1,0:T(1,128)}), s32[32,1,32]{2,1,0:T(1,128)S(1)}, u32[]{:S(2)}, u32[]{:S(2)}) %all-to-all-start) | async-done | bytes 4128 | tf_op jit(solution)/shard_map/all_to_all | solution.py:215
  57.7 3.7 %select.1 = bf16[32,32,8,128]{3,2,1,0:T(8,128)(2,1)S(1)} custom-call(s32[32,32]{1,0:T(8,128)S(1)} %bitcast.22, bf16[2,4,48,8,128]{4,3,2,1,0:T(8,128)(2,1)S(1)} %bitcast.19, bf16[2,4,48,8,128]{4,3,2,1,0:T(8,128)(2,1)S(1)} %bitcast.20), custom_call_target="tpu_custom_call" | custom-call | tf_op jit(solution)/shard_map/select/pallas_call | solution.py:248
  61.5 31.5 %all_to_all.21 = bf16[32,32,8,128]{3,2,1,0:T(8,128)(2,1)S(1)} all-to-all(bf16[32,32,8,128]{3,2,1,0:T(8,128)(2,1)S(1)} %select.1), channel_id=1, replica_groups={{0,1,2,3,8,9,10,11,128,129,130,131,136,137,138,139,256,257,258,259,264,..., dimensions={0} | all-to-all | bytes 4194304 | tf_op jit(solution)/shard_map/all_to_all | solution.py:215
  93.0 2.9 %products.1 = (f32[72,32,128]{2,1,0:T(8,128)S(1)}, bf16[14,32,128]{2,1,0:T(8,128)(2,1)S(1)}, bf16[14,32,128]{2,1,0:T(8,128)(2,1)S(1)}) custom-call(s32[1,128]{1,0:T(1,128)S(1)} %bitcast.23, s32[1,128]{1,0:T(1,128)S(1)} %bitcast.24, bf16[8,4,32,8,128]{4,3,2,1,0:T(8,128)(2,1)S(1)} %bitcast.17, bf16[128,128,128]{2,1,0:T(8,128)(2,1)S(1)} %bitcast.18), custom_call_target="tpu_custom_call" | custom-call | tf_op jit(solution)/shard_map/products/pallas_call | solution.py:257
  95.9 0.0 copy-start.1
  95.9 3.8 %collective-permute-start.2 = (bf16[14,32,128]{2,1,0:T(8,128)(2,1)S(1)}, bf16[14,32,128]{2,1,0:T(8,128)(2,1)S(1)}, u32[]{:S(2)}, u32[]{:S(2)}) collective-permute-start(bf16[14,32,128]{2,1,0:T(8,128)(2,1)S(1)} %get-tuple-element.18), channel_id=1, source_target_pairs={{0,508},{4,8},{8,4},{12,16},{16,12},{20,24},{24,20},{28,32},{32,28... | collective-permute-start | bytes 344072 | tf_op jit(solution)/shard_map/ppermute | solution.py:189
  99.8 2.1 %all-gather.3 = bf16[28,32,128]{2,1,0:T(8,128)(2,1)S(1)} all-gather(bf16[14,32,128]{2,1,0:T(8,128)(2,1)S(1)} %get-tuple-element.17), channel_id=5, replica_groups=mesh['y'=4,'zhigh'=4,'zmid'=2,'zlow'=2,'core'=2,'rep'=4] {'core'}, dimensions={0}, use_global_device_ids=true | all-gather | bytes 344064 | tf_op jit(solution)/shard_map/all_gather | solution.py:269
  101.9 3.6 %collective-permute-done.2.far_ref = bf16[14,32,128]{2,1,0:T(8,128)(2,1)S(1)} collective-permute-done((bf16[14,32,128]{2,1,0:T(8,128)(2,1)S(1)}, bf16[14,32,128]{2,1,0:T(8,128)(2,1)S(1)}, u32[]{:S(2)}, u32[]{:S(2)}) %collective-permute-start.2) | collective-permute-done | bytes 114720 | tf_op jit(solution)/shard_map/ppermute | solution.py:189
  105.5 0.1 combine.1
  105.6 11.9 %all_to_all.22.parts_ref = bf16[4,50,8,128]{3,2,1,0:T(8,128)(2,1)S(1)} all-to-all(bf16[4,50,8,128]{3,2,1,0:T(8,128)(2,1)S(1)} %combine.1), channel_id=1, replica_groups=mesh['y'=4,'zhigh'=4,'zmid'=2,'zlow'=2,'core'=2,'rep'=4] {'rep'}, dimensions={0} | all-to-all | bytes 819200 | tf_op jit(solution)/shard_map/all_to_all | solution.py:279
  117.5 1.2 %inverse.1 = f32[8,6144]{1,0:T(8,128)} custom-call(bf16[4,50,8,128]{3,2,1,0:T(8,128)(2,1)S(1)} %all_to_all.22.parts_ref, f32[512,256]{1,0:T(8,128)S(1)} %copy-done.1), custom_call_target="tpu_custom_call" | custom-call | tf_op jit(solution)/shard_map/inverse/pallas_call | solution.py:280
  (11 shorter events, 0.0 us)
Async XLA Ops:
  0.7 15.8 %collective-permute-start = (f32[8,128]{1,0:T(8,128)S(1)}, f32[8,128]{1,0:T(8,128)S(1)}, u32[]{:S(2)}, u32[]{:S(2)}) collective-permute-start(f32[8,128]{1,0:T(8,128)S(1)} %slice.3), channel_id=1, source_target_pairs={{0,508},{4,0},{8,4},{12,8},{16,12},{20,16},{24,20},{28,24},{32,28}... | collective-permute-start | bytes 12296 | tf_op jit(solution)/shard_map/ppermute | solution.py:189
  14.0 0.9 copy-start.2
  39.6 13.5 %collective-permute-start.1 = (bf16[4,48,8,128]{3,2,1,0:T(8,128)(2,1)S(1)}, bf16[4,48,8,128]{3,2,1,0:T(8,128)(2,1)S(1)}, u32[]{:S(2)}, u32[]{:S(2)}) collective-permute-start(bf16[4,48,8,128]{3,2,1,0:T(8,128)(2,1)S(1)} %bitcast.25), channel_id=1, source_target_pairs={{0,16},{4,116},{8,24},{12,124},{16,0},{20,36},{24,8},{28,44},{32,4... | collective-permute-start | bytes 1179656 | tf_op jit(solution)/shard_map/ppermute | solution.py:189
  41.5 16.2 %all-to-all-start = ((s32[32,1,32]{2,1,0:T(1,128)}), s32[32,1,32]{2,1,0:T(1,128)S(1)}, u32[]{:S(2)}, u32[]{:S(2)}) async-start(s32[32,1,32]{2,1,0:T(1,128)} %bitcast.5), calls=%async_computation | async-start | bytes 32768 | tf_op jit(solution)/shard_map/all_to_all | solution.py:215
  61.4 31.5 %copy-start = (bf16[1,1,128,128,128]{4,3,2,1,0:T(8,128)(2,1)S(1)}, bf16[1,1,128,128,128]{4,3,2,1,0:T(8,128)(2,1)}, u32[]{:S(2)}) copy-start(bf16[1,1,128,128,128]{4,3,2,1,0:T(8,128)(2,1)} %param.10) | copy-start | bytes 12582916
  61.5 31.5 %copy-start.3 = (s32[1,1,128]{2,1,0:T(1,128)S(1)}, s32[1,1,128]{2,1,0:T(1,128)}, u32[]{:S(2)}) copy-start(s32[1,1,128]{2,1,0:T(1,128)} %param.8) | copy-start | bytes 1540
  61.5 31.5 %copy-start.4 = (s32[1,1,128]{2,1,0:T(1,128)S(1)}, s32[1,1,128]{2,1,0:T(1,128)}, u32[]{:S(2)}) copy-start(s32[1,1,128]{2,1,0:T(1,128)} %param.9) | copy-start | bytes 1540
  95.9 21.5 %copy-start.1 = (f32[512,256]{1,0:T(8,128)S(1)}, f32[512,256]{1,0:T(8,128)}, u32[]{:S(2)}) copy-start(f32[512,256]{1,0:T(8,128)} %constant.2.clone.taps_ref) | copy-start | bytes 1572868
  95.9 9.6 %collective-permute-start.2 = (bf16[14,32,128]{2,1,0:T(8,128)(2,1)S(1)}, bf16[14,32,128]{2,1,0:T(8,128)(2,1)S(1)}, u32[]{:S(2)}, u32[]{:S(2)}) collective-permute-start(bf16[14,32,128]{2,1,0:T(8,128)(2,1)S(1)} %get-tuple-element.18), channel_id=1, source_target_pairs={{0,508},{4,8},{8,4},{12,16},{16,12},{20,24},{24,20},{28,32},{32,28... | collective-permute-start | bytes 344072 | tf_op jit(solution)/shard_map/ppermute | solution.py:189

commit v9 on v8

--- a/solution.py
+++ b/solution.py
@@ -115,7 +115,7 @@
     return (lax.axis_index("y") * NZ + z) * NC + lax.axis_index("core")
 
 
-def product_kernel(rows_ref, slots_ref, vectors_ref, coupling_ref, total_ref, near_ref, far_ref):
+def product_kernel(rows_ref, slots_ref, vectors_ref, coupling_ref, parts_ref, total_ref):
     edge = seg_index() * BLOCKS_HERE - MARGIN
     total_ref[...] = jnp.zeros_like(total_ref)
     for n in range(NNZ):
@@ -136,48 +136,51 @@
         )
         total_ref[row] += product
 
+    for r in range(NR):
+        for row in range(WINDOW):
+            parts_ref[r, row] = total_ref[row, PORTS_DEV * r : PORTS_DEV * (r + 1)].astype(
+                jnp.bfloat16
+            )
+
+
+def sum_kernel(parts_ref, total_ref, near_ref, far_ref):
+    total = parts_ref[0].astype(jnp.float32)
+    for r in range(1, NR):
+        total = total + parts_ref[r].astype(jnp.float32)
+    total_ref[...] = total
+
     def margins(up_ref, down_ref):
-        down_ref[:MARGIN] = total_ref[:MARGIN].astype(jnp.bfloat16)
-        down_ref[MARGIN:] = jnp.zeros((2, PORTS, BS), jnp.bfloat16)
-        up_ref[:MARGIN] = total_ref[MARGIN + BLOCKS_HERE :].astype(jnp.bfloat16)
-        up_ref[MARGIN] = total_ref[MARGIN + LOWS - 1].astype(jnp.bfloat16)
-        up_ref[MARGIN + 1] = total_ref[MARGIN + BLOCKS_HERE - 1].astype(jnp.bfloat16)
+        down_ref[:MARGIN] = total_ref[:MARGIN]
+        down_ref[MARGIN:] = jnp.zeros((2, PORTS_DEV, BS), jnp.float32)
+        up_ref[:MARGIN] = total_ref[MARGIN + BLOCKS_HERE :]
+        up_ref[MARGIN] = total_ref[MARGIN + LOWS - 1]
+        up_ref[MARGIN + 1] = total_ref[MARGIN + BLOCKS_HERE - 1]
 
     core = lax.axis_index("core")
     pl.when(core == 0)(lambda: margins(near_ref, far_ref))
     pl.when(core == 1)(lambda: margins(far_ref, near_ref))
 
 
-def combine_kernel(total_ref, nears_ref, far_ref, out_ref):
-    def combine(above_ref, below_ref):
-        for row in range(BLOCKS_HERE + 2):
-            if row < BLOCKS_HERE:
-                value = total_ref[MARGIN + row]
-                if row < MARGIN:
-                    value = value + above_ref[row].astype(jnp.float32)
-                if row >= BLOCKS_HERE - MARGIN:
-                    value = value + below_ref[row - BLOCKS_HERE + MARGIN].astype(jnp.float32)
-            else:
-                value = above_ref[MARGIN + row - BLOCKS_HERE].astype(jnp.float32)
-                if row == BLOCKS_HERE + 1:
-                    value = value + total_ref[MARGIN - 1]
-            for r in range(NR):
-                out_ref[r, row] = value[PORTS_DEV * r : PORTS_DEV * (r + 1)].astype(jnp.bfloat16)
-
-    core = lax.axis_index("core")
-    pl.when(core == 0)(lambda: combine(far_ref, nears_ref.at[1]))
-    pl.when(core == 1)(lambda: combine(nears_ref.at[0], far_ref))
-
-
-def inverse_kernel(parts_ref, taps_ref, out_ref):
-    rows = parts_ref[0].astype(jnp.float32)
-    for r in range(1, NR):
-        rows = rows + parts_ref[r].astype(jnp.float32)
+def inverse_kernel(total_ref, nears_ref, far_ref, taps_ref, out_ref):
+    first = lax.axis_index("core") == 0
+    above = jnp.where(first, far_ref[...], nears_ref[0])
+    below = jnp.where(first, nears_ref[1], far_ref[...])
+    own = total_ref[MARGIN : MARGIN + BLOCKS_HERE]
+    rows = jnp.concatenate(
+        [
+            own[:MARGIN] + above[:MARGIN],
+            own[MARGIN : BLOCKS_HERE - MARGIN],
+            own[BLOCKS_HERE - MARGIN :] + below[:MARGIN],
+        ],
+        axis=0,
+    )
+    low_edge = above[MARGIN]
+    high_edge = above[MARGIN + 1] + total_ref[MARGIN - 1]
     flat = LOWS * PORTS_DEV
     low = rows[:LOWS].reshape(flat, BS)
     high = rows[LOWS:BLOCKS_HERE].reshape(flat, BS)
-    low_before = jnp.concatenate([rows[BLOCKS_HERE], low[: flat - PORTS_DEV]], axis=0)
-    high_before = jnp.concatenate([rows[BLOCKS_HERE + 1], high[: flat - PORTS_DEV]], axis=0)
+    low_before = jnp.concatenate([low_edge, low[: flat - PORTS_DEV]], axis=0)
+    high_before = jnp.concatenate([high_edge, high[: flat - PORTS_DEV]], axis=0)
     stacked = jnp.concatenate([low, high, low_before, high_before], axis=1)
     volts = dot_exact(stacked, taps_ref[...])
     for b in range(LOWS):
@@ -254,37 +257,38 @@
         name="select",
     )(wanted, same, other)
     vectors = to_window(chosen).reshape(NY * NL, NR, SLOTS, PORTS_DEV, BS)
-    total, near, far = pl.pallas_call(
+    parts = pl.pallas_call(
         product_kernel,
-        out_shape=[
-            jax.ShapeDtypeStruct((WINDOW, PORTS, BS), jnp.float32),
-            jax.ShapeDtypeStruct((UP_ROWS, PORTS, BS), bf16),
-            jax.ShapeDtypeStruct((UP_ROWS, PORTS, BS), bf16),
-        ],
+        out_shape=jax.ShapeDtypeStruct((NR, WINDOW, PORTS_DEV, BS), bf16),
         in_specs=[SMEM, SMEM, VMEM, VMEM],
-        out_specs=[VMEM, VMEM, VMEM],
+        out_specs=VMEM,
+        scratch_shapes=[pltpu.VMEM((WINDOW, PORTS, BS), jnp.float32)],
         compiler_params=pltpu.CompilerParams(vmem_limit_bytes=24 * 1024 * 1024),
         name="products",
     )(block_rows[0], block_slots[0], vectors, coupling[0, 0])
+    parts = lax.all_to_all(parts, "rep", 0, 0, tiled=True)
+    total, near, far = pl.pallas_call(
+        sum_kernel,
+        out_shape=[
+            jax.ShapeDtypeStruct((WINDOW, PORTS_DEV, BS), jnp.float32),
+            jax.ShapeDtypeStruct((UP_ROWS, PORTS_DEV, BS), jnp.float32),
+            jax.ShapeDtypeStruct((UP_ROWS, PORTS_DEV, BS), jnp.float32),
+        ],
+        in_specs=[VMEM],
+        out_specs=[VMEM, VMEM, VMEM],
+        compiler_params=PARAMS,
+        name="sums",
+    )(parts)
     nears = lax.all_gather(near, "core", axis=0)
     far = route(far, lambda i: i + 1 if i % 2 else i - 1)
-    parts = pl.pallas_call(
-        combine_kernel,
-        out_shape=jax.ShapeDtypeStruct((NR, BLOCKS_HERE + 2, PORTS_DEV, BS), bf16),
-        in_specs=[VMEM, VMEM, VMEM],
-        out_specs=VMEM,
-        compiler_params=PARAMS,
-        name="combine",
-    )(total, nears, far)
-    parts = lax.all_to_all(parts, "rep", 0, 0, tiled=True)
     return pl.pallas_call(
         inverse_kernel,
         out_shape=jax.ShapeDtypeStruct(currents.shape, jnp.float32),
-        in_specs=[VMEM, VMEM],
+        in_specs=[VMEM, VMEM, VMEM, VMEM],
         out_specs=VMEM,
         compiler_params=PARAMS,
         name="inverse",
-    )(parts, jnp.asarray(inverse_matrix()))
+    )(total, nears, far, jnp.asarray(inverse_matrix()))
 
 
 def solution(mesh):

time: 119 us -> 121 us (1.017)
  the two profiles are of different devices: /device:TPU:2 before, /device:TPU:1 now
where the time goes in v9:
time: 121 us
  blocking collectives  74.6 us (62%)
  starting transfers between devices  33.4 us (28%)
  Pallas kernels  9.18 us (8%)
  local copies, waits for them, and re-layouts  2.59 us (2%)
    all_to_all x1, blocking collectives, to_window(): lax.all_to_all(block, EVERY, 0, 0, tiled=True, axis_index_groups=windows())  31.4 us
    all_gather x1, blocking collectives, shards(): same = lax.all_gather(same, 'zhigh', axis=0)  22.4 us
    ppermute x3, starting transfers between devices, route(): lax.ppermute(block, FINE, [(i, partner(i) % count) for i in range(count)])  22.1 us
    all_to_all x1, blocking collectives, shards(): parts = lax.all_to_all(parts, 'rep', 0, 0, tiled=True)  11.3 us
    all_to_all x1, starting transfers between devices, to_window(): lax.all_to_all(block, EVERY, 0, 0, tiled=True, axis_index_groups=windows())  11.3 us
    all_gather x1, blocking collectives, shards(): same = lax.all_gather(same, 'core', axis=0)  5.17 us
    pallas_call x1, Pallas kernels, shards(): pl.pallas_call(select_kernel, out_shape=jax.ShapeDtypeStruct((NY * NL * N...  3.72 us
    pallas_call x1, Pallas kernels, shards(): pl.pallas_call(product_kernel, out_shape=jax.ShapeDtypeStruct((NR, WINDOW...  2.98 us
  transfers between devices with their start and end apart: 4, of which 2 were waited for; matrix products, arithmetic and copies ran while one was open for 1% of the time, Pallas kernels for 0%

profile of v9, /device:TPU:1, one launch (start us, length us, event | category | flops | bytes accessed | tf_op | source)
XLA Modules:
  0.0 120.8 jit_solution(12960407659635690493)
XLA Ops:
  0.0 0.7 slice.3
  0.7 8.8 %collective-permute-start = (f32[8,128]{1,0:T(8,128)S(1)}, f32[8,128]{1,0:T(8,128)S(1)}, u32[]{:S(2)}, u32[]{:S(2)}) collective-permute-start(f32[8,128]{1,0:T(8,128)S(1)} %slice.3), channel_id=1, source_target_pairs={{0,508},{4,0},{8,4},{12,8},{16,12},{20,16},{24,20},{28,24},{32,28}... | collective-permute-start | bytes 12296 | tf_op jit(solution)/shard_map/ppermute | solution.py:192
  9.5 0.9 copy-done.2
  10.4 0.6 forward.1.bands_ref
  11.0 0.8 copy.9
  11.8 0.1 reshape.11
  11.9 0.1 reshape.12.asked_ref
  12.0 0.6 finish.1
  12.6 22.4 %all-gather = bf16[192,8,128]{2,1,0:T(8,128)(2,1)S(1)} all-gather(bf16[48,8,128]{2,1,0:T(8,128)(2,1)S(1)} %get-tuple-element.12), channel_id=2, replica_groups=mesh['y'=4,'zhigh'=4,'zmid'=2,'zlow'=2,'core'=2,'rep'=4] {'zhigh'}, dimensions={0}, use_global_device_ids=true | all-gather | bytes 491520 | tf_op jit(solution)/shard_map/all_gather | solution.py:245
  35.0 2.4 %collective-permute-start.1 = (bf16[4,48,8,128]{3,2,1,0:T(8,128)(2,1)S(1)}, bf16[4,48,8,128]{3,2,1,0:T(8,128)(2,1)S(1)}, u32[]{:S(2)}, u32[]{:S(2)}) collective-permute-start(bf16[4,48,8,128]{3,2,1,0:T(8,128)(2,1)S(1)} %bitcast.25), channel_id=1, source_target_pairs={{0,16},{4,116},{8,24},{12,124},{16,0},{20,36},{24,8},{28,44},{32,4... | collective-permute-start | bytes 1179656 | tf_op jit(solution)/shard_map/ppermute | solution.py:192
  37.5 11.3 %all-to-all-start = ((s32[32,1,32]{2,1,0:T(1,128)}), s32[32,1,32]{2,1,0:T(1,128)S(1)}, u32[]{:S(2)}, u32[]{:S(2)}) async-start(s32[32,1,32]{2,1,0:T(1,128)} %bitcast.5), calls=%async_computation | async-start | bytes 32768 | tf_op jit(solution)/shard_map/all_to_all | solution.py:218
  48.7 5.2 %all-gather.1 = bf16[8,48,8,128]{3,2,1,0:T(8,128)(2,1)S(1)} all-gather(bf16[4,48,8,128]{3,2,1,0:T(8,128)(2,1)S(1)} %bitcast.26), channel_id=3, replica_groups=mesh['y'=4,'zhigh'=4,'zmid'=2,'zlow'=2,'core'=2,'rep'=4] {'core'}, dimensions={0}, use_global_device_ids=true | all-gather | bytes 1179648 | tf_op jit(solution)/shard_map/all_gather | solution.py:248
  53.9 2.4 %all-gather.2 = bf16[8,48,8,128]{3,2,1,0:T(8,128)(2,1)S(1)} all-gather(bf16[4,48,8,128]{3,2,1,0:T(8,128)(2,1)S(1)} %collective-permute-done.1), channel_id=4, replica_groups=mesh['y'=4,'zhigh'=4,'zmid'=2,'zlow'=2,'core'=2,'rep'=4] {'core'}, dimensions={0}, use_global_device_ids=true | all-gather | bytes 1179648 | tf_op jit(solution)/shard_map/all_gather | solution.py:250
  56.3 0.7 all-to-all-done
  57.0 3.7 %select.1 = bf16[32,32,8,128]{3,2,1,0:T(8,128)(2,1)S(1)} custom-call(s32[32,32]{1,0:T(8,128)S(1)} %bitcast.22, bf16[2,4,48,8,128]{4,3,2,1,0:T(8,128)(2,1)S(1)} %bitcast.19, bf16[2,4,48,8,128]{4,3,2,1,0:T(8,128)(2,1)S(1)} %bitcast.20), custom_call_target="tpu_custom_call" | custom-call | tf_op jit(solution)/shard_map/select/pallas_call | solution.py:251
  60.8 31.4 %all_to_all.21 = bf16[32,32,8,128]{3,2,1,0:T(8,128)(2,1)S(1)} all-to-all(bf16[32,32,8,128]{3,2,1,0:T(8,128)(2,1)S(1)} %select.1), channel_id=1, replica_groups={{0,1,2,3,8,9,10,11,128,129,130,131,136,137,138,139,256,257,258,259,264,..., dimensions={0} | all-to-all | bytes 4194304 | tf_op jit(solution)/shard_map/all_to_all | solution.py:218
  92.2 3.0 %products.1 = bf16[4,72,8,128]{3,2,1,0:T(8,128)(2,1)S(1)} custom-call(s32[1,128]{1,0:T(1,128)S(1)} %bitcast.23, s32[1,128]{1,0:T(1,128)S(1)} %bitcast.24, bf16[8,4,32,8,128]{4,3,2,1,0:T(8,128)(2,1)S(1)} %bitcast.17, bf16[128,128,128]{2,1,0:T(8,128)(2,1)S(1)} %bitcast.18), custom_call_target="tpu_custom_call" | custom-call | tf_op jit(solution)/shard_map/products/pallas_call | solution.py:260
  95.2 0.0 copy-start.1
  95.2 11.3 %all_to_all.22.parts_ref = bf16[4,72,8,128]{3,2,1,0:T(8,128)(2,1)S(1)} all-to-all(bf16[4,72,8,128]{3,2,1,0:T(8,128)(2,1)S(1)} %products.1), channel_id=1, replica_groups=mesh['y'=4,'zhigh'=4,'zmid'=2,'zlow'=2,'core'=2,'rep'=4] {'rep'}, dimensions={0} | all-to-all | bytes 1179648 | tf_op jit(solution)/shard_map/all_to_all | solution.py:269
  106.5 0.1 sums.1
  106.6 10.9 %collective-permute-start.2 = (f32[14,8,128]{2,1,0:T(8,128)S(1)}, f32[14,8,128]{2,1,0:T(8,128)S(1)}, u32[]{:S(2)}, u32[]{:S(2)}) collective-permute-start(f32[14,8,128]{2,1,0:T(8,128)S(1)} %get-tuple-element.18), channel_id=1, source_target_pairs={{0,508},{4,8},{8,4},{12,16},{16,12},{20,24},{24,20},{28,32},{32,28... | collective-permute-start | bytes 172040 | tf_op jit(solution)/shard_map/ppermute | solution.py:192
  117.5 1.9 %all-gather.3 = f32[28,8,128]{2,1,0:T(8,128)S(1)} all-gather(f32[14,8,128]{2,1,0:T(8,128)S(1)} %get-tuple-element.17), channel_id=5, replica_groups=mesh['y'=4,'zhigh'=4,'zmid'=2,'zlow'=2,'core'=2,'rep'=4] {'core'}, dimensions={0}, use_global_device_ids=true | all-gather | bytes 172032 | tf_op jit(solution)/shard_map/all_gather | solution.py:282
  119.4 0.3 collective-permute-done.2.far_ref
  119.6 1.2 inverse.1
  (11 shorter events, 0.0 us)
Async XLA Ops:
  0.7 11.3 %collective-permute-start = (f32[8,128]{1,0:T(8,128)S(1)}, f32[8,128]{1,0:T(8,128)S(1)}, u32[]{:S(2)}, u32[]{:S(2)}) collective-permute-start(f32[8,128]{1,0:T(8,128)S(1)} %slice.3), channel_id=1, source_target_pairs={{0,508},{4,0},{8,4},{12,8},{16,12},{20,16},{24,20},{28,24},{32,28}... | collective-permute-start | bytes 12296 | tf_op jit(solution)/shard_map/ppermute | solution.py:192
  9.5 0.9 copy-start.2
  35.0 18.9 %collective-permute-start.1 = (bf16[4,48,8,128]{3,2,1,0:T(8,128)(2,1)S(1)}, bf16[4,48,8,128]{3,2,1,0:T(8,128)(2,1)S(1)}, u32[]{:S(2)}, u32[]{:S(2)}) collective-permute-start(bf16[4,48,8,128]{3,2,1,0:T(8,128)(2,1)S(1)} %bitcast.25), channel_id=1, source_target_pairs={{0,16},{4,116},{8,24},{12,124},{16,0},{20,36},{24,8},{28,44},{32,4... | collective-permute-start | bytes 1179656 | tf_op jit(solution)/shard_map/ppermute | solution.py:192
  37.5 19.6 %all-to-all-start = ((s32[32,1,32]{2,1,0:T(1,128)}), s32[32,1,32]{2,1,0:T(1,128)S(1)}, u32[]{:S(2)}, u32[]{:S(2)}) async-start(s32[32,1,32]{2,1,0:T(1,128)} %bitcast.5), calls=%async_computation | async-start | bytes 32768 | tf_op jit(solution)/shard_map/all_to_all | solution.py:218
  60.7 31.4 %copy-start = (bf16[1,1,128,128,128]{4,3,2,1,0:T(8,128)(2,1)S(1)}, bf16[1,1,128,128,128]{4,3,2,1,0:T(8,128)(2,1)}, u32[]{:S(2)}) copy-start(bf16[1,1,128,128,128]{4,3,2,1,0:T(8,128)(2,1)} %param.10) | copy-start | bytes 12582916
  60.8 31.4 %copy-start.3 = (s32[1,1,128]{2,1,0:T(1,128)S(1)}, s32[1,1,128]{2,1,0:T(1,128)}, u32[]{:S(2)}) copy-start(s32[1,1,128]{2,1,0:T(1,128)} %param.8) | copy-start | bytes 1540
  60.8 31.4 %copy-start.4 = (s32[1,1,128]{2,1,0:T(1,128)S(1)}, s32[1,1,128]{2,1,0:T(1,128)}, u32[]{:S(2)}) copy-start(s32[1,1,128]{2,1,0:T(1,128)} %param.9) | copy-start | bytes 1540
  95.2 24.4 %copy-start.1 = (f32[512,256]{1,0:T(8,128)S(1)}, f32[512,256]{1,0:T(8,128)}, u32[]{:S(2)}) copy-start(f32[512,256]{1,0:T(8,128)} %constant.2.clone.taps_ref) | copy-start | bytes 1572868
  106.6 13.0 %collective-permute-start.2 = (f32[14,8,128]{2,1,0:T(8,128)S(1)}, f32[14,8,128]{2,1,0:T(8,128)S(1)}, u32[]{:S(2)}, u32[]{:S(2)}) collective-permute-start(f32[14,8,128]{2,1,0:T(8,128)S(1)} %get-tuple-element.18), channel_id=1, source_target_pairs={{0,508},{4,8},{8,4},{12,16},{16,12},{20,24},{24,20},{28,32},{32,28... | collective-permute-start | bytes 172040 | tf_op jit(solution)/shard_map/ppermute | solution.py:192

commit v10 on v7

--- a/solution.py
+++ b/solution.py
@@ -39,15 +39,14 @@
 
 
 def inverse_matrix():
-    taps = np.zeros((4 * BS, 2 * BS), np.float32)
+    taps = np.zeros((2 * BS, 2 * BS), np.float32)
     for k in range(BS):
         for odd in range(2):
             taps[k, 2 * k + odd] = LOW_PASS[odd]
             taps[BS + k, 2 * k + odd] = HIGH_PASS[odd]
-            before = k - 1 if k else 2 * BS + BS - 1
-            taps[before, 2 * k + odd] = LOW_PASS[2 + odd]
-            before = BS + k - 1 if k else 3 * BS + BS - 1
-            taps[before, 2 * k + odd] = HIGH_PASS[2 + odd]
+            if k:
+                taps[k - 1, 2 * k + odd] = LOW_PASS[2 + odd]
+                taps[BS + k - 1, 2 * k + odd] = HIGH_PASS[2 + odd]
     return taps
 
 
@@ -55,7 +54,10 @@
     return jnp.dot(a, b, precision=lax.Precision.HIGHEST, preferred_element_type=jnp.float32)
 
 
-def forward_kernel(x_ref, next_ref, out_ref):
+def forward_kernel(x_ref, asked_ref, out_ref, wanted_ref):
+    asked = jnp.maximum(asked_ref[...], 0)
+    for i in range(NY * NL * NR):
+        wanted_ref[i] = asked
     wide = 2 * BS
     row = lax.broadcasted_iota(jnp.int32, (wide + BS, wide), 0)
     lane = lax.broadcasted_iota(jnp.int32, (wide + BS, wide), 1)
@@ -68,27 +70,42 @@
         [x_ref[:, wide * b : wide * (b + 1)] for b in range(LOWS)], axis=0
     )
     after = jnp.concatenate(
-        [x_ref[:, wide * b : wide * b + BS] for b in range(1, LOWS)] + [next_ref[...]], axis=0
+        [x_ref[:, wide * b : wide * b + BS] for b in range(1, LOWS)]
+        + [jnp.zeros((PORTS_DEV, BS), jnp.float32)],
+        axis=0,
     )
     bands = dot_exact(here, taps[:wide]) + dot_exact(after, taps[wide:])
-    bands = bands.astype(jnp.bfloat16)
     for b in range(BLOCKS_HERE):
         rows = PORTS_DEV * (b % LOWS)
         lanes = BS * (b // LOWS)
         out_ref[b] = bands[rows : rows + PORTS_DEV, lanes : lanes + BS]
 
 
+def finish_kernel(bands_ref, next_ref, out_ref):
+    lane = lax.broadcasted_iota(jnp.int32, (PORTS_DEV, BS), 1)
+    for b in range(BLOCKS_HERE):
+        band = bands_ref[b]
+        if b % LOWS == LOWS - 1:
+            taps = HIGH_PASS if b // LOWS else LOW_PASS
+            head = taps[2] * next_ref[:, 0:1] + taps[3] * next_ref[:, 1:2]
+            band = band + jnp.where(lane == BS - 1, head, 0.0)
+        out_ref[b] = band.astype(jnp.bfloat16)
+
+
 def select_kernel(wanted_ref, same_ref, other_ref, out_ref):
     middle = lax.axis_index("zmid")
+    corner = (lax.axis_index("y") * NZ + lax.axis_index("zlow")) * NC
 
     def one(reader, carry):
         for high in range(NH):
             for swap, table_ref in enumerate((same_ref, other_ref)):
-                place = (high * NM + (middle ^ swap)) * NC * 2
+                pair = high * NM + (middle ^ swap)
                 for core in range(NC):
+                    source = corner + pair * NL * NC + core
                     for k in range(2):
-                        slot = place + 2 * core + k
-                        out_ref[reader, slot] = table_ref[core, high, wanted_ref[reader, slot]]
+                        block = wanted_ref[reader, k, source]
+                        slot = (pair * NC + core) * 2 + k
+                        out_ref[reader, slot] = table_ref[core, high, block]
         return carry
 
     lax.fori_loop(0, NY * NL * NR, one, 0)
@@ -163,10 +180,16 @@
     high = rows[LOWS:BLOCKS_HERE].reshape(flat, BS)
     low_before = jnp.concatenate([rows[BLOCKS_HERE], low[: flat - PORTS_DEV]], axis=0)
     high_before = jnp.concatenate([rows[BLOCKS_HERE + 1], high[: flat - PORTS_DEV]], axis=0)
-    stacked = jnp.concatenate([low, high, low_before, high_before], axis=1)
-    volts = dot_exact(stacked, taps_ref[...])
+    volts = dot_exact(jnp.concatenate([low, high], axis=1), taps_ref[...])
+    low_last, high_last = low_before[:, BS - 1 :], high_before[:, BS - 1 :]
+    lane = lax.broadcasted_iota(jnp.int32, (flat, BS), 1)
+    edge = jnp.where(lane == 0, LOW_PASS[2] * low_last + HIGH_PASS[2] * high_last, 0.0)
+    edge = jnp.where(lane == 1, LOW_PASS[3] * low_last + HIGH_PASS[3] * high_last, edge)
+    near_edge = volts[:, :BS] + edge
     for b in range(LOWS):
-        out_ref[:, 2 * BS * b : 2 * BS * (b + 1)] = volts[PORTS_DEV * b : PORTS_DEV * (b + 1)]
+        rows = slice(PORTS_DEV * b, PORTS_DEV * (b + 1))
+        out_ref[:, 2 * BS * b : 2 * BS * b + BS] = near_edge[rows]
+        out_ref[:, 2 * BS * b + BS : 2 * BS * (b + 1)] = volts[rows, BS:]
 
 
 def route(block, partner):
@@ -203,17 +226,25 @@
 def shards(currents, requested, block_rows, block_slots, coupling):
     bf16 = jnp.bfloat16
     next_head = route(currents[:, :BS], lambda i: i - 1)
+    bands, wanted = pl.pallas_call(
+        forward_kernel,
+        out_shape=[
+            jax.ShapeDtypeStruct((BLOCKS_HERE, PORTS_DEV, BS), jnp.float32),
+            jax.ShapeDtypeStruct((NY * NL * NR,) + requested.shape[:1:-1], jnp.int32),
+        ],
+        in_specs=[VMEM, VMEM],
+        out_specs=[VMEM, VMEM],
+        compiler_params=PARAMS,
+        name="forward",
+    )(currents, requested[0, 0].T)
     same = pl.pallas_call(
-        forward_kernel,
+        finish_kernel,
         out_shape=jax.ShapeDtypeStruct((BLOCKS_HERE, PORTS_DEV, BS), bf16),
         in_specs=[VMEM, VMEM],
         out_specs=VMEM,
         compiler_params=PARAMS,
-        name="forward",
-    )(currents, next_head)
-    wanted = jnp.maximum(requested, 0).reshape(NY, NH * NM, NL, NC * 2).transpose(0, 2, 1, 3)
-    wanted = jnp.broadcast_to(wanted.reshape(NY, NL, 1, SLOTS), (NY, NL, NR, SLOTS))
-    wanted = wanted.reshape(NY * NL * NR, SLOTS)
+        name="finish",
+    )(bands, next_head)
     same = lax.all_gather(same, "zhigh", axis=0)
     same, wanted = lax.optimization_barrier((same, wanted))
     other = route(same, two_away)

time: 119 us -> 119 us (level)
  the two profiles are of different devices: /device:TPU:8 before, /device:TPU:2 now
where the time goes in v10:
time: 119 us
  blocking collectives  72.4 us (61%)
  starting transfers between devices  28.3 us (24%)
  Pallas kernels  9.4 us (8%)
  waiting for transfers between devices  6.1 us (5%)
  local copies, waits for them, and re-layouts  2.31 us (2%)
    all_to_all x1, blocking collectives, to_window(): lax.all_to_all(block, EVERY, 0, 0, tiled=True, axis_index_groups=windows())  31.3 us
    all_gather x1, blocking collectives, shards(): same = lax.all_gather(same, 'zhigh', axis=0)  22.5 us
    ppermute x3, starting transfers between devices, route(): lax.ppermute(block, FINE, [(i, partner(i) % count) for i in range(count)])  19.1 us
    all_to_all x1, blocking collectives, shards(): parts = lax.all_to_all(parts, 'rep', 0, 0, tiled=True)  11.9 us
    all_to_all x1, starting transfers between devices, to_window(): lax.all_to_all(block, EVERY, 0, 0, tiled=True, axis_index_groups=windows())  9.24 us
    pallas_call x1, Pallas kernels, shards(): pl.pallas_call(select_kernel, out_shape=jax.ShapeDtypeStruct((NY * NL * N...  4.1 us
    ppermute x3, waiting for transfers between devices, route(): lax.ppermute(block, FINE, [(i, partner(i) % count) for i in range(count)])  3.65 us
    pallas_call x1, Pallas kernels, shards(): pl.pallas_call(product_kernel, out_shape=[jax.ShapeDtypeStruct((WINDOW, P...  2.92 us
  transfers between devices with their start and end apart: 4, of which 2 were waited for; matrix products, arithmetic and copies ran while one was open for 0% of the time, Pallas kernels for 1%

profile of v10, /device:TPU:2, one launch (start us, length us, event | category | flops | bytes accessed | tf_op | source)
XLA Modules:
  0.0 118.6 jit_solution(6074946030314281152)
XLA Ops:
  0.0 0.7 slice.3
  0.7 13.3 %collective-permute-start = (f32[8,128]{1,0:T(8,128)S(1)}, f32[8,128]{1,0:T(8,128)S(1)}, u32[]{:S(2)}, u32[]{:S(2)}) collective-permute-start(f32[8,128]{1,0:T(8,128)S(1)} %slice.3), channel_id=1, source_target_pairs={{0,508},{4,0},{8,4},{12,8},{16,12},{20,16},{24,20},{28,24},{32,28}... | collective-permute-start | bytes 12296 | tf_op jit(solution)/shard_map/ppermute | solution.py:197
  14.0 0.0 copy-start.2
  14.0 0.9 copy-done.2
  14.9 0.7 copy-done.3
  15.6 1.1 forward.1
  16.7 0.1 finish.1
  16.9 22.5 %all-gather = bf16[192,8,128]{2,1,0:T(8,128)(2,1)S(1)} all-gather(bf16[48,8,128]{2,1,0:T(8,128)(2,1)S(1)} %finish.1), channel_id=2, replica_groups=mesh['y'=4,'zhigh'=4,'zmid'=2,'zlow'=2,'core'=2,'rep'=4] {'zhigh'}, dimensions={0}, use_global_device_ids=true | all-gather | bytes 491520 | tf_op jit(solution)/shard_map/all_gather | solution.py:248
  39.3 1.9 %collective-permute-start.1 = (bf16[4,48,8,128]{3,2,1,0:T(8,128)(2,1)S(1)}, bf16[4,48,8,128]{3,2,1,0:T(8,128)(2,1)S(1)}, u32[]{:S(2)}, u32[]{:S(2)}) collective-permute-start(bf16[4,48,8,128]{3,2,1,0:T(8,128)(2,1)S(1)} %bitcast.19), channel_id=1, source_target_pairs={{0,16},{4,116},{8,24},{12,124},{16,0},{20,36},{24,8},{28,44},{32,4... | collective-permute-start | bytes 1179656 | tf_op jit(solution)/shard_map/ppermute | solution.py:197
  41.2 9.2 %all-to-all-start = ((s32[32,2,128]{2,1,0:T(2,128)}), s32[32,2,128]{2,1,0:T(2,128)S(1)}, u32[]{:S(2)}, u32[]{:S(2)}) async-start(s32[32,2,128]{2,1,0:T(2,128)} %get-tuple-element.14), calls=%async_computation | async-start | bytes 65536 | tf_op jit(solution)/shard_map/all_to_all | solution.py:223
  50.5 2.4 %all-gather.1 = bf16[8,48,8,128]{3,2,1,0:T(8,128)(2,1)S(1)} all-gather(bf16[4,48,8,128]{3,2,1,0:T(8,128)(2,1)S(1)} %bitcast.20), channel_id=3, replica_groups=mesh['y'=4,'zhigh'=4,'zmid'=2,'zlow'=2,'core'=2,'rep'=4] {'core'}, dimensions={0}, use_global_device_ids=true | all-gather | bytes 1179648 | tf_op jit(solution)/shard_map/all_gather | solution.py:251
  52.8 2.4 %all-gather.2 = bf16[8,48,8,128]{3,2,1,0:T(8,128)(2,1)S(1)} all-gather(bf16[4,48,8,128]{3,2,1,0:T(8,128)(2,1)S(1)} %collective-permute-done.1), channel_id=4, replica_groups=mesh['y'=4,'zhigh'=4,'zmid'=2,'zlow'=2,'core'=2,'rep'=4] {'core'}, dimensions={0}, use_global_device_ids=true | all-gather | bytes 1179648 | tf_op jit(solution)/shard_map/all_gather | solution.py:253
  55.2 2.4 %all-to-all-done.wanted_ref = s32[32,2,128]{2,1,0:T(2,128)S(1)} async-done(((s32[32,2,128]{2,1,0:T(2,128)}), s32[32,2,128]{2,1,0:T(2,128)S(1)}, u32[]{:S(2)}, u32[]{:S(2)}) %all-to-all-start) | async-done | bytes 32800 | tf_op jit(solution)/shard_map/all_to_all | solution.py:223
  57.7 4.1 %select.1 = bf16[32,32,8,128]{3,2,1,0:T(8,128)(2,1)S(1)} custom-call(s32[32,2,128]{2,1,0:T(2,128)S(1)} %all-to-all-done.wanted_ref, bf16[2,4,48,8,128]{4,3,2,1,0:T(8,128)(2,1)S(1)} %bitcast.13, bf16[2,4,48,8,128]{4,3,2,1,0:T(8,128)(2,1)S(1)} %bitcast.14), custom_call_target="tpu_custom_call" | custom-call | tf_op jit(solution)/shard_map/select/pallas_call | solution.py:254
  61.8 0.0 copy-start
  61.8 31.3 %all_to_all.15 = bf16[32,32,8,128]{3,2,1,0:T(8,128)(2,1)S(1)} all-to-all(bf16[32,32,8,128]{3,2,1,0:T(8,128)(2,1)S(1)} %select.1), channel_id=1, replica_groups={{0,1,2,3,8,9,10,11,128,129,130,131,136,137,138,139,256,257,258,259,264,..., dimensions={0} | all-to-all | bytes 4194304 | tf_op jit(solution)/shard_map/all_to_all | solution.py:223
  93.1 2.9 %products.1 = (f32[72,32,128]{2,1,0:T(8,128)S(1)}, bf16[14,32,128]{2,1,0:T(8,128)(2,1)S(1)}, bf16[14,32,128]{2,1,0:T(8,128)(2,1)S(1)}) custom-call(s32[1,128]{1,0:T(1,128)S(1)} %bitcast.17, s32[1,128]{1,0:T(1,128)S(1)} %bitcast.18, bf16[8,4,32,8,128]{4,3,2,1,0:T(8,128)(2,1)S(1)} %bitcast.11, bf16[128,128,128]{2,1,0:T(8,128)(2,1)S(1)} %bitcast.12), custom_call_target="tpu_custom_call" | custom-call | tf_op jit(solution)/shard_map/products/pallas_call | solution.py:263
  96.1 0.0 copy-start.1
  96.1 3.9 %collective-permute-start.2 = (bf16[14,32,128]{2,1,0:T(8,128)(2,1)S(1)}, bf16[14,32,128]{2,1,0:T(8,128)(2,1)S(1)}, u32[]{:S(2)}, u32[]{:S(2)}) collective-permute-start(bf16[14,32,128]{2,1,0:T(8,128)(2,1)S(1)} %get-tuple-element.18), channel_id=1, source_target_pairs={{0,508},{4,8},{8,4},{12,16},{16,12},{20,24},{24,20},{28,32},{32,28... | collective-permute-start | bytes 344072 | tf_op jit(solution)/shard_map/ppermute | solution.py:197
  100.0 2.0 %all-gather.3 = bf16[28,32,128]{2,1,0:T(8,128)(2,1)S(1)} all-gather(bf16[14,32,128]{2,1,0:T(8,128)(2,1)S(1)} %get-tuple-element.17), channel_id=5, replica_groups=mesh['y'=4,'zhigh'=4,'zmid'=2,'zlow'=2,'core'=2,'rep'=4] {'core'}, dimensions={0}, use_global_device_ids=true | all-gather | bytes 344064 | tf_op jit(solution)/shard_map/all_gather | solution.py:275
  102.0 3.6 %collective-permute-done.2.far_ref = bf16[14,32,128]{2,1,0:T(8,128)(2,1)S(1)} collective-permute-done((bf16[14,32,128]{2,1,0:T(8,128)(2,1)S(1)}, bf16[14,32,128]{2,1,0:T(8,128)(2,1)S(1)}, u32[]{:S(2)}, u32[]{:S(2)}) %collective-permute-start.2) | collective-permute-done | bytes 114720 | tf_op jit(solution)/shard_map/ppermute | solution.py:197
  105.6 0.1 combine.1
  105.7 11.9 %all_to_all.16.parts_ref = bf16[4,50,8,128]{3,2,1,0:T(8,128)(2,1)S(1)} all-to-all(bf16[4,50,8,128]{3,2,1,0:T(8,128)(2,1)S(1)} %combine.1), channel_id=1, replica_groups=mesh['y'=4,'zhigh'=4,'zmid'=2,'zlow'=2,'core'=2,'rep'=4] {'rep'}, dimensions={0} | all-to-all | bytes 819200 | tf_op jit(solution)/shard_map/all_to_all | solution.py:285
  117.6 1.0 inverse.1
  (9 shorter events, 0.0 us)
Async XLA Ops:
  0.7 16.0 %collective-permute-start = (f32[8,128]{1,0:T(8,128)S(1)}, f32[8,128]{1,0:T(8,128)S(1)}, u32[]{:S(2)}, u32[]{:S(2)}) collective-permute-start(f32[8,128]{1,0:T(8,128)S(1)} %slice.3), channel_id=1, source_target_pairs={{0,508},{4,0},{8,4},{12,8},{16,12},{20,16},{24,20},{28,24},{32,28}... | collective-permute-start | bytes 12296 | tf_op jit(solution)/shard_map/ppermute | solution.py:197
  14.0 0.9 copy-start.2
  14.9 0.7 copy-start.3
  39.3 13.5 %collective-permute-start.1 = (bf16[4,48,8,128]{3,2,1,0:T(8,128)(2,1)S(1)}, bf16[4,48,8,128]{3,2,1,0:T(8,128)(2,1)S(1)}, u32[]{:S(2)}, u32[]{:S(2)}) collective-permute-start(bf16[4,48,8,128]{3,2,1,0:T(8,128)(2,1)S(1)} %bitcast.19), channel_id=1, source_target_pairs={{0,16},{4,116},{8,24},{12,124},{16,0},{20,36},{24,8},{28,44},{32,4... | collective-permute-start | bytes 1179656 | tf_op jit(solution)/shard_map/ppermute | solution.py:197
  41.2 16.4 %all-to-all-start = ((s32[32,2,128]{2,1,0:T(2,128)}), s32[32,2,128]{2,1,0:T(2,128)S(1)}, u32[]{:S(2)}, u32[]{:S(2)}) async-start(s32[32,2,128]{2,1,0:T(2,128)} %get-tuple-element.14), calls=%async_computation | async-start | bytes 65536 | tf_op jit(solution)/shard_map/all_to_all | solution.py:223
  61.8 31.4 %copy-start = (bf16[1,1,128,128,128]{4,3,2,1,0:T(8,128)(2,1)S(1)}, bf16[1,1,128,128,128]{4,3,2,1,0:T(8,128)(2,1)}, u32[]{:S(2)}) copy-start(bf16[1,1,128,128,128]{4,3,2,1,0:T(8,128)(2,1)} %param.10) | copy-start | bytes 12582916
  61.8 31.4 %copy-start.4 = (s32[1,1,128]{2,1,0:T(1,128)S(1)}, s32[1,1,128]{2,1,0:T(1,128)}, u32[]{:S(2)}) copy-start(s32[1,1,128]{2,1,0:T(1,128)} %param.8) | copy-start | bytes 1540
  61.8 31.4 %copy-start.5 = (s32[1,1,128]{2,1,0:T(1,128)S(1)}, s32[1,1,128]{2,1,0:T(1,128)}, u32[]{:S(2)}) copy-start(s32[1,1,128]{2,1,0:T(1,128)} %param.9) | copy-start | bytes 1540
  96.1 21.5 %copy-start.1 = (f32[256,256]{1,0:T(8,128)S(1)}, f32[256,256]{1,0:T(8,128)}, u32[]{:S(2)}) copy-start(f32[256,256]{1,0:T(8,128)} %constant.2.clone.taps_ref) | copy-start | bytes 786436
  96.1 9.6 %collective-permute-start.2 = (bf16[14,32,128]{2,1,0:T(8,128)(2,1)S(1)}, bf16[14,32,128]{2,1,0:T(8,128)(2,1)S(1)}, u32[]{:S(2)}, u32[]{:S(2)}) collective-permute-start(bf16[14,32,128]{2,1,0:T(8,128)(2,1)S(1)} %get-tuple-element.18), channel_id=1, source_target_pairs={{0,508},{4,8},{8,4},{12,16},{16,12},{20,24},{24,20},{28,32},{32,28... | collective-permute-start | bytes 344072 | tf_op jit(solution)/shard_map/ppermute | solution.py:197

commit v11 on v10

--- a/solution.py
+++ b/solution.py
@@ -127,9 +127,10 @@
         slot = slots_ref[0, n]
         source = slot >> 1
         z = (source >> 1) & (NZ - 1)
-        sender = (source >> 5) * NL + (z & 1)
         place = (z >> 1) * NC * 2 + (slot & 3)
-        vector = jnp.concatenate([vectors_ref[sender, r, place] for r in range(NR)], axis=0)
+        vector = jnp.concatenate(
+            [vectors_ref[r, z & 1, source >> 5, place] for r in range(NR)], axis=0
+        )
         product = lax.dot_general(
             vector,
             coupling_ref[n],
@@ -205,9 +206,9 @@
             groups.append(
                 [
                     ((y * NZ + z) * NC + core) * NR + r
+                    for r in range(NR)
+                    for z in (even, odd)
                     for y in range(NY)
-                    for z in (even, odd)
-                    for r in range(NR)
                 ]
             )
     return groups
@@ -259,7 +260,7 @@
         compiler_params=PARAMS,
         name="select",
     )(wanted, same, other)
-    vectors = to_window(chosen).reshape(NY * NL, NR, SLOTS, PORTS_DEV, BS)
+    vectors = to_window(chosen).reshape(NR, NL, NY, SLOTS, PORTS_DEV, BS)
     total, near, far = pl.pallas_call(
         product_kernel,
         out_shape=[

time: 119 us -> 119 us (level)
    all_to_all x1, blocking collectives: 11.9 us -> 10.4 us  [shards(): parts = lax.all_to_all(parts, 'rep', 0, 0, tiled=True)]
    all_to_all x1, blocking collectives: 31.3 us -> 32.5 us  [to_window(): lax.all_to_all(block, EVERY, 0, 0, tiled=True, axis_index_groups=windows())]
where the time goes in v11:
time: 119 us; the launch traced here: 118 us
  blocking collectives  72.4 us (61%)
  starting transfers between devices  27.8 us (23%)
  Pallas kernels  9.39 us (8%)
  waiting for transfers between devices  6.44 us (5%)
  local copies, waits for them, and re-layouts  2.31 us (2%)
    all_to_all x1, blocking collectives, to_window(): lax.all_to_all(block, EVERY, 0, 0, tiled=True, axis_index_groups=windows())  32.5 us
    all_gather x1, blocking collectives, shards(): same = lax.all_gather(same, 'zhigh', axis=0)  22.5 us
    ppermute x3, starting transfers between devices, route(): lax.ppermute(block, FINE, [(i, partner(i) % count) for i in range(count)])  18.5 us
    all_to_all x1, blocking collectives, shards(): parts = lax.all_to_all(parts, 'rep', 0, 0, tiled=True)  10.4 us
    all_to_all x1, starting transfers between devices, to_window(): lax.all_to_all(block, EVERY, 0, 0, tiled=True, axis_index_groups=windows())  9.24 us
    pallas_call x1, Pallas kernels, shards(): pl.pallas_call(select_kernel, out_shape=jax.ShapeDtypeStruct((NY * NL * N...  4.1 us
    ppermute x3, waiting for transfers between devices, route(): lax.ppermute(block, FINE, [(i, partner(i) % count) for i in range(count)])  3.98 us
    pallas_call x1, Pallas kernels, shards(): pl.pallas_call(product_kernel, out_shape=[jax.ShapeDtypeStruct((WINDOW, P...  2.91 us
  transfers between devices with their start and end apart: 4, of which 2 were waited for; matrix products, arithmetic and copies ran while one was open for 0% of the time, Pallas kernels for 1%

profile of v11, /device:TPU:2, one launch (start us, length us, event | category | flops | bytes accessed | tf_op | source)
XLA Modules:
  0.0 118.4 jit_solution(6242745896844685057)
XLA Ops:
  0.0 0.7 slice.3
  0.7 13.3 %collective-permute-start = (f32[8,128]{1,0:T(8,128)S(1)}, f32[8,128]{1,0:T(8,128)S(1)}, u32[]{:S(2)}, u32[]{:S(2)}) collective-permute-start(f32[8,128]{1,0:T(8,128)S(1)} %slice.3), channel_id=1, source_target_pairs={{0,508},{4,0},{8,4},{12,8},{16,12},{20,16},{24,20},{28,24},{32,28}... | collective-permute-start | bytes 12296 | tf_op jit(solution)/shard_map/ppermute | solution.py:198
  14.0 0.0 copy-start.2
  14.0 0.9 copy-done.2
  14.9 0.7 copy-done.3
  15.6 1.1 forward.1
  16.7 0.1 finish.1
  16.9 22.5 %all-gather = bf16[192,8,128]{2,1,0:T(8,128)(2,1)S(1)} all-gather(bf16[48,8,128]{2,1,0:T(8,128)(2,1)S(1)} %finish.1), channel_id=2, replica_groups=mesh['y'=4,'zhigh'=4,'zmid'=2,'zlow'=2,'core'=2,'rep'=4] {'zhigh'}, dimensions={0}, use_global_device_ids=true | all-gather | bytes 491520 | tf_op jit(solution)/shard_map/all_gather | solution.py:249
  39.3 1.9 %collective-permute-start.1 = (bf16[4,48,8,128]{3,2,1,0:T(8,128)(2,1)S(1)}, bf16[4,48,8,128]{3,2,1,0:T(8,128)(2,1)S(1)}, u32[]{:S(2)}, u32[]{:S(2)}) collective-permute-start(bf16[4,48,8,128]{3,2,1,0:T(8,128)(2,1)S(1)} %bitcast.19), channel_id=1, source_target_pairs={{0,16},{4,116},{8,24},{12,124},{16,0},{20,36},{24,8},{28,44},{32,4... | collective-permute-start | bytes 1179656 | tf_op jit(solution)/shard_map/ppermute | solution.py:198
  41.2 9.2 %all-to-all-start = ((s32[32,2,128]{2,1,0:T(2,128)}), s32[32,2,128]{2,1,0:T(2,128)S(1)}, u32[]{:S(2)}, u32[]{:S(2)}) async-start(s32[32,2,128]{2,1,0:T(2,128)} %get-tuple-element.14), calls=%async_computation | async-start | bytes 65536 | tf_op jit(solution)/shard_map/all_to_all | solution.py:224
  50.5 2.4 %all-gather.1 = bf16[8,48,8,128]{3,2,1,0:T(8,128)(2,1)S(1)} all-gather(bf16[4,48,8,128]{3,2,1,0:T(8,128)(2,1)S(1)} %bitcast.20), channel_id=3, replica_groups=mesh['y'=4,'zhigh'=4,'zmid'=2,'zlow'=2,'core'=2,'rep'=4] {'core'}, dimensions={0}, use_global_device_ids=true | all-gather | bytes 1179648 | tf_op jit(solution)/shard_map/all_gather | solution.py:252
  52.8 2.4 %all-gather.2 = bf16[8,48,8,128]{3,2,1,0:T(8,128)(2,1)S(1)} all-gather(bf16[4,48,8,128]{3,2,1,0:T(8,128)(2,1)S(1)} %collective-permute-done.1), channel_id=4, replica_groups=mesh['y'=4,'zhigh'=4,'zmid'=2,'zlow'=2,'core'=2,'rep'=4] {'core'}, dimensions={0}, use_global_device_ids=true | all-gather | bytes 1179648 | tf_op jit(solution)/shard_map/all_gather | solution.py:254
  55.2 2.5 %all-to-all-done.wanted_ref = s32[32,2,128]{2,1,0:T(2,128)S(1)} async-done(((s32[32,2,128]{2,1,0:T(2,128)}), s32[32,2,128]{2,1,0:T(2,128)S(1)}, u32[]{:S(2)}, u32[]{:S(2)}) %all-to-all-start) | async-done | bytes 32800 | tf_op jit(solution)/shard_map/all_to_all | solution.py:224
  57.7 4.1 %select.1 = bf16[32,32,8,128]{3,2,1,0:T(8,128)(2,1)S(1)} custom-call(s32[32,2,128]{2,1,0:T(2,128)S(1)} %all-to-all-done.wanted_ref, bf16[2,4,48,8,128]{4,3,2,1,0:T(8,128)(2,1)S(1)} %bitcast.13, bf16[2,4,48,8,128]{4,3,2,1,0:T(8,128)(2,1)S(1)} %bitcast.14), custom_call_target="tpu_custom_call" | custom-call | tf_op jit(solution)/shard_map/select/pallas_call | solution.py:255
  61.8 0.0 copy-start.4
  61.8 32.5 %all_to_all.15 = bf16[32,32,8,128]{3,2,1,0:T(8,128)(2,1)S(1)} all-to-all(bf16[32,32,8,128]{3,2,1,0:T(8,128)(2,1)S(1)} %select.1), channel_id=1, replica_groups={{0,128,256,384,8,136,264,392,1,129,257,385,9,137,265,393,2,130,258,386,..., dimensions={0} | all-to-all | bytes 4194304 | tf_op jit(solution)/shard_map/all_to_all | solution.py:224
  94.4 2.9 %products.1 = (f32[72,32,128]{2,1,0:T(8,128)S(1)}, bf16[14,32,128]{2,1,0:T(8,128)(2,1)S(1)}, bf16[14,32,128]{2,1,0:T(8,128)(2,1)S(1)}) custom-call(s32[1,128]{1,0:T(1,128)S(1)} %bitcast.17, s32[1,128]{1,0:T(1,128)S(1)} %bitcast.18, bf16[4,2,4,32,8,128]{5,4,3,2,1,0:T(8,128)(2,1)S(1)} %bitcast.11, bf16[128,128,128]{2,1,0:T(8,128)(2,1)S(1)} %bitcast.12), custom_call_target="tpu_custom_call" | custom-call | tf_op jit(solution)/shard_map/products/pallas_call | solution.py:264
  97.3 0.0 copy-start.1
  97.3 3.3 %collective-permute-start.2 = (bf16[14,32,128]{2,1,0:T(8,128)(2,1)S(1)}, bf16[14,32,128]{2,1,0:T(8,128)(2,1)S(1)}, u32[]{:S(2)}, u32[]{:S(2)}) collective-permute-start(bf16[14,32,128]{2,1,0:T(8,128)(2,1)S(1)} %get-tuple-element.18), channel_id=1, source_target_pairs={{0,508},{4,8},{8,4},{12,16},{16,12},{20,24},{24,20},{28,32},{32,28... | collective-permute-start | bytes 344072 | tf_op jit(solution)/shard_map/ppermute | solution.py:198
  100.6 2.3 %all-gather.3 = bf16[28,32,128]{2,1,0:T(8,128)(2,1)S(1)} all-gather(bf16[14,32,128]{2,1,0:T(8,128)(2,1)S(1)} %get-tuple-element.17), channel_id=5, replica_groups=mesh['y'=4,'zhigh'=4,'zmid'=2,'zlow'=2,'core'=2,'rep'=4] {'core'}, dimensions={0}, use_global_device_ids=true | all-gather | bytes 344064 | tf_op jit(solution)/shard_map/all_gather | solution.py:276
  102.9 4.0 %collective-permute-done.2.far_ref = bf16[14,32,128]{2,1,0:T(8,128)(2,1)S(1)} collective-permute-done((bf16[14,32,128]{2,1,0:T(8,128)(2,1)S(1)}, bf16[14,32,128]{2,1,0:T(8,128)(2,1)S(1)}, u32[]{:S(2)}, u32[]{:S(2)}) %collective-permute-start.2) | collective-permute-done | bytes 114720 | tf_op jit(solution)/shard_map/ppermute | solution.py:198
  106.8 0.1 combine.1
  106.9 10.4 %all_to_all.16.parts_ref = bf16[4,50,8,128]{3,2,1,0:T(8,128)(2,1)S(1)} all-to-all(bf16[4,50,8,128]{3,2,1,0:T(8,128)(2,1)S(1)} %combine.1), channel_id=1, replica_groups=mesh['y'=4,'zhigh'=4,'zmid'=2,'zlow'=2,'core'=2,'rep'=4] {'rep'}, dimensions={0} | all-to-all | bytes 819200 | tf_op jit(solution)/shard_map/all_to_all | solution.py:286
  117.3 1.0 inverse.1
  (9 shorter events, 0.0 us)
Async XLA Ops:
  0.7 16.0 %collective-permute-start = (f32[8,128]{1,0:T(8,128)S(1)}, f32[8,128]{1,0:T(8,128)S(1)}, u32[]{:S(2)}, u32[]{:S(2)}) collective-permute-start(f32[8,128]{1,0:T(8,128)S(1)} %slice.3), channel_id=1, source_target_pairs={{0,508},{4,0},{8,4},{12,8},{16,12},{20,16},{24,20},{28,24},{32,28}... | collective-permute-start | bytes 12296 | tf_op jit(solution)/shard_map/ppermute | solution.py:198
  14.0 0.9 copy-start.2
  14.9 0.7 copy-start.3
  39.3 13.5 %collective-permute-start.1 = (bf16[4,48,8,128]{3,2,1,0:T(8,128)(2,1)S(1)}, bf16[4,48,8,128]{3,2,1,0:T(8,128)(2,1)S(1)}, u32[]{:S(2)}, u32[]{:S(2)}) collective-permute-start(bf16[4,48,8,128]{3,2,1,0:T(8,128)(2,1)S(1)} %bitcast.19), channel_id=1, source_target_pairs={{0,16},{4,116},{8,24},{12,124},{16,0},{20,36},{24,8},{28,44},{32,4... | collective-permute-start | bytes 1179656 | tf_op jit(solution)/shard_map/ppermute | solution.py:198
  41.2 16.4 %all-to-all-start = ((s32[32,2,128]{2,1,0:T(2,128)}), s32[32,2,128]{2,1,0:T(2,128)S(1)}, u32[]{:S(2)}, u32[]{:S(2)}) async-start(s32[32,2,128]{2,1,0:T(2,128)} %get-tuple-element.14), calls=%async_computation | async-start | bytes 65536 | tf_op jit(solution)/shard_map/all_to_all | solution.py:224
  61.8 32.6 %copy-start = (bf16[1,1,128,128,128]{4,3,2,1,0:T(8,128)(2,1)S(1)}, bf16[1,1,128,128,128]{4,3,2,1,0:T(8,128)(2,1)}, u32[]{:S(2)}) copy-start(bf16[1,1,128,128,128]{4,3,2,1,0:T(8,128)(2,1)} %param.10) | copy-start | bytes 12582916
  61.8 32.6 %copy-start.4 = (s32[1,1,128]{2,1,0:T(1,128)S(1)}, s32[1,1,128]{2,1,0:T(1,128)}, u32[]{:S(2)}) copy-start(s32[1,1,128]{2,1,0:T(1,128)} %param.8) | copy-start | bytes 1540
  61.8 32.5 %copy-start.5 = (s32[1,1,128]{2,1,0:T(1,128)S(1)}, s32[1,1,128]{2,1,0:T(1,128)}, u32[]{:S(2)}) copy-start(s32[1,1,128]{2,1,0:T(1,128)} %param.9) | copy-start | bytes 1540
  97.3 20.1 %copy-start.1 = (f32[256,256]{1,0:T(8,128)S(1)}, f32[256,256]{1,0:T(8,128)}, u32[]{:S(2)}) copy-start(f32[256,256]{1,0:T(8,128)} %constant.2.clone.taps_ref) | copy-start | bytes 786436
  97.3 9.6 %collective-permute-start.2 = (bf16[14,32,128]{2,1,0:T(8,128)(2,1)S(1)}, bf16[14,32,128]{2,1,0:T(8,128)(2,1)S(1)}, u32[]{:S(2)}, u32[]{:S(2)}) collective-permute-start(bf16[14,32,128]{2,1,0:T(8,128)(2,1)S(1)} %get-tuple-element.18), channel_id=1, source_target_pairs={{0,508},{4,8},{8,4},{12,16},{16,12},{20,24},{24,20},{28,32},{32,28... | collective-permute-start | bytes 344072 | tf_op jit(solution)/shard_map/ppermute | solution.py:198
